TPU v7x, 512 devices: a whole 4x8x8 slice. The times are simulated.
512 devices in a mesh: dp: 16 (over x, y_lo), seq: 32 (over y_hi, z, core).
Axes of the slice: x: 4, y: 8 (y_hi: 2, y_lo: 4; y = y_hi * 4 + y_lo), z: 8, core: 2. Of those that a mesh axis runs over, the one named last changes fastest.
Arguments:
- inputs: bfloat16 [16, 8192, 768], P('dp', 'seq'), may hold values from -11 to 11
- gain: float32 [768], replicated, may hold values from 0.1 to 1.9
- shift: float32 [768], replicated, may hold values from -1 to 1
- kernel: bfloat16 [768, 3, 768], P('seq'), may hold values from -0.21875 to 0.21875
- cotangent: bfloat16 [16, 8192, 768], P('dp', 'seq'), may hold values from -6 to 6
Outputs:
- output: bfloat16 [16, 8192, 768], P('dp', 'seq')
- grad_in: bfloat16 [16, 8192, 768], P('dp', 'seq')
- weight_grad: float32 [768, 3, 768], P('seq')
- gain_grad: float32 [768], replicated
- shift_grad: float32 [768], replicated
All inputs are finite; a program needn't handle non-finite values.
Results may differ from a plain program's by a relative error of at most 0.008.
Values may be sent and summed in bfloat16 or wider, within the bound.
No kernel may reach another device: no remote copies, remote signals or barrier semaphores. Data moves between devices by JAX's collectives and lax.ppermute only.
A program may use at most 64 MiB of HBM per device.

v0:
```python
import jax
import jax.numpy as jnp
from jax import lax
from jax.sharding import PartitionSpec as P

HOPS = 1


def shifted(block, axis, distance):
    devices = range(lax.axis_size(axis))
    route = [(i - distance, i) for i in devices if i - distance in devices]
    return lax.ppermute(block, axis, route)


def gelu_exact(values):
    return jax.nn.gelu(values, approximate=False)


def body(inputs, gain, shift, kernel, cotangent):
    count_all = inputs.shape[0] * inputs.shape[1] * lax.axis_size("dp") * lax.axis_size("seq")
    norm_scale = 1.0 / jnp.sqrt(jnp.float32(count_all))
    values = inputs.astype(jnp.float32)
    col_mean = lax.psum(jnp.sum(values, axis=(0, 1)), ("dp", "seq")) / count_all
    centred = values - col_mean
    variance = lax.psum(jnp.sum(centred * centred, axis=(0, 1)), ("dp", "seq")) / count_all
    inv_std = lax.rsqrt(variance + 1e-05)
    normed = centred * inv_std
    pre_act = gain * normed + shift
    activated = gelu_exact(pre_act).astype(jnp.bfloat16)
    below_pair = shifted((activated, cotangent), "seq", HOPS)
    above_pair = shifted((activated, cotangent), "seq", -HOPS)
    act_stack = jnp.stack([below_pair[0], activated, above_pair[0]], axis=2)
    cot_stack = jnp.stack([above_pair[1], cotangent, below_pair[1]], axis=2)
    columns = act_stack
    mixed_sum = jnp.einsum(
        "blki,ikc->blc",
        columns,
        lax.all_gather(kernel, "seq", axis=0, tiled=True),
        preferred_element_type=jnp.float32,
    )
    back_proj = jnp.einsum(
        "blkc,ikc->bli",
        cot_stack,
        lax.all_gather(kernel, "seq", axis=0, tiled=True),
        preferred_element_type=jnp.float32,
    )
    output = (values + mixed_sum).astype(jnp.bfloat16)
    unused, tangent = jax.vjp(gelu_exact, pre_act)
    pre_grad = tangent(back_proj)[0]
    shift_total, gain_total = lax.psum(
        (jnp.sum(pre_grad, axis=(0, 1)), jnp.sum(pre_grad * normed, axis=(0, 1))), ("dp", "seq")
    )
    bn_grad = (
        gain * inv_std * (pre_grad - shift_total / count_all - normed * gain_total / count_all)
    )
    grad_in = (cotangent.astype(jnp.float32) + bn_grad).astype(jnp.bfloat16)
    columns = act_stack
    grad_shard = lax.psum_scatter(
        (
            jnp.einsum("blki,blc->ikc", columns, cotangent, preferred_element_type=jnp.float32)
            * norm_scale
        ).astype(jnp.bfloat16),
        "seq",
        scatter_dimension=0,
        tiled=True,
    ).astype(jnp.float32)
    weight_grad = lax.psum(grad_shard, "dp")
    return (output, grad_in, weight_grad, gain_total * norm_scale, shift_total * norm_scale)


def solution(mesh):
    return jax.shard_map(
        body,
        mesh=mesh,
        in_specs=(P("dp", "seq", None), P(), P(), P("seq", None, None), P("dp", "seq", None)),
        out_specs=(P("dp", "seq", None), P("dp", "seq", None), P("seq", None, None), P(), P()),
        check_vma=False,
    )
```

profile of v0, /device:TPU:1, one launch (start us, length us, event | category | flops | bytes accessed | tf_op | source)
XLA Modules:
  0.0 652.7 jit_solution(7131315179374507481)
XLA Ops:
  7.2 0.0 all-gather.2.cloned.1.call-start
  7.2 0.7 all-gather.2.cloned.1.call-update
  7.9 0.0 reduce-scatter.4.cloned.1.call-start
  7.9 8.8 %collective-permute-start.2 = (bf16[1,256,768]{2,1,0:T(8,128)(2,1)}, bf16[1,256,768]{2,1,0:T(8,128)(2,1)S(1)}, u32[]{:S(2)}, u32[]{:S(2)}) collective-permute-start(bf16[1,256,768]{2,1,0:T(8,128)(2,1)} %param.9), channel_id=1, source_target_pairs={{1,0},{2,1},{3,2},{4,3},{5,4},{6,5},{7,6},{8,7},{9,8},{10,9},{11,1... | collective-permute-start | bytes 1179656 | tf_op jit(solution)/shard_map/ppermute | solution.py:12
  16.7 1.9 collective-permute-start.3
  18.7 1.1 convert_reduce_fusion
  19.7 110.2 %psum.35 = f32[768]{0:T(1024)S(1)} all-reduce(f32[768]{0:T(1024)S(1)} %convert_reduce_fusion), channel_id=1, replica_groups=mesh['dp'=16,'seq'=32] {'dp','seq'}, use_global_device_ids=true, to_apply=%region_1.0 | all-reduce | flops 768 | bytes 6144 | tf_op jit(solution)/shard_map/psum | solution.py:23
  130.0 1.1 fusion.22
  131.1 95.9 %psum.36 = f32[768]{0:T(1024)S(1)} all-reduce(f32[768]{0:T(1024)S(1)} %fusion.22), channel_id=1, replica_groups=mesh['dp'=16,'seq'=32] {'dp','seq'}, use_global_device_ids=true, to_apply=%region_3.0 | all-reduce | flops 768 | bytes 6144 | tf_op jit(solution)/shard_map/psum | solution.py:25
  227.0 0.7 fusion.33
  227.7 0.0 collective-permute-done.2
  227.7 0.0 collective-permute-done.3
  227.7 0.0 all-gather.2.cloned.1.call-done
  227.8 0.0 copy-start
  227.8 0.0 copy-start.1
  227.8 0.0 copy-start.2
  227.8 0.0 copy-start.3
  227.8 5.2 fusion.34
  233.0 93.5 %all-reduce = (f32[768]{0:T(1024)S(1)}, f32[768]{0:T(1024)S(1)}) all-reduce(f32[768]{0:T(1024)S(1)} %get-tuple-element.6, f32[768]{0:T(1024)S(1)} %get-tuple-element.5), channel_id=1, replica_groups=mesh['dp'=16,'seq'=32] {'dp','seq'}, use_global_device_ids=true, to_apply=%region_7.0 | all-reduce | flops 1536 | bytes 12288 | tf_op jit(solution)/shard_map/psum | solution.py:50
  326.5 0.6 broadcast_multiply_fusion
  327.1 0.0 copy-done
  327.1 0.0 copy-done.1
  327.1 0.0 copy-done.2
  327.1 0.0 copy-done.3
  327.1 2.8 fusion.21
  329.9 2.6 collective-permute-start.1
  332.4 3.0 collective-permute-start
  335.4 3.5 collective-permute-done.1
  339.0 1.2 collective-permute-done
  340.1 1.2 fusion
  341.3 2.0 copy.16
  343.3 0.0 reduce-scatter.4.cloned.1.call-update
  343.4 0.0 all-reduce.3.cloned.1.call-start
  343.4 0.6 broadcast_multiply_fusion.1
  344.0 146.8 %reduce-scatter.4.cloned.1.call-done = bf16[24,2304]{1,0:T(8,128)(2,1)} async-done(((bf16[768,2304]{1,0:T(8,128)(2,1)}), bf16[24,2304]{1,0:T(8,128)(2,1)}) %reduce-scatter.4.cloned.1.call-update) | async-done | bytes 110608
  490.8 1.6 bitcast_convert_fusion
  492.4 0.0 all-reduce.3.cloned.1.call-update
  492.5 3.9 fusion.2
  496.3 148.2 %all-reduce.3.cloned.1.call-done = f32[24,3,768]{2,0,1:T(8,128)} async-done(((f32[24,3,768]{2,0,1:T(8,128)}), f32[24,3,768]{2,0,1:T(8,128)}) %all-reduce.3.cloned.1.call-update) | async-done | bytes 221200 | tf_op jit(solution)/shard_map/psum | solution.py:67
  644.5 1.6 copy.19
  (1 shorter events, 0.0 us)
Async XLA Ops:
  7.2 220.6 %all-gather.2.cloned.1.call-start = ((), (), s32[]{:S(2)}) async-start(), calls=%async_computation.1 | async-start | bytes 3649536 | tf_op jit(solution)/shard_map/all_gather | solution.py:38
  7.9 482.9 %reduce-scatter.4.cloned.1.call-start = ((), (), s32[]{:S(2)}) async-start(), calls=%async_computation.3 | async-start | bytes 3649536
  7.9 219.8 %collective-permute-start.2 = (bf16[1,256,768]{2,1,0:T(8,128)(2,1)}, bf16[1,256,768]{2,1,0:T(8,128)(2,1)S(1)}, u32[]{:S(2)}, u32[]{:S(2)}) collective-permute-start(bf16[1,256,768]{2,1,0:T(8,128)(2,1)} %param.9), channel_id=1, source_target_pairs={{1,0},{2,1},{3,2},{4,3},{5,4},{6,5},{7,6},{8,7},{9,8},{10,9},{11,1... | collective-permute-start | bytes 1179656 | tf_op jit(solution)/shard_map/ppermute | solution.py:12
  16.7 211.0 %collective-permute-start.3 = (bf16[1,256,768]{2,1,0:T(8,128)(2,1)}, bf16[1,256,768]{2,1,0:T(8,128)(2,1)S(1)}, u32[]{:S(2)}, u32[]{:S(2)}) collective-permute-start(bf16[1,256,768]{2,1,0:T(8,128)(2,1)} %param.9), channel_id=1, source_target_pairs={{0,1},{1,2},{2,3},{3,4},{4,5},{5,6},{6,7},{7,8},{8,9},{9,10},{10,1... | collective-permute-start | bytes 1179656 | tf_op jit(solution)/shard_map/ppermute | solution.py:12
  227.8 99.3 %copy-start = (bf16[1,256,768]{2,1,0:T(8,128)(2,1)S(1)}, bf16[1,256,768]{2,1,0:T(8,128)(2,1)}, u32[]{:S(2)}) copy-start(bf16[1,256,768]{2,1,0:T(8,128)(2,1)} %param.5) | copy-start | bytes 1179652
  227.8 99.3 %copy-start.1 = (bf16[1,256,768]{2,1,0:T(8,128)(2,1)S(1)}, bf16[1,256,768]{2,1,0:T(8,128)(2,1)}, u32[]{:S(2)}) copy-start(bf16[1,256,768]{2,1,0:T(8,128)(2,1)} %param.9) | copy-start | bytes 1179652
  227.8 99.3 %copy-start.2 = (f32[768]{0:T(1024)S(1)}, f32[768]{0:T(1024)}, u32[]{:S(2)}) copy-start(f32[768]{0:T(1024)} %param.6) | copy-start | bytes 9220
  227.8 99.3 %copy-start.3 = (f32[768]{0:T(1024)S(1)}, f32[768]{0:T(1024)}, u32[]{:S(2)}) copy-start(f32[768]{0:T(1024)} %param.7) | copy-start | bytes 9220
  329.9 9.1 %collective-permute-start.1 = (bf16[1,256,768]{2,1,0:T(8,128)(2,1)S(1)}, bf16[1,256,768]{2,1,0:T(8,128)(2,1)S(1)}, u32[]{:S(2)}, u32[]{:S(2)}) collective-permute-start(bf16[1,256,768]{2,1,0:T(8,128)(2,1)S(1)} %get-tuple-element.10), channel_id=1, source_target_pairs={{1,0},{2,1},{3,2},{4,3},{5,4},{6,5},{7,6},{8,7},{9,8},{10,9},{11,1... | collective-permute-start | bytes 1179656 | tf_op jit(solution)/shard_map/ppermute | solution.py:12
  332.4 7.7 %collective-permute-start = (bf16[1,256,768]{2,1,0:T(8,128)(2,1)S(1)}, bf16[1,256,768]{2,1,0:T(8,128)(2,1)S(1)}, u32[]{:S(2)}, u32[]{:S(2)}) collective-permute-start(bf16[1,256,768]{2,1,0:T(8,128)(2,1)S(1)} %get-tuple-element.10), channel_id=1, source_target_pairs={{0,1},{1,2},{2,3},{3,4},{4,5},{5,6},{6,7},{7,8},{8,9},{9,10},{10,1... | collective-permute-start | bytes 1179656 | tf_op jit(solution)/shard_map/ppermute | solution.py:12
  343.4 301.2 %all-reduce.3.cloned.1.call-start = ((), (), s32[]{:S(2)}) async-start(), calls=%async_computation.2 | async-start | bytes 442368 | tf_op jit(solution)/shard_map/psum | solution.py:67
Sparse Core Ops, SparseCore 0:
  11.3 108.8 all-gather.1
  343.5 147.3 reduce-scatter.3
  494.3 150.1 all-reduce.2
where the time goes:
time: 663 us; the launch traced here: 653 us
  waiting for transfers between devices  300 us (45%)
  blocking collectives  300 us (45%)
  starting transfers between devices  16.4 us (2%)
  between operations  13.8 us (2%)
  matrix products  10.2 us (2%)
  other arithmetic  8.43 us (1%)
    psum x1, waiting for transfers between devices, body(): weight_grad = lax.psum(grad_shard, 'dp')  148 us
    unnamed x4, waiting for transfers between devices  148 us
    psum x1, blocking collectives, body(): col_mean = lax.psum(jnp.sum(values, axis=(0, 1)), ('dp', 'seq')) / count_all  110 us
    psum x1, blocking collectives, body(): lax.psum(jnp.sum(centred * centred, axis=(0, 1)), ('dp', 'seq')) / count_all  95.9 us
    psum x1, blocking collectives, body(): lax.psum((jnp.sum(pre_grad, axis=(0, 1)), jnp.sum(pre_grad * normed, axis...  93.5 us
    ppermute x4, starting transfers between devices, shifted(): return lax.ppermute(block, axis, route)  16.3 us
  transfers between devices with their start and end apart: 7, of which 4 were waited for; matrix products, arithmetic and copies ran while one was open for 1% of the time, Pallas kernels for 0%

commit v1 on v0

v1 whole, which is shorter than its diff:
```python
import jax
import jax.numpy as jnp
from jax import lax
from jax.sharding import Mesh, PartitionSpec as P

F32 = jnp.float32
BF16 = jnp.bfloat16
AXES = ("x", "yl", "yh", "z", "c")
NX, NYL, NYH, NZ, NC = 4, 4, 2, 8, 2
SEQ = ("yh", "z", "c")
SEQ_N = NYH * NZ * NC
C = 768
L = 256
ROWS = 24
PIECE = 27
SQRT_HALF = 0.7071067811865476
INV_SQRT_2PI = 0.3989422804014327


def broadcast_all(value, axes):
    n = lax.axis_size(axes)
    return lax.all_to_all(jnp.broadcast_to(value[None], (n,) + value.shape), axes, 0, 0, tiled=True)


def merge_stats(parts, count):
    sums, squares = parts[:, 0], parts[:, 1]
    n = parts.shape[0]
    total = jnp.sum(sums, axis=0)
    off = sums / count - total / (count * n)
    return jnp.stack([total, jnp.sum(squares, axis=0) + count * jnp.sum(off * off, axis=0)])


def split(value):
    high = lax.reduce_precision(value, 8, 7)
    return high.astype(BF16), (value - high).astype(BF16)


def body(inputs, gain, shift, kernel, cotangent):
    xi, yl, yh, zi, ci = (lax.axis_index(a) for a in AXES)
    count_all = L * SEQ_N * NX * NYL
    norm_scale = 1.0 / jnp.sqrt(jnp.float32(count_all))
    inputs, cotangent = inputs[0], cotangent[0]
    values = inputs.astype(F32)

    swap_y = []
    for l in range(NYL):
        for h in range(NYH):
            y = 7 - (h * NYL + l)
            swap_y.append((l * NYH + h, (y % NYL) * NYH + y // NYL))
    own = kernel.reshape(ROWS * 3, C)
    other = lax.ppermute(own, ("yl", "yh"), swap_y)
    first = yh == 0
    both = jnp.stack([jnp.where(first, own, other), jnp.where(first, other, own)])
    kernel_c = lax.all_gather(both, "z", axis=0, tiled=False)

    pair = jnp.concatenate([cotangent, inputs], axis=0)
    swap_c = [(0, 1), (1, 0)]
    mate = lax.ppermute(pair, "c", swap_c)
    outer = lax.ppermute(
        pair, SEQ, [(i, j) for i in range(1, SEQ_N - 1, 2) for i, j in ((i, i + 1), (i + 1, i))]
    )
    far = lax.ppermute(outer[:L], "c", swap_c)

    total = jnp.sum(values, axis=0)
    off = values - total / L
    stats = jnp.stack([total, jnp.sum(off * off, axis=0)])
    stats = merge_stats(broadcast_all(stats, ("x", "yl", "yh")), L)
    stats = merge_stats(broadcast_all(stats, ("z", "c")), L * NX * NYL * NYH)
    col_mean = stats[0] / count_all
    inv_std = lax.rsqrt(stats[1] / count_all + 1e-05)

    def activate(block):
        normed = (block.astype(F32) - col_mean) * inv_std
        v = gain * normed + shift
        half = 0.5 * (1.0 + lax.erf(v * SQRT_HALF))
        return normed, v, half

    normed, v, half = activate(inputs)
    act = (v * half).astype(BF16)
    slope = half + v * (INV_SQRT_2PI * jnp.exp(-0.5 * v * v))
    _, v_m, half_m = activate(mate[L:])
    act_mate = (v_m * half_m).astype(BF16)
    _, v_o, half_o = activate(outer[L:])
    seq = (yh * NZ + zi) * NC + ci
    has_outer = jnp.logical_and(seq > 0, seq < SEQ_N - 1)
    act_outer = jnp.where(has_outer, v_o * half_o, 0.0).astype(BF16)

    low = ci == 0
    cot_mate, cot_outer = mate[:L], outer[:L]
    q0 = jnp.where(low, cot_outer, far)
    q1 = jnp.where(low, cotangent, cot_mate)
    q2 = jnp.where(low, cot_mate, cotangent)
    q3 = jnp.where(low, far, cot_outer)
    quad = jnp.concatenate([q0, q1, q2, q3], axis=0)
    act_pair = jnp.concatenate([jnp.where(low, act, act_mate), jnp.where(low, act_mate, act)], axis=0)

    order = jnp.arange(C // 2)
    quarter, owner, row = order // 96, (order // 6) % 16, order % 6
    source = (owner * NC + ci) * ROWS + quarter * 6 + row
    select = (jnp.arange(C)[:, None] == source[None, :]).astype(BF16)
    act_sel = jnp.dot(act_pair, select, preferred_element_type=F32).astype(BF16)
    terms = jnp.concatenate(
        [
            jnp.einsum("li,lc->ic", act_sel, quad[(2 - k) * L : (4 - k) * L], preferred_element_type=F32)
            for k in range(3)
        ],
        axis=1,
    )
    terms = (terms * norm_scale).astype(BF16)
    terms = lax.all_to_all(terms.reshape(NX, 96, 3 * C), "x", 0, 0, tiled=True)
    terms = jnp.sum(terms.astype(F32), axis=0).astype(BF16)
    terms = terms.reshape(NYH, NZ, NYL, PIECE, 128).transpose(2, 0, 1, 3, 4).reshape(64, PIECE, 128)

    kernel_o = lax.ppermute(kernel_c, "c", swap_c)
    k0 = jnp.where(low, kernel_c, kernel_o)
    k1 = jnp.where(low, kernel_o, kernel_c)
    full = jnp.stack([k0, k1]).transpose(2, 1, 0, 3, 4).reshape(C, 3, C)

    cots = jnp.stack(
        [jnp.where(low, q2, q3), cotangent, jnp.where(low, q0, q1)], axis=1
    )
    back_proj = jnp.einsum("lkc,ikc->li", cots, full, preferred_element_type=F32)
    pre_grad = back_proj * slope
    totals = jnp.stack([jnp.sum(pre_grad, axis=0), jnp.sum(pre_grad * normed, axis=0)])
    totals = lax.psum(totals, "c")
    high, rest = split(totals)
    packed = jnp.concatenate([high.reshape(12, 128), rest.reshape(12, 128)], axis=0)
    message = jnp.concatenate([terms, jnp.broadcast_to(packed[None], (64, 24, 128))], axis=1)
    got = lax.all_to_all(message, ("yl", "yh", "z"), 0, 0, tiled=True)
    got = jnp.sum(got.astype(F32), axis=0)
    totals = got[PIECE : PIECE + 12] + got[PIECE + 12 :]
    high, rest = split(totals)
    packed = jnp.concatenate([got[:PIECE].astype(BF16), high, rest], axis=0)
    got = broadcast_all(packed, ("x", "yl")).astype(F32)
    weight_grad = got[:, :PIECE].reshape(ROWS, 3, C)
    totals = jnp.sum(got.reshape(NX, NYL, PIECE + 24, 128)[:, 0, PIECE:], axis=0)
    totals = (totals[:12] + totals[12:]).reshape(2, C)
    shift_total, gain_total = totals[0], totals[1]

    before = jnp.where(low, act_outer, act_mate)
    after = jnp.where(low, act_mate, act_outer)
    acts = jnp.stack([before, act, after], axis=1)
    mixed_sum = jnp.einsum("lki,ikc->lc", acts, full, preferred_element_type=F32)
    output = (values + mixed_sum).astype(BF16)
    bn_grad = gain * inv_std * (pre_grad - shift_total / count_all - normed * gain_total / count_all)
    grad_in = (cotangent.astype(F32) + bn_grad).astype(BF16)
    return (output[None], grad_in[None], weight_grad, gain_total * norm_scale, shift_total * norm_scale)


def solution(mesh):
    split_mesh = Mesh(mesh.devices.reshape(NX, NYL, NYH, NZ, NC), AXES)
    rows = P(("x", "yl"), SEQ, None)
    return jax.shard_map(
        body,
        mesh=split_mesh,
        in_specs=(rows, P(), P(), P(SEQ, None, None), rows),
        out_specs=(rows, rows, P(SEQ, None, None), P(), P()),
        check_vma=False,
    )
```

time: 663 us -> 197 us (0.30); the launches traced: 653 us -> 195 us
  blocking collectives: 300 us -> 28.9 us
  waiting for transfers between devices: 300 us -> 50.5 us
  starting transfers between devices: 16.4 us -> 59.8 us
  local copies, waits for them, and re-layouts: 3.7 us -> 17 us
    psum x3 -> x1, blocking collectives: 300 us -> 3.56 us  [body(): totals = lax.psum(totals, 'c')]
    psum x1 -> x0, waiting for transfers between devices: 148 us -> none  [body(): weight_grad = lax.psum(grad_shard, 'dp')]
    unnamed x4 -> x1, waiting for transfers between devices: 148 us -> 0.02 us
    all_to_all x0 -> x4, waiting for transfers between devices: none -> 40.5 us  [the longest x1 25.7 us: body(): got = lax.all_to_all(message, ('yl', 'yh', 'z'), 0, 0, tiled=True)]
    all_to_all x0 -> x4, starting transfers between devices: none -> 39.3 us  [the longest x3 26.4 us: broadcast_all(): lax.all_to_all(jnp.broadcast_to(value[None], (n,) + value.shape), axes, 0...]
    all_to_all x0 -> x1, blocking collectives: none -> 25.4 us  [body(): terms = lax.all_to_all(terms.reshape(NX, 96, 3 * C), 'x', 0, 0, tiled=True)]
    all_gather x1, waiting for transfers between devices: 0.02 us -> 8.93 us  [body(): kernel_c = lax.all_gather(both, 'z', axis=0, tiled=False)]
    reshape x0 -> x6, local copies, waits for them, and re-layouts: none -> 7.31 us  [the longest x1 5.53 us: body(): full = jnp.stack([k0, k1]).transpose(2, 1, 0, 3, 4).reshape(C, 3, C)]
  transfers between devices with their start and end apart: 7 -> 10, of which waited for: 4 -> 6; matrix products, arithmetic and copies ran while one was open for 1% -> 10% of each run, Pallas kernels for 0% -> 0%
where the time goes in v1:
time: 197 us; the launch traced here: 195 us
  starting transfers between devices  59.8 us (30%)
  waiting for transfers between devices  50.5 us (26%)
  blocking collectives  28.9 us (15%)
  local copies, waits for them, and re-layouts  17 us (9%)
  between operations  14.5 us (7%)
  other arithmetic  14 us (7%)
  matrix products  10.5 us (5%)
    all_to_all x3, starting transfers between devices, broadcast_all(): lax.all_to_all(jnp.broadcast_to(value[None], (n,) + value.shape), axes, 0...  26.4 us
    all_to_all x1, waiting for transfers between devices, body(): got = lax.all_to_all(message, ('yl', 'yh', 'z'), 0, 0, tiled=True)  25.7 us
    all_to_all x1, blocking collectives, body(): terms = lax.all_to_all(terms.reshape(NX, 96, 3 * C), 'x', 0, 0, tiled=True)  25.4 us
    all_to_all x3, waiting for transfers between devices, broadcast_all(): lax.all_to_all(jnp.broadcast_to(value[None], (n,) + value.shape), axes, 0...  14.8 us
    all_to_all x1, starting transfers between devices, body(): got = lax.all_to_all(message, ('yl', 'yh', 'z'), 0, 0, tiled=True)  12.9 us
    all_gather x1, waiting for transfers between devices, body(): kernel_c = lax.all_gather(both, 'z', axis=0, tiled=False)  8.93 us
    ppermute x1, starting transfers between devices, body(): other = lax.ppermute(own, ('yl', 'yh'), swap_y)  5.93 us
    reshape x1, local copies, waits for them, and re-layouts, body(): full = jnp.stack([k0, k1]).transpose(2, 1, 0, 3, 4).reshape(C, 3, C)  5.53 us
  transfers between devices with their start and end apart: 10, of which 6 were waited for; matrix products, arithmetic and copies ran while one was open for 10% of the time, Pallas kernels for 0%

profile of v1, /device:TPU:1, one launch (start us, length us, event | category | flops | bytes accessed | tf_op | source)
XLA Modules:
  0.0 195.3 jit_solution(12062781095969763903)
XLA Ops:
  7.2 0.0 copy-start
  7.2 0.0 copy-start.3
  7.2 1.0 copy.43
  8.2 0.1 reshape.251
  8.3 5.9 %collective-permute-start.2 = (bf16[72,768]{1,0:T(8,128)(2,1)S(1)}, bf16[72,768]{1,0:T(8,128)(2,1)S(1)}, u32[]{:S(2)}, u32[]{:S(2)}) collective-permute-start(bf16[72,768]{1,0:T(8,128)(2,1)S(1)} %reshape.251), channel_id=1, source_target_pairs={{0,112},{16,96},{32,80},{48,64},{64,48},{80,32},{96,16},{112,0},{1... | collective-permute-start | bytes 331784 | tf_op jit(solution)/shard_map/ppermute | solution.py:51
  14.3 1.1 convert_reduce_fusion.1
  15.3 1.1 fusion.37
  16.5 0.7 broadcast_in_dim.15
  17.2 6.9 %all-to-all-start = ((f32[32,2,768]{2,1,0:T(2,128)}), f32[32,2,768]{2,1,0:T(2,128)S(1)}, u32[]{:S(2)}, u32[]{:S(2)}) async-start(f32[32,2,768]{2,1,0:T(2,128)} %broadcast_in_dim.15), calls=%async_computation | async-start | bytes 393216 | tf_op jit(solution)/shard_map/all_to_all | solution.py:22
  24.1 0.0 all-gather.3.cloned.1.call-start
  24.2 0.1 pad_maximum_fusion.1
  24.2 0.0 copy-start.8
  24.3 0.0 copy-start.9
  24.3 5.1 %collective-permute-start = (bf16[512,768]{1,0:T(8,128)(2,1)S(1)}, bf16[512,768]{1,0:T(8,128)(2,1)S(1)}, u32[]{:S(2)}, u32[]{:S(2)}) collective-permute-start(bf16[512,768]{1,0:T(8,128)(2,1)S(1)} %pad_maximum_fusion.1), channel_id=1, source_target_pairs={{1,2},{2,1},{3,4},{4,3},{5,6},{6,5},{7,8},{8,7},{9,10},{10,9},{11,... | collective-permute-start | bytes 2359304 | tf_op jit(solution)/shard_map/ppermute | solution.py:59
  29.4 0.7 pad_maximum_fusion.2
  30.1 0.0 all-gather.3.cloned.1.call-update
  30.2 3.7 %all-to-all-done = f32[32,2,768]{2,1,0:T(2,128)S(1)} async-done(((f32[32,2,768]{2,1,0:T(2,128)}), f32[32,2,768]{2,1,0:T(2,128)S(1)}, u32[]{:S(2)}, u32[]{:S(2)}) %all-to-all-start) | async-done | bytes 196640 | tf_op jit(solution)/shard_map/all_to_all | solution.py:22
  33.9 0.2 slice_reduce_fusion.1
  34.2 0.7 broadcast_in_dim.16
  34.9 13.1 %all-to-all-start.1 = ((f32[16,2,768]{2,1,0:T(2,128)}), f32[16,2,768]{2,1,0:T(2,128)S(1)}, u32[]{:S(2)}, u32[]{:S(2)}) async-start(f32[16,2,768]{2,1,0:T(2,128)} %broadcast_in_dim.16), calls=%async_computation.1 | async-start | bytes 196608 | tf_op jit(solution)/shard_map/all_to_all | solution.py:22
  48.0 2.0 %collective-permute-start.1 = (bf16[512,768]{1,0:T(8,128)(2,1)S(1)}, bf16[512,768]{1,0:T(8,128)(2,1)S(1)}, u32[]{:S(2)}, u32[]{:S(2)}) collective-permute-start(bf16[512,768]{1,0:T(8,128)(2,1)S(1)} %pad_maximum_fusion.1), channel_id=1, source_target_pairs={{0,1},{1,0},{2,3},{3,2},{4,5},{5,4},{6,7},{7,6},{8,9},{9,8},{10,11... | collective-permute-start | bytes 2359304 | tf_op jit(solution)/shard_map/ppermute | solution.py:58
  50.0 7.2 %all-to-all-done.1 = f32[16,2,768]{2,1,0:T(2,128)S(1)} async-done(((f32[16,2,768]{2,1,0:T(2,128)}), f32[16,2,768]{2,1,0:T(2,128)S(1)}, u32[]{:S(2)}, u32[]{:S(2)}) %all-to-all-start.1) | async-done | bytes 98336 | tf_op jit(solution)/shard_map/all_to_all | solution.py:22
  57.2 0.1 slice_reduce_fusion.4
  57.4 1.9 collective-permute-start.4
  59.4 0.6 fusion.109
  60.0 1.0 collective-permute-done.4
  61.0 1.7 select_bitcast_fusion.3
  62.7 1.1 select_bitcast_fusion.5
  63.9 0.9 broadcast_select_fusion
  64.7 0.6 convolution_convert_fusion
  65.3 0.5 fusion.66
  65.9 0.2 copy-done.11
  66.1 0.5 fusion.62
  66.6 8.9 %all-gather.3.cloned.1.call-done = bf16[16,72,768]{2,1,0:T(8,128)(2,1)} async-done(((bf16[2,72,768]{2,1,0:T(8,128)(2,1)}), bf16[16,72,768]{2,1,0:T(8,128)(2,1)}) %all-gather.3.cloned.1.call-update) | async-done | bytes 1769488 | tf_op jit(solution)/shard_map/all_gather | solution.py:54
  75.5 2.9 %copy.45 = bf16[8,2,72,768]{3,2,0,1:T(8,128)(2,1)} copy(bf16[8,2,72,768]{3,2,1,0:T(8,128)(2,1)} %bitcast.93) | data formatting | bytes 3538944 | tf_op jit(solution)/shard_map/all_gather | solution.py:54
  78.4 5.5 %collective-permute-start.3 = (bf16[8,2,72,768]{3,2,0,1:T(8,128)(2,1)}, bf16[8,2,72,768]{3,2,0,1:T(8,128)(2,1)}, u32[]{:S(2)}, u32[]{:S(2)}) collective-permute-start(bf16[8,2,72,768]{3,2,0,1:T(8,128)(2,1)} %copy.45), channel_id=1, source_target_pairs={{0,1},{1,0},{2,3},{3,2},{4,5},{5,4},{6,7},{7,6},{8,9},{9,8},{10,11... | collective-permute-start | bytes 5308424 | tf_op jit(solution)/shard_map/ppermute | solution.py:114
  83.9 0.5 fusion.58
  84.4 0.3 fusion
  84.7 25.4 %all_to_all.25 = bf16[4,96,2304]{2,1,0:T(8,128)(2,1)S(1)} all-to-all(bf16[4,96,2304]{2,1,0:T(8,128)(2,1)S(1)} %fusion), channel_id=1, replica_groups=mesh['x'=4,'yl'=4,'yh'=2,'z'=8,'c'=2] {'x'}, dimensions={0} | all-to-all | bytes 3538944 | tf_op jit(solution)/shard_map/all_to_all | solution.py:110
  110.1 1.2 reduce_sum.128
  111.3 1.5 reshape.253
  112.8 1.1 copy.50
  113.9 1.7 select_bitcast_fusion.1
  115.6 0.3 maximum_bitcast_fusion
  115.9 5.5 %reshape.252 = bf16[768,3,768]{2,1,0:T(4,128)(2,1)} reshape(bf16[2,8,2,72,768]{4,3,2,1,0:T(8,128)(2,1)S(1)} %maximum_bitcast_fusion) | data formatting | bytes 7077888 | tf_op jit(solution)/shard_map/reshape | solution.py:117
  121.5 4.2 %fusion.108 = (f32[768]{0:T(1024)S(1)}, f32[768]{0:T(1024)S(1)}, f32[256,768]{1,0:T(8,128)S(1)}) fusion(f32[768]{0:T(1024)S(1)} %get-tuple-element.32, f32[768]{0:T(1024)S(1)} %broadcast_multiply_fusion.1, bf16[1,256,768]{2,1,0:T(8,128)(2,1)} %param.5, f32[768]{0:T(1024)S(1)} %copy-done.9, f32[768]{0:T(1024)S(1)} %copy-done.8, ...), kind=kOutput, calls=%fused_computation.166 | convolution fusion | flops 910490112 | bytes 5916672 | tf_op jit(solution)/shard_map/lkc,ikc->li/dot_general | solution.py:122
  125.7 3.6 %psum.7 = f32[2,768]{1,0:T(2,128)S(1)} all-reduce(f32[2,768]{1,0:T(2,128)S(1)} %pad_maximum_fusion.6), channel_id=1, replica_groups=mesh['x'=4,'yl'=4,'yh'=2,'z'=8,'c'=2] {'c'}, use_global_device_ids=true, to_apply=%region_11.12 | all-reduce | flops 1536 | bytes 12288 | tf_op jit(solution)/shard_map/psum | solution.py:125
  129.3 0.1 broadcast_in_dim.19
  129.4 0.1 pad_maximum_fusion
  129.5 0.0 copy-start.1
  129.5 1.5 copy.51
  131.0 12.9 %all-to-all-start.3 = ((bf16[64,51,128]{2,1,0:T(8,128)(2,1)}), bf16[64,51,128]{2,1,0:T(8,128)(2,1)S(1)}, u32[]{:S(2)}, u32[]{:S(2)}) async-start(bf16[64,51,128]{2,1,0:T(8,128)(2,1)} %copy.51), calls=%async_computation.3 | async-start | bytes 1835008 | tf_op jit(solution)/shard_map/all_to_all | solution.py:129
  143.9 0.3 fusion.78
  144.2 25.7 %all-to-all-done.3 = bf16[64,51,128]{2,1,0:T(8,128)(2,1)S(1)} async-done(((bf16[64,51,128]{2,1,0:T(8,128)(2,1)}), bf16[64,51,128]{2,1,0:T(8,128)(2,1)S(1)}, u32[]{:S(2)}, u32[]{:S(2)}) %all-to-all-start.3) | async-done | bytes 835616 | tf_op jit(solution)/shard_map/all_to_all | solution.py:129
  170.0 0.2 convert_reduce_fusion
  170.2 0.7 broadcast_in_dim.20
  170.9 6.3 %all-to-all-start.4 = ((bf16[16,51,128]{2,1,0:T(8,128)(2,1)}), bf16[16,51,128]{2,1,0:T(8,128)(2,1)S(1)}, u32[]{:S(2)}, u32[]{:S(2)}) async-start(bf16[16,51,128]{2,1,0:T(8,128)(2,1)} %broadcast_in_dim.20), calls=%async_computation.4 | async-start | bytes 458752 | tf_op jit(solution)/shard_map/all_to_all | solution.py:22
  177.3 4.2 %fusion.19 = bf16[1,256,768]{2,1,0:T(8,128)(2,1)} fusion(bf16[768,3,768]{2,1,0:T(4,128)(2,1)} %reshape.252, bf16[256,1,768]{2,0,1:T(8,128)(2,1)S(1)} %copy-done.7, bf16[256,1,768]{2,0,1:T(8,128)(2,1)S(1)} %fusion.78, bf16[256,1,768]{2,0,1:T(8,128)(2,1)S(1)} %copy-done.6, bf16[1,256,768]{2,1,0:T(8,128)(2,1)S(1)} %copy-done.1), kind=kOutput, calls=%fused_computation.19 | convolution fusion | flops 907739136 | bytes 5505024 | tf_op jit(solution)/shard_map/lki,ikc->lc/dot_general | solution.py:143
  181.5 3.9 %all-to-all-done.4 = bf16[16,51,128]{2,1,0:T(8,128)(2,1)S(1)} async-done(((bf16[16,51,128]{2,1,0:T(8,128)(2,1)}), bf16[16,51,128]{2,1,0:T(8,128)(2,1)S(1)}, u32[]{:S(2)}, u32[]{:S(2)}) %all-to-all-start.4) | async-done | bytes 208928 | tf_op jit(solution)/shard_map/all_to_all | solution.py:22
  185.4 0.6 multiply_bitcast_fusion
  186.0 0.6 broadcast_multiply_fusion
  186.6 0.1 reshape.258
  186.7 0.7 copy.52
  187.5 1.0 fusion.80
  (53 shorter events, 0.4 us)
Async XLA Ops:
  7.2 17.0 %copy-start = (bf16[1,256,768]{2,1,0:T(8,128)(2,1)S(1)}, bf16[1,256,768]{2,1,0:T(8,128)(2,1)}, u32[]{:S(2)}) copy-start(bf16[1,256,768]{2,1,0:T(8,128)(2,1)} %param.5) | copy-start | bytes 1179652
  7.2 17.0 %copy-start.3 = (bf16[1,256,768]{2,1,0:T(8,128)(2,1)S(1)}, bf16[1,256,768]{2,1,0:T(8,128)(2,1)}, u32[]{:S(2)}) copy-start(bf16[1,256,768]{2,1,0:T(8,128)(2,1)} %param.9) | copy-start | bytes 1179652
  8.3 21.1 %collective-permute-start.2 = (bf16[72,768]{1,0:T(8,128)(2,1)S(1)}, bf16[72,768]{1,0:T(8,128)(2,1)S(1)}, u32[]{:S(2)}, u32[]{:S(2)}) collective-permute-start(bf16[72,768]{1,0:T(8,128)(2,1)S(1)} %reshape.251), channel_id=1, source_target_pairs={{0,112},{16,96},{32,80},{48,64},{64,48},{80,32},{96,16},{112,0},{1... | collective-permute-start | bytes 331784 | tf_op jit(solution)/shard_map/ppermute | solution.py:51
  17.2 16.7 %all-to-all-start = ((f32[32,2,768]{2,1,0:T(2,128)}), f32[32,2,768]{2,1,0:T(2,128)S(1)}, u32[]{:S(2)}, u32[]{:S(2)}) async-start(f32[32,2,768]{2,1,0:T(2,128)} %broadcast_in_dim.15), calls=%async_computation | async-start | bytes 393216 | tf_op jit(solution)/shard_map/all_to_all | solution.py:22
  24.1 51.4 %all-gather.3.cloned.1.call-start = ((), (), s32[]{:S(2)}) async-start(), calls=%async_computation.5 | async-start | bytes 1990656 | tf_op jit(solution)/shard_map/all_gather | solution.py:54
  24.2 35.1 %copy-start.8 = (f32[768]{0:T(1024)S(1)}, f32[768]{0:T(1024)}, u32[]{:S(2)}) copy-start(f32[768]{0:T(1024)} %param.6) | copy-start | bytes 9220
  24.3 36.8 %copy-start.9 = (f32[768]{0:T(1024)S(1)}, f32[768]{0:T(1024)}, u32[]{:S(2)}) copy-start(f32[768]{0:T(1024)} %param.7) | copy-start | bytes 9220
  24.3 33.1 %collective-permute-start = (bf16[512,768]{1,0:T(8,128)(2,1)S(1)}, bf16[512,768]{1,0:T(8,128)(2,1)S(1)}, u32[]{:S(2)}, u32[]{:S(2)}) collective-permute-start(bf16[512,768]{1,0:T(8,128)(2,1)S(1)} %pad_maximum_fusion.1), channel_id=1, source_target_pairs={{1,2},{2,1},{3,4},{4,3},{5,6},{6,5},{7,8},{8,7},{9,10},{10,9},{11,... | collective-permute-start | bytes 2359304 | tf_op jit(solution)/shard_map/ppermute | solution.py:59
  34.9 22.4 %all-to-all-start.1 = ((f32[16,2,768]{2,1,0:T(2,128)}), f32[16,2,768]{2,1,0:T(2,128)S(1)}, u32[]{:S(2)}, u32[]{:S(2)}) async-start(f32[16,2,768]{2,1,0:T(2,128)} %broadcast_in_dim.16), calls=%async_computation.1 | async-start | bytes 196608 | tf_op jit(solution)/shard_map/all_to_all | solution.py:22
  48.0 12.0 %collective-permute-start.1 = (bf16[512,768]{1,0:T(8,128)(2,1)S(1)}, bf16[512,768]{1,0:T(8,128)(2,1)S(1)}, u32[]{:S(2)}, u32[]{:S(2)}) collective-permute-start(bf16[512,768]{1,0:T(8,128)(2,1)S(1)} %pad_maximum_fusion.1), channel_id=1, source_target_pairs={{0,1},{1,0},{2,3},{3,2},{4,5},{5,4},{6,7},{7,6},{8,9},{9,8},{10,11... | collective-permute-start | bytes 2359304 | tf_op jit(solution)/shard_map/ppermute | solution.py:58
  57.4 3.6 %collective-permute-start.4 = (bf16[256,768]{1,0:T(8,128)(2,1)S(1)}, bf16[256,768]{1,0:T(8,128)(2,1)S(1)}, u32[]{:S(2)}, u32[]{:S(2)}) collective-permute-start(bf16[256,768]{1,0:T(8,128)(2,1)S(1)} %slice.85), channel_id=1, source_target_pairs={{0,1},{1,0},{2,3},{3,2},{4,5},{5,4},{6,7},{7,6},{8,9},{9,8},{10,11... | collective-permute-start | bytes 1179656 | tf_op jit(solution)/shard_map/ppermute | solution.py:62
  65.3 0.8 copy-start.11
  75.5 8.4 %copy-start.12 = (bf16[512,384]{1,0:T(8,128)(2,1)S(1)}, bf16[512,384]{1,0:T(8,128)(2,1)}, u32[]{:S(2)}) copy-start(bf16[512,384]{1,0:T(8,128)(2,1)} %copy-done.11) | copy-start | bytes 1179652
  78.4 35.5 %collective-permute-start.3 = (bf16[8,2,72,768]{3,2,0,1:T(8,128)(2,1)}, bf16[8,2,72,768]{3,2,0,1:T(8,128)(2,1)}, u32[]{:S(2)}, u32[]{:S(2)}) collective-permute-start(bf16[8,2,72,768]{3,2,0,1:T(8,128)(2,1)} %copy.45), channel_id=1, source_target_pairs={{0,1},{1,0},{2,3},{3,2},{4,5},{5,4},{6,7},{7,6},{8,9},{9,8},{10,11... | collective-permute-start | bytes 5308424 | tf_op jit(solution)/shard_map/ppermute | solution.py:114
  110.1 3.8 %copy-start.2 = (bf16[16,72,768]{2,1,0:T(8,128)(2,1)S(1)}, bf16[16,72,768]{2,1,0:T(8,128)(2,1)}, u32[]{:S(2)}) copy-start(bf16[16,72,768]{2,1,0:T(8,128)(2,1)} %all-gather.3.cloned.1.call-done) | copy-start | bytes 5308420
  121.4 8.0 %copy-start.5 = (bf16[4,2,8,27,128]{4,2,1,0,3:T(8,128)(2,1)S(1)}, bf16[4,2,8,27,128]{4,2,1,0,3:T(8,128)(2,1)}, u32[]{:S(2)}) copy-start(bf16[4,2,8,27,128]{4,2,1,0,3:T(8,128)(2,1)} %copy.50) | copy-start | bytes 1327108
  129.5 14.4 %copy-start.1 = (bf16[1,256,768]{2,1,0:T(8,128)(2,1)S(1)}, bf16[1,256,768]{2,1,0:T(8,128)(2,1)}, u32[]{:S(2)}) copy-start(bf16[1,256,768]{2,1,0:T(8,128)(2,1)} %param.5) | copy-start | bytes 1179652
  131.0 39.0 %all-to-all-start.3 = ((bf16[64,51,128]{2,1,0:T(8,128)(2,1)}), bf16[64,51,128]{2,1,0:T(8,128)(2,1)S(1)}, u32[]{:S(2)}, u32[]{:S(2)}) async-start(bf16[64,51,128]{2,1,0:T(8,128)(2,1)} %copy.51), calls=%async_computation.3 | async-start | bytes 1835008 | tf_op jit(solution)/shard_map/all_to_all | solution.py:129
  143.9 33.3 %copy-start.6 = (bf16[256,1,768]{2,0,1:T(8,128)(2,1)S(1)}, bf16[256,1,768]{2,0,1:T(8,128)(2,1)}, u32[]{:S(2)}) copy-start(bf16[256,1,768]{2,0,1:T(8,128)(2,1)} %get-tuple-element.42) | copy-start | bytes 1179652
  143.9 33.3 %copy-start.7 = (bf16[256,1,768]{2,0,1:T(8,128)(2,1)S(1)}, bf16[256,1,768]{2,0,1:T(8,128)(2,1)}, u32[]{:S(2)}) copy-start(bf16[256,1,768]{2,0,1:T(8,128)(2,1)} %get-tuple-element.53) | copy-start | bytes 1179652
  170.9 14.4 %all-to-all-start.4 = ((bf16[16,51,128]{2,1,0:T(8,128)(2,1)}), bf16[16,51,128]{2,1,0:T(8,128)(2,1)S(1)}, u32[]{:S(2)}, u32[]{:S(2)}) async-start(bf16[16,51,128]{2,1,0:T(8,128)(2,1)} %broadcast_in_dim.20), calls=%async_computation.4 | async-start | bytes 458752 | tf_op jit(solution)/shard_map/all_to_all | solution.py:22
  181.5 6.0 %copy-start.4 = (bf16[1,256,768]{2,1,0:T(8,128)(2,1)S(1)}, bf16[1,256,768]{2,1,0:T(8,128)(2,1)}, u32[]{:S(2)}) copy-start(bf16[1,256,768]{2,1,0:T(8,128)(2,1)} %param.9) | copy-start | bytes 1179652
  181.5 6.0 %copy-start.10 = (f32[768]{0:T(1024)S(1)}, f32[768]{0:T(1024)}, u32[]{:S(2)}) copy-start(f32[768]{0:T(1024)} %get-tuple-element.31) | copy-start | bytes 9220
Sparse Core Ops, SparseCore 0:
  30.3 45.1 all-gather.2

commit v2 on v1

v2 whole, which is shorter than its diff:
```python
import jax
import jax.numpy as jnp
from jax import lax
from jax.experimental import pallas as pl
from jax.experimental.pallas import tpu as pltpu
from jax.sharding import Mesh, PartitionSpec as P

F32 = jnp.float32
BF16 = jnp.bfloat16
AXES = ("x", "yl", "yh", "z", "c")
NX, NYL, NYH, NZ, NC = 4, 4, 2, 8, 2
SEQ = ("yh", "z", "c")
SEQ_N = NYH * NZ * NC
C = 768
HALF = C // 2
L = 256
ROWS = 24
PIECE = 27
TOT = 24
SQRT_HALF = 0.7071067811865476
INV_SQRT_2PI = 0.3989422804014327
PARAMS = pltpu.CompilerParams(vmem_limit_bytes=40 * 1024 * 1024)


def broadcast_all(value, axes):
    n = lax.axis_size(axes)
    return lax.all_to_all(jnp.broadcast_to(value[None], (n,) + value.shape), axes, 0, 0, tiled=True)


def merge_stats(parts, count):
    sums, squares = parts[:, 0], parts[:, 1]
    n = parts.shape[0]
    total = jnp.sum(sums, axis=0)
    off = sums / count - total / (count * n)
    return jnp.stack([total, jnp.sum(squares, axis=0) + count * jnp.sum(off * off, axis=0)])


def pack(totals):
    high = lax.reduce_precision(totals, 8, 7)
    return jnp.concatenate([high.astype(BF16), (totals - high).astype(BF16)], axis=0).reshape(TOT, 128)


def unpack(packed):
    return (packed[: TOT // 2] + packed[TOT // 2 :]).reshape(2, C)


def by_taps(ref, tap):
    return ref[:, tap].reshape(HALF, C)


def back_kernel(q0, q1, q2, kc, ko, sc, so, slope, normed, pre_grad, totals):
    total = jnp.zeros((L, C), F32)
    for kern, sel in ((kc, sc), (ko, so)):
        part = jnp.zeros((L, HALF), F32)
        for tap, q in enumerate((q0, q1, q2)):
            part += lax.dot_general(
                q[...], by_taps(kern, tap), (((1,), (1,)), ((), ())), preferred_element_type=F32
            )
        high = part.astype(BF16)
        low = (part - high.astype(F32)).astype(BF16)
        total += jnp.dot(high, sel[...], preferred_element_type=F32)
        total += jnp.dot(low, sel[...], preferred_element_type=F32)
    grad = total * slope[...]
    pre_grad[...] = grad
    totals[0:1] = jnp.sum(grad, axis=0, keepdims=True)
    totals[1:2] = jnp.sum(grad * normed[...], axis=0, keepdims=True)


def forward_kernel(a0, a1, a2, kc, ko, sc, so, inputs, output):
    total = inputs[...].astype(F32)
    for kern, sel in ((kc, sc), (ko, so)):
        for tap, a in enumerate((a0, a1, a2)):
            chosen = lax.dot_general(
                a[...], sel[...], (((1,), (1,)), ((), ())), preferred_element_type=F32
            ).astype(BF16)
            total += jnp.dot(chosen, by_taps(kern, tap), preferred_element_type=F32)
    output[...] = total.astype(BF16)


def cost(flops, size):
    return pl.CostEstimate(flops=flops, bytes_accessed=size, transcendentals=0)


def body(inputs, gain, shift, kernel, cotangent):
    xi, yl, yh, zi, ci = (lax.axis_index(a) for a in AXES)
    count_all = L * SEQ_N * NX * NYL
    norm_scale = 1.0 / jnp.sqrt(jnp.float32(count_all))
    inputs, cotangent = inputs[0], cotangent[0]
    values = inputs.astype(F32)
    low = ci == 0
    swap_c = [(0, 1), (1, 0)]

    swap_y = []
    for l in range(NYL):
        for h in range(NYH):
            y = 7 - (h * NYL + l)
            swap_y.append((l * NYH + h, (y % NYL) * NYH + y // NYL))
    own = kernel.transpose(1, 0, 2)
    other = lax.ppermute(own, ("yl", "yh"), swap_y)

    pair = jnp.concatenate([cotangent, inputs], axis=0)
    mate = lax.ppermute(pair, "c", swap_c)
    outer = lax.ppermute(
        pair, SEQ, [(i, j) for i in range(1, SEQ_N - 1, 2) for i, j in ((i, i + 1), (i + 1, i))]
    )
    far = lax.ppermute(outer[:L], "c", swap_c)

    total = jnp.sum(values, axis=0)
    off = values - total / L
    stats = jnp.stack([total, jnp.sum(off * off, axis=0)])
    stats = merge_stats(broadcast_all(stats, ("z", "c")), L)

    first = yh == 0
    both = jnp.concatenate([jnp.where(first, own, other), jnp.where(first, other, own)], axis=1)
    stats, both = lax.optimization_barrier((stats, both))
    kernel_c = broadcast_all(both, "z")

    stats = merge_stats(broadcast_all(stats, ("x", "yl", "yh")), L * NZ * NC)
    col_mean = stats[0] / count_all
    inv_std = lax.rsqrt(stats[1] / count_all + 1e-05)

    order = jnp.arange(HALF)
    quarter, owner, row = order // 96, (order // 6) % 16, order % 6
    source = (owner * NC + ci) * ROWS + quarter * 6 + row
    choose = source[None, :] == jnp.arange(C)[:, None]
    select = choose.astype(BF16)
    mate_in = mate[L:]
    in_pair = jnp.concatenate([jnp.where(low, inputs, mate_in), jnp.where(low, mate_in, inputs)], axis=0)
    in_sel = jnp.dot(in_pair, select, preferred_element_type=F32)
    vectors = jnp.stack([col_mean, inv_std, gain, shift])
    vectors = jnp.sum(jnp.where(choose[None], vectors[:, :, None], 0.0), axis=1)
    v = vectors[2] * ((in_sel - vectors[0]) * vectors[1]) + vectors[3]
    act_sel = (v * (0.5 * (1.0 + lax.erf(v * SQRT_HALF)))).astype(BF16)

    cot_mate, cot_outer = mate[:L], outer[:L]
    q0 = jnp.where(low, cot_outer, far)
    q1 = jnp.where(low, cotangent, cot_mate)
    q2 = jnp.where(low, cot_mate, cotangent)
    q3 = jnp.where(low, far, cot_outer)
    quad = jnp.concatenate([q0, q1, q2, q3], axis=0)
    terms = jnp.concatenate(
        [
            jnp.einsum("li,lc->ic", act_sel, quad[(2 - k) * L : (4 - k) * L], preferred_element_type=F32)
            for k in range(3)
        ],
        axis=1,
    )
    terms = (terms * norm_scale).astype(BF16)
    terms, held_in, held_outer, held_mate = lax.optimization_barrier((terms, inputs, outer[L:], mate[L:]))
    terms = lax.all_to_all(terms.reshape(NX, 96, 3 * C), "x", 0, 0, tiled=True)

    def activate(block):
        normed = (block.astype(F32) - col_mean) * inv_std
        v = gain * normed + shift
        return normed, v, 0.5 * (1.0 + lax.erf(v * SQRT_HALF))

    normed, v, half = activate(held_in)
    act = (v * half).astype(BF16)
    slope = half + v * (INV_SQRT_2PI * jnp.exp(-0.5 * v * v))
    _, v_m, half_m = activate(held_mate)
    act_mate = (v_m * half_m).astype(BF16)
    _, v_o, half_o = activate(held_outer)
    seq = (yh * NZ + zi) * NC + ci
    has_outer = jnp.logical_and(seq > 0, seq < SEQ_N - 1)
    act_outer = jnp.where(has_outer, v_o * half_o, 0.0).astype(BF16)

    kernel_o = lax.ppermute(kernel_c, "c", swap_c)
    gz, gy, gr = order // (NYH * ROWS), (order // ROWS) % NYH, order % ROWS
    channel = (gy * NZ + gz) * NC * ROWS + gr
    sel_c = ((channel + ci * ROWS)[:, None] == jnp.arange(C)[None]).astype(BF16)
    sel_o = ((channel + (1 - ci) * ROWS)[:, None] == jnp.arange(C)[None]).astype(BF16)

    pre_grad, totals = pl.pallas_call(
        back_kernel,
        out_shape=(jax.ShapeDtypeStruct((L, C), F32), jax.ShapeDtypeStruct((2, C), F32)),
        compiler_params=PARAMS,
        cost_estimate=cost(2 * L * C * C * 5, 8 * 1024 * 1024),
        name="back",
    )(jnp.where(low, q2, q3), cotangent, jnp.where(low, q0, q1), kernel_c, kernel_o, sel_c, sel_o, slope, normed)
    totals = lax.psum(totals, "c")

    terms = jnp.sum(terms.astype(F32), axis=0).astype(BF16)
    terms = terms.reshape(NYH, NZ, NYL, PIECE, 128).transpose(2, 0, 1, 3, 4).reshape(8, NZ * PIECE, 128)
    message = jnp.concatenate([terms, jnp.broadcast_to(pack(totals)[None], (8, TOT, 128))], axis=1)
    got = jnp.sum(lax.all_to_all(message, ("yl", "yh"), 0, 0, tiled=True).astype(F32), axis=0)
    terms, totals = got[: NZ * PIECE].astype(BF16), unpack(got[NZ * PIECE :])
    message = jnp.concatenate(
        [terms.reshape(NZ, PIECE, 128), jnp.broadcast_to(pack(totals)[None], (NZ, TOT, 128))], axis=1
    )
    got = jnp.sum(lax.all_to_all(message, "z", 0, 0, tiled=True).astype(F32), axis=0)
    message = jnp.concatenate([got[:PIECE].astype(BF16), pack(unpack(got[PIECE:]))], axis=0)
    got = broadcast_all(message, ("x", "yl")).astype(F32)
    weight_grad = got[:, :PIECE].reshape(ROWS, 3, C)
    totals = unpack(jnp.sum(got.reshape(NX, NYL, PIECE + TOT, 128)[:, 0, PIECE:], axis=0))
    shift_total, gain_total = totals[0], totals[1]

    output = pl.pallas_call(
        forward_kernel,
        out_shape=jax.ShapeDtypeStruct((L, C), BF16),
        compiler_params=PARAMS,
        cost_estimate=cost(2 * L * C * C * 6, 6 * 1024 * 1024),
        name="forward",
    )(
        jnp.where(low, act_outer, act_mate), act, jnp.where(low, act_mate, act_outer),
        kernel_c, kernel_o, sel_c, sel_o, inputs,
    )
    bn_grad = gain * inv_std * (pre_grad - shift_total / count_all - normed * gain_total / count_all)
    grad_in = (cotangent.astype(F32) + bn_grad).astype(BF16)
    return (output[None], grad_in[None], weight_grad, gain_total * norm_scale, shift_total * norm_scale)


def solution(mesh):
    split_mesh = Mesh(mesh.devices.reshape(NX, NYL, NYH, NZ, NC), AXES)
    rows = P(("x", "yl"), SEQ, None)
    return jax.shard_map(
        body,
        mesh=split_mesh,
        in_specs=(rows, P(), P(), P(SEQ, None, None), rows),
        out_specs=(rows, rows, P(SEQ, None, None), P(), P()),
        check_vma=False,
    )
```

time: 197 us -> 227 us (1.15)
  waiting for transfers between devices: 50.5 us -> 87.9 us
  between operations: 14.5 us -> 1.16 us
  other arithmetic: 14 us -> 26.4 us
  Pallas kernels: 0 us -> 10.2 us
  blocking collectives: 28.9 us -> 20 us
  starting transfers between devices: 59.8 us -> 53 us
  matrix products: 10.5 us -> 5.27 us
  local copies, waits for them, and re-layouts: 17 us -> 20.2 us
    ppermute x1, waiting for transfers between devices: 0.01 us -> 42.2 us  [body(): lax.ppermute(pair, SEQ, [(i, j) for i in range(1, SEQ_N - 1, 2) for i, j...]
    all_to_all x1 -> x3, waiting for transfers between devices: 25.7 us -> 37 us  [the longest x1 19.7 us: body(): terms = lax.all_to_all(terms.reshape(NX, 96, 3 * C), 'x', 0, 0, tiled=True)]
    pallas_call x0 -> x2, Pallas kernels: none -> 10.2 us  [the longest x1 5.52 us: body(): pl.pallas_call(forward_kernel, out_shape=jax.ShapeDtypeStruct((L, C), BF1...]
    all_gather x1 -> x0, waiting for transfers between devices: 8.93 us -> none  [body(): kernel_c = lax.all_gather(both, 'z', axis=0, tiled=False)]
    all_to_all x1, blocking collectives: 25.4 us -> 16.7 us  [broadcast_all(): lax.all_to_all(jnp.broadcast_to(value[None], (n,) + value.shape), axes, 0...]
    dot_general x3 -> x1, matrix products: 9.01 us -> 0.73 us  [body(): in_sel = jnp.dot(in_pair, select, preferred_element_type=F32)]
    all_to_all x3, waiting for transfers between devices: 14.8 us -> 7.54 us  [broadcast_all(): lax.all_to_all(jnp.broadcast_to(value[None], (n,) + value.shape), axes, 0...]
    unnamed x28 -> x43, local copies, waits for them, and re-layouts: 2.05 us -> 8.94 us
  transfers between devices with their start and end apart: 10 -> 11, of which waited for: 6 -> 6; matrix products, arithmetic and copies ran while one was open for 10% -> 13% of each run, Pallas kernels for 0% -> 2%
where the time goes in v2:
time: 227 us; the launch traced here: 224 us
  waiting for transfers between devices  87.9 us (39%)
  starting transfers between devices  53 us (23%)
  other arithmetic  26.4 us (12%)
  local copies, waits for them, and re-layouts  20.2 us (9%)
  blocking collectives  20 us (9%)
  Pallas kernels  10.2 us (4%)
  matrix products  5.27 us (2%)
    ppermute x1, waiting for transfers between devices, body(): lax.ppermute(pair, SEQ, [(i, j) for i in range(1, SEQ_N - 1, 2) for i, j...  42.2 us
    all_to_all x3, starting transfers between devices, broadcast_all(): lax.all_to_all(jnp.broadcast_to(value[None], (n,) + value.shape), axes, 0...  22.4 us
    all_to_all x1, waiting for transfers between devices, body(): terms = lax.all_to_all(terms.reshape(NX, 96, 3 * C), 'x', 0, 0, tiled=True)  19.7 us
    all_to_all x1, blocking collectives, broadcast_all(): lax.all_to_all(jnp.broadcast_to(value[None], (n,) + value.shape), axes, 0...  16.7 us
    all_to_all x1, waiting for transfers between devices, body(): lax.all_to_all(message, ('yl', 'yh'), 0, 0, tiled=True).astype(F32)  11.9 us
    unnamed x43, local copies, waits for them, and re-layouts  8.94 us
    all_to_all x3, waiting for transfers between devices, broadcast_all(): lax.all_to_all(jnp.broadcast_to(value[None], (n,) + value.shape), axes, 0...  7.54 us
    ppermute x1, starting transfers between devices, body(): lax.ppermute(pair, SEQ, [(i, j) for i in range(1, SEQ_N - 1, 2) for i, j...  6.06 us
  transfers between devices with their start and end apart: 11, of which 6 were waited for; matrix products, arithmetic and copies ran while one was open for 13% of the time, Pallas kernels for 2%

profile of v2, /device:TPU:1, one launch (start us, length us, event | category | flops | bytes accessed | tf_op | source)
XLA Modules:
  0.0 224.0 jit_solution(9879375250216219442)
XLA Ops:
  0.6 5.9 %collective-permute-start = (bf16[3,24,768]{2,1,0:T(8,128)(2,1)}, bf16[3,24,768]{2,1,0:T(8,128)(2,1)S(1)}, u32[]{:S(2)}, u32[]{:S(2)}) collective-permute-start(bf16[3,24,768]{2,1,0:T(8,128)(2,1)} %bitcast.54), channel_id=1, source_target_pairs={{0,112},{16,96},{32,80},{48,64},{64,48},{80,32},{96,16},{112,0},{1... | collective-permute-start | bytes 331784 | tf_op jit(solution)/shard_map/ppermute | solution.py:99
  6.6 1.1 convert_reduce_fusion.1
  7.7 1.1 fusion.7
  8.8 0.7 broadcast_in_dim.47
  9.5 11.3 %all-to-all-start = ((f32[16,2,768]{2,1,0:T(2,128)}), f32[16,2,768]{2,1,0:T(2,128)S(1)}, u32[]{:S(2)}, u32[]{:S(2)}) async-start(f32[16,2,768]{2,1,0:T(2,128)} %broadcast_in_dim.47), calls=%async_computation | async-start | bytes 196608 | tf_op jit(solution)/shard_map/all_to_all | solution.py:27
  20.8 0.9 broadcast_select_fusion.11
  21.7 7.5 %all-to-all-done = f32[16,2,768]{2,1,0:T(2,128)S(1)} async-done(((f32[16,2,768]{2,1,0:T(2,128)}), f32[16,2,768]{2,1,0:T(2,128)S(1)}, u32[]{:S(2)}, u32[]{:S(2)}) %all-to-all-start) | async-done | bytes 98336 | tf_op jit(solution)/shard_map/all_to_all | solution.py:27
  29.5 16.7 %all_to_all.35 = f32[32,2,768]{2,1,0:T(2,128)S(1)} all-to-all(f32[32,2,768]{2,1,0:T(2,128)S(1)} %broadcast_in_dim.48), channel_id=1, replica_groups=mesh['x'=4,'yl'=4,'yh'=2,'z'=8,'c'=2] {'x','yl','yh'}, dimensions={0} | all-to-all | bytes 393216 | tf_op jit(solution)/shard_map/all_to_all | solution.py:27
  46.2 1.3 broadcast_in_dim.53
  47.5 3.7 %all-to-all-start.2 = ((bf16[8,3,48,768]{3,2,1,0:T(8,128)(2,1)}), bf16[8,3,48,768]{3,2,1,0:T(8,128)(2,1)S(1)}, u32[]{:S(2)}, u32[]{:S(2)}) async-start(bf16[8,3,48,768]{3,2,1,0:T(8,128)(2,1)} %broadcast_in_dim.53), calls=%async_computation.2 | async-start | bytes 3538944 | tf_op jit(solution)/shard_map/all_to_all | solution.py:27
  51.3 0.9 pad_maximum_fusion
  52.3 6.1 %collective-permute-start.2 = (bf16[512,768]{1,0:T(8,128)(2,1)}, bf16[512,768]{1,0:T(8,128)(2,1)S(1)}, u32[]{:S(2)}, u32[]{:S(2)}) collective-permute-start(bf16[512,768]{1,0:T(8,128)(2,1)} %pad_maximum_fusion), channel_id=1, source_target_pairs={{1,2},{2,1},{3,4},{4,3},{5,6},{6,5},{7,8},{8,7},{9,10},{10,9},{11,... | collective-permute-start | bytes 2359304 | tf_op jit(solution)/shard_map/ppermute | solution.py:103
  58.3 1.9 collective-permute-start.1
  60.8 0.6 fusion.67
  61.4 42.2 %collective-permute-done.2 = bf16[512,768]{1,0:T(8,128)(2,1)S(1)} collective-permute-done((bf16[512,768]{1,0:T(8,128)(2,1)}, bf16[512,768]{1,0:T(8,128)(2,1)S(1)}, u32[]{:S(2)}, u32[]{:S(2)}) %collective-permute-start.2) | collective-permute-done | bytes 786464 | tf_op jit(solution)/shard_map/ppermute | solution.py:103
  103.6 1.9 collective-permute-start.3
  106.1 1.1 collective-permute-done.3
  107.2 2.5 %broadcast_select_fusion.1 = (bf16[256,768]{1,0:T(8,128)(2,1)}, bf16[256,768]{1,0:T(8,128)(2,1)}, bf16[256,768]{1,0:T(8,128)(2,1)S(1)}, bf16[256,768]{1,0:T(8,12...) fusion(pred[]{:T(512)S(6)} %eq.54, ...), kind=kLoop, calls=%fused_computation.49 | loop fusion | flops 1572864 | bytes 6684673 | tf_op jit(solution)/shard_map/jit(_where)/select_n | solution.py:179
  109.8 0.7 multiply_convert_fusion.2
  110.5 1.5 fusion.23
  112.0 1.5 fusion.19
  113.6 2.2 collective-permute-start.4
  115.8 1.5 fusion.15
  117.3 1.5 fusion
  118.8 4.4 %all-to-all-start.3 = ((bf16[4,96,2304]{2,1,0:T(8,128)(2,1)}), bf16[4,96,2304]{2,1,0:T(8,128)(2,1)}, u32[]{:S(2)}, u32[]{:S(2)}) async-start(bf16[4,96,2304]{2,1,0:T(8,128)(2,1)} %bitcast.50), calls=%async_computation.3 | async-start | bytes 3538944 | tf_op jit(solution)/shard_map/all_to_all | solution.py:150
  123.2 1.3 fusion.4
  124.5 1.6 fusion.11
  126.1 19.7 %all-to-all-done.3 = bf16[4,96,2304]{2,1,0:T(8,128)(2,1)} async-done(((bf16[4,96,2304]{2,1,0:T(8,128)(2,1)}), bf16[4,96,2304]{2,1,0:T(8,128)(2,1)}, u32[]{:S(2)}, u32[]{:S(2)}) %all-to-all-start.3) | async-done | bytes 1769504 | tf_op jit(solution)/shard_map/all_to_all | solution.py:150
  145.8 2.6 %reduce_sum.129 = bf16[96,2304]{1,0:T(8,128)(2,1)} reduce(bf16[4,96,2304]{2,1,0:T(8,128)(2,1)} %all-to-all-done.3, bf16[]{:T(256)} %constant.128.clone.1), dimensions={0}, to_apply=%region_9.10 | reduce | flops 663552 | bytes 2211842 | tf_op jit(solution)/shard_map/reduce_sum | solution.py:182
  148.4 2.3 %reshape.235 = bf16[2,8,4,27,128]{4,3,2,1,0:T(8,128)(2,1)} reshape(bf16[96,2304]{1,0:T(8,128)(2,1)} %reduce_sum.129) | data formatting | bytes 884736 | tf_op jit(solution)/shard_map/reshape | solution.py:183
  150.8 2.3 %copy.22 = bf16[4,2,8,27,128]{4,1,0,3,2:T(2,128)(2,1)} copy(bf16[4,2,8,27,128]{4,3,0,2,1:T(8,128)(2,1)} %bitcast.51) | data formatting | bytes 884736 | tf_op jit(solution)/shard_map/transpose | solution.py:183
  153.1 1.1 copy-done.2
  154.2 1.1 copy-done.3
  155.3 1.1 copy-done.5
  156.3 1.0 copy-done.7
  157.3 1.0 copy-done.8
  158.3 4.6 %back.1 = (f32[256,768]{1,0:T(8,128)S(1)}, f32[2,768]{1,0:T(2,128)S(1)}) custom-call(bf16[256,768]{1,0:T(8,128)(2,1)S(1)} %copy-done.7, bf16[256,768]{1,0:T(8,128)(2,1)S(1)} %bitcast.49, bf16[256,768]{1,0:T(8,128)(2,1)S(1)} %copy-done.8, bf16[8,3,48,768]{3,2,1,0:T(8,128)(2,1)S(1)} %all-to-all-done.2.kc, bf16[8,3,48,768]{3,2,1,0:T(8,128)(2,1)} %collective-permute-done.4.ko, ...), custom_call_target="tpu_custom_call" | custom-call | flops 1509949440 | bytes 8388608 | tf_op jit(solution)/shard_map/back/pallas_call | solution.py:173
  163.0 0.9 copy-done.9
  163.8 3.3 %psum.7 = f32[2,768]{1,0:T(2,128)S(1)} all-reduce(f32[2,768]{1,0:T(2,128)S(1)} %get-tuple-element.20), channel_id=1, replica_groups=mesh['x'=4,'yl'=4,'yh'=2,'z'=8,'c'=2] {'c'}, use_global_device_ids=true, to_apply=%region_10.11 | all-reduce | flops 1536 | bytes 12288 | tf_op jit(solution)/shard_map/psum | solution.py:180
  167.2 1.1 pad_maximum_fusion.1
  168.3 0.8 copy.23
  169.1 3.5 %all-to-all-start.4 = ((bf16[8,240,128]{2,1,0:T(8,128)(2,1)}), bf16[8,240,128]{2,1,0:T(8,128)(2,1)S(1)}, u32[]{:S(2)}, u32[]{:S(2)}) async-start(bf16[8,240,128]{2,1,0:T(8,128)(2,1)} %copy.23), calls=%async_computation.4 | async-start | bytes 983040 | tf_op jit(solution)/shard_map/all_to_all | solution.py:185
  172.6 11.9 %all-to-all-done.4 = bf16[8,240,128]{2,1,0:T(8,128)(2,1)S(1)} async-done(((bf16[8,240,128]{2,1,0:T(8,128)(2,1)}), bf16[8,240,128]{2,1,0:T(8,128)(2,1)S(1)}, u32[]{:S(2)}, u32[]{:S(2)}) %all-to-all-start.4) | async-done | bytes 491552 | tf_op jit(solution)/shard_map/all_to_all | solution.py:185
  184.8 0.7 pad_maximum_fusion.3
  185.4 4.7 %all-to-all-start.5 = ((bf16[8,51,128]{2,1,0:T(8,128)(2,1)}), bf16[8,51,128]{2,1,0:T(8,128)(2,1)}, u32[]{:S(2)}, u32[]{:S(2)}) async-start(bf16[8,51,128]{2,1,0:T(8,128)(2,1)} %pad_maximum_fusion.3), calls=%async_computation.5 | async-start | bytes 229376 | tf_op jit(solution)/shard_map/all_to_all | solution.py:190
  190.2 2.5 %broadcast_select_fusion.2 = (bf16[256,768]{1,0:T(8,128)(2,1)}, bf16[256,768]{1,0:T(8,128)(2,1)}, bf16[256,768]{1,0:T(8,128)(2,1)}) fusion(pred[]{:T(512)S(6)} %eq.54, f32[768]{0:T(1024)S(1)} %copy-done.19, f32[768]{0:T(1024)S(1)} %get-tuple-element.50, f32[768]{0:T(1024)S(1)} %broadcast_multiply_fusion.1, bf16[256,768]{1,0:T(8,128)(2,1)} %get-tuple-element.15, ...), kind=kLoop, calls=%fused_computation.50 | loop fusion | flops 4325376 | bytes 1978370 | tf_op jit(solution)/shard_map/jit(_where)/select_n | solution.py:204
  192.7 5.4 %all-to-all-done.5 = bf16[8,51,128]{2,1,0:T(8,128)(2,1)} async-done(((bf16[8,51,128]{2,1,0:T(8,128)(2,1)}), bf16[8,51,128]{2,1,0:T(8,128)(2,1)}, u32[]{:S(2)}, u32[]{:S(2)}) %all-to-all-start.5) | async-done | bytes 104480 | tf_op jit(solution)/shard_map/all_to_all | solution.py:190
  198.0 0.9 convert_reduce_fusion.2
  199.0 0.6 slice.169
  199.6 0.6 reshape.239
  200.2 0.7 reduce-precision_convert_fusion
  200.9 0.6 reshape.240
  201.5 0.7 pad_maximum_fusion.4
  202.2 0.7 broadcast_in_dim.59
  202.9 7.4 %all-to-all-start.6 = ((bf16[16,51,128]{2,1,0:T(8,128)(2,1)}), bf16[16,51,128]{2,1,0:T(8,128)(2,1)}, u32[]{:S(2)}, u32[]{:S(2)}) async-start(bf16[16,51,128]{2,1,0:T(8,128)(2,1)} %broadcast_in_dim.59), calls=%async_computation.6 | async-start | bytes 458752 | tf_op jit(solution)/shard_map/all_to_all | solution.py:27
  210.3 1.1 broadcast_select_fusion.3.a0
  211.4 1.1 copy-done.6
  212.5 1.0 copy-done.12
  213.4 5.5 %forward.1 = bf16[256,768]{1,0:T(8,128)(2,1)} custom-call(bf16[256,768]{1,0:T(8,128)(2,1)S(1)} %broadcast_select_fusion.3.a0, bf16[256,768]{1,0:T(8,128)(2,1)S(1)} %copy-done.11, bf16[256,768]{1,0:T(8,128)(2,1)S(1)} %copy-done.12, bf16[8,3,48,768]{3,2,1,0:T(8,128)(2,1)S(1)} %all-to-all-done.2.kc, bf16[8,3,48,768]{3,2,1,0:T(8,128)(2,1)} %collective-permute-done.4.ko, ...), custom_call_target="tpu_custom_call" | custom-call | flops 1811939328 | bytes 6291456 | tf_op jit(solution)/shard_map/forward/pallas_call | solution.py:197
  219.0 1.0 convert_element_type.91
  220.6 0.6 broadcast_multiply_fusion
  221.2 0.9 slice.137
  222.3 0.7 copy.24
  223.0 1.0 fusion.29
  (86 shorter events, 2.3 us)
Async XLA Ops:
  0.6 20.1 %collective-permute-start = (bf16[3,24,768]{2,1,0:T(8,128)(2,1)}, bf16[3,24,768]{2,1,0:T(8,128)(2,1)S(1)}, u32[]{:S(2)}, u32[]{:S(2)}) collective-permute-start(bf16[3,24,768]{2,1,0:T(8,128)(2,1)} %bitcast.54), channel_id=1, source_target_pairs={{0,112},{16,96},{32,80},{48,64},{64,48},{80,32},{96,16},{112,0},{1... | collective-permute-start | bytes 331784 | tf_op jit(solution)/shard_map/ppermute | solution.py:99
  9.5 19.8 %all-to-all-start = ((f32[16,2,768]{2,1,0:T(2,128)}), f32[16,2,768]{2,1,0:T(2,128)S(1)}, u32[]{:S(2)}, u32[]{:S(2)}) async-start(f32[16,2,768]{2,1,0:T(2,128)} %broadcast_in_dim.47), calls=%async_computation | async-start | bytes 196608 | tf_op jit(solution)/shard_map/all_to_all | solution.py:27
  47.5 3.8 %copy-start = (bf16[1,256,768]{2,1,0:T(8,128)(2,1)S(1)}, bf16[1,256,768]{2,1,0:T(8,128)(2,1)}, u32[]{:S(2)}) copy-start(bf16[1,256,768]{2,1,0:T(8,128)(2,1)} %param.5) | copy-start | bytes 1179652
  47.5 3.8 %copy-start.1 = (bf16[1,256,768]{2,1,0:T(8,128)(2,1)S(1)}, bf16[1,256,768]{2,1,0:T(8,128)(2,1)}, u32[]{:S(2)}) copy-start(bf16[1,256,768]{2,1,0:T(8,128)(2,1)} %param.9) | copy-start | bytes 1179652
  47.5 66.0 %all-to-all-start.2 = ((bf16[8,3,48,768]{3,2,1,0:T(8,128)(2,1)}), bf16[8,3,48,768]{3,2,1,0:T(8,128)(2,1)S(1)}, u32[]{:S(2)}, u32[]{:S(2)}) async-start(bf16[8,3,48,768]{3,2,1,0:T(8,128)(2,1)} %broadcast_in_dim.53), calls=%async_computation.2 | async-start | bytes 3538944 | tf_op jit(solution)/shard_map/all_to_all | solution.py:27
  51.3 9.0 %copy-start.19 = (f32[768]{0:T(1024)S(1)}, f32[768]{0:T(1024)}, u32[]{:S(2)}) copy-start(f32[768]{0:T(1024)} %param.7) | copy-start | bytes 9220
  51.3 9.0 %copy-start.18 = (f32[768]{0:T(1024)S(1)}, f32[768]{0:T(1024)}, u32[]{:S(2)}) copy-start(f32[768]{0:T(1024)} %param.6) | copy-start | bytes 9220
  52.3 51.3 %collective-permute-start.2 = (bf16[512,768]{1,0:T(8,128)(2,1)}, bf16[512,768]{1,0:T(8,128)(2,1)S(1)}, u32[]{:S(2)}, u32[]{:S(2)}) collective-permute-start(bf16[512,768]{1,0:T(8,128)(2,1)} %pad_maximum_fusion), channel_id=1, source_target_pairs={{1,2},{2,1},{3,4},{4,3},{5,6},{6,5},{7,8},{8,7},{9,10},{10,9},{11,... | collective-permute-start | bytes 2359304 | tf_op jit(solution)/shard_map/ppermute | solution.py:103
  58.3 47.8 %collective-permute-start.1 = (bf16[512,768]{1,0:T(8,128)(2,1)}, bf16[512,768]{1,0:T(8,128)(2,1)}, u32[]{:S(2)}, u32[]{:S(2)}) collective-permute-start(bf16[512,768]{1,0:T(8,128)(2,1)} %pad_maximum_fusion), channel_id=1, source_target_pairs={{0,1},{1,0},{2,3},{3,2},{4,5},{5,4},{6,7},{7,6},{8,9},{9,8},{10,11... | collective-permute-start | bytes 2359304 | tf_op jit(solution)/shard_map/ppermute | solution.py:102
  103.6 3.6 %collective-permute-start.3 = (bf16[256,768]{1,0:T(8,128)(2,1)S(1)}, bf16[256,768]{1,0:T(8,128)(2,1)S(1)}, u32[]{:S(2)}, u32[]{:S(2)}) collective-permute-start(bf16[256,768]{1,0:T(8,128)(2,1)S(1)} %slice.124), channel_id=1, source_target_pairs={{0,1},{1,0},{2,3},{3,2},{4,5},{5,4},{6,7},{7,6},{8,9},{9,8},{10,11... | collective-permute-start | bytes 1179656 | tf_op jit(solution)/shard_map/ppermute | solution.py:106
  109.8 2.3 %copy-start.17 = (bf16[256,768]{1,0:T(8,128)(2,1)}, bf16[256,768]{1,0:T(8,128)(2,1)S(1)}, u32[]{:S(2)}) copy-start(bf16[256,768]{1,0:T(8,128)(2,1)S(1)} %get-tuple-element.56) | copy-start | bytes 1179652
  112.0 3.7 %copy-start.16 = (bf16[256,768]{1,0:T(8,128)(2,1)S(1)}, bf16[256,768]{1,0:T(8,128)(2,1)}, u32[]{:S(2)}) copy-start(bf16[256,768]{1,0:T(8,128)(2,1)} %get-tuple-element.55) | copy-start | bytes 1179652
  113.6 3.7 %copy-start.14 = (f32[384,768]{1,0:T(8,128)S(1)}, f32[384,768]{1,0:T(8,128)}, u32[]{:S(2)}) copy-start(f32[384,768]{1,0:T(8,128)} %fusion.23) | copy-start | bytes 3538948
  113.6 3.7 %copy-start.15 = (f32[384,768]{1,0:T(8,128)S(1)}, f32[384,768]{1,0:T(8,128)}, u32[]{:S(2)}) copy-start(f32[384,768]{1,0:T(8,128)} %fusion.19) | copy-start | bytes 3538948
  113.6 39.5 %collective-permute-start.4 = (bf16[8,3,48,768]{3,2,1,0:T(8,128)(2,1)S(1)}, bf16[8,3,48,768]{3,2,1,0:T(8,128)(2,1)}, u32[]{:S(2)}, u32[]{:S(2)}) collective-permute-start(bf16[8,3,48,768]{3,2,1,0:T(8,128)(2,1)S(1)} %all-to-all-done.2.kc), channel_id=1, source_target_pairs={{0,1},{1,0},{2,3},{3,2},{4,5},{5,4},{6,7},{7,6},{8,9},{9,8},{10,11... | collective-permute-start | bytes 5308424 | tf_op jit(solution)/shard_map/ppermute | solution.py:167
  118.8 27.0 %all-to-all-start.3 = ((bf16[4,96,2304]{2,1,0:T(8,128)(2,1)}), bf16[4,96,2304]{2,1,0:T(8,128)(2,1)}, u32[]{:S(2)}, u32[]{:S(2)}) async-start(bf16[4,96,2304]{2,1,0:T(8,128)(2,1)} %bitcast.50), calls=%async_computation.3 | async-start | bytes 3538944 | tf_op jit(solution)/shard_map/all_to_all | solution.py:150
  153.1 1.1 copy-start.2
  154.2 1.1 copy-start.3
  155.2 1.1 copy-start.5
  156.3 1.0 copy-start.7
  157.3 1.0 copy-start.8
  162.9 0.9 copy-start.9
  168.2 21.9 %copy-start.13 = (bf16[256,768]{1,0:T(8,128)(2,1)S(1)}, bf16[256,768]{1,0:T(8,128)(2,1)}, u32[]{:S(2)}) copy-start(bf16[256,768]{1,0:T(8,128)(2,1)} %get-tuple-element.14) | copy-start | bytes 1179652
  169.1 15.4 %all-to-all-start.4 = ((bf16[8,240,128]{2,1,0:T(8,128)(2,1)}), bf16[8,240,128]{2,1,0:T(8,128)(2,1)S(1)}, u32[]{:S(2)}, u32[]{:S(2)}) async-start(bf16[8,240,128]{2,1,0:T(8,128)(2,1)} %copy.23), calls=%async_computation.4 | async-start | bytes 983040 | tf_op jit(solution)/shard_map/all_to_all | solution.py:185
  185.4 12.6 %all-to-all-start.5 = ((bf16[8,51,128]{2,1,0:T(8,128)(2,1)}), bf16[8,51,128]{2,1,0:T(8,128)(2,1)}, u32[]{:S(2)}, u32[]{:S(2)}) async-start(bf16[8,51,128]{2,1,0:T(8,128)(2,1)} %pad_maximum_fusion.3), calls=%async_computation.5 | async-start | bytes 229376 | tf_op jit(solution)/shard_map/all_to_all | solution.py:190
  192.7 18.7 %copy-start.4 = (bf16[384,768]{1,0:T(8,128)(2,1)S(1)}, bf16[384,768]{1,0:T(8,128)(2,1)}, u32[]{:S(2)}) copy-start(bf16[384,768]{1,0:T(8,128)(2,1)} %get-tuple-element.86.sc) | copy-start | bytes 1769476
  192.7 18.7 %copy-start.11 = (bf16[256,768]{1,0:T(8,128)(2,1)S(1)}, bf16[256,768]{1,0:T(8,128)(2,1)}, u32[]{:S(2)}) copy-start(bf16[256,768]{1,0:T(8,128)(2,1)} %get-tuple-element.71.a1) | copy-start | bytes 1179652
  202.9 16.0 %all-to-all-start.6 = ((bf16[16,51,128]{2,1,0:T(8,128)(2,1)}), bf16[16,51,128]{2,1,0:T(8,128)(2,1)}, u32[]{:S(2)}, u32[]{:S(2)}) async-start(bf16[16,51,128]{2,1,0:T(8,128)(2,1)} %broadcast_in_dim.59), calls=%async_computation.6 | async-start | bytes 458752 | tf_op jit(solution)/shard_map/all_to_all | solution.py:27
  211.4 1.1 copy-start.6
  212.4 1.0 copy-start.12
  219.0 4.0 %copy-start.10 = (f32[256,768]{1,0:T(8,128)S(1)}, f32[256,768]{1,0:T(8,128)}, u32[]{:S(2)}) copy-start(f32[256,768]{1,0:T(8,128)} %copy-done.9) | copy-start | bytes 2359300
  219.0 4.0 %copy-start.20 = (f32[768]{0:T(1024)S(1)}, f32[768]{0:T(1024)}, u32[]{:S(2)}) copy-start(f32[768]{0:T(1024)} %get-tuple-element.49) | copy-start | bytes 9220

commit v3 on v0

v3 whole, which is shorter than its diff:
```python
import jax
import jax.numpy as jnp
from jax import lax
from jax.experimental import pallas as pl
from jax.experimental.pallas import tpu as pltpu
from jax.sharding import Mesh, PartitionSpec as P

F32 = jnp.float32
BF16 = jnp.bfloat16
AXES = ("x", "yl", "yh", "z", "c")
NX, NYL, NYH, NZ, NC = 4, 4, 2, 8, 2
SEQ = ("yh", "z", "c")
SEQ_N = NYH * NZ * NC
C = 768
HALF = C // 2
L = 256
ROWS = 24
OWNERS = NYH * NZ
SUB = ROWS // NX
PIECE = 27
TOT = 24
MSG = 64
COUNT = L * SEQ_N * NX * NYL
NORM = float(COUNT) ** -0.5
SQRT_HALF = 0.7071067811865476
INV_SQRT_2PI = 0.3989422804014327
NT = (((1,), (1,)), ((), ()))
TN = (((0,), (0,)), ((), ()))


def call(kernel, out_shape, name, megabytes, flops=0, size=1 << 20, smem=False, scratch=()):
    specs = None
    params = pltpu.CompilerParams(vmem_limit_bytes=megabytes * 1024 * 1024)
    estimate = pl.CostEstimate(flops=flops, bytes_accessed=size, transcendentals=0)
    extra = {}
    if smem:
        extra["in_specs"] = [pl.BlockSpec(memory_space=pltpu.SMEM)] + [
            pl.BlockSpec(memory_space=pltpu.VMEM)
        ] * (smem - 1)
    return pl.pallas_call(
        kernel, out_shape=out_shape, compiler_params=params, cost_estimate=estimate, name=name,
        scratch_shapes=list(scratch), **extra,
    )


def spread(value, n):
    return jnp.broadcast_to(value[None], (n,) + value.shape)


def stats_kernel(inputs, message):
    values = inputs[...].astype(F32)
    total = jnp.sum(values, axis=0, keepdims=True)
    off = values - total / L
    squares = jnp.sum(off * off, axis=0, keepdims=True)
    message[...] = spread(jnp.concatenate([total, squares], axis=0), NZ * NC)


def merged(parts, count):
    sums, squares = parts[:, 0, :], parts[:, 1, :]
    n = sums.shape[0]
    total = jnp.sum(sums, axis=0, keepdims=True)
    off = sums / count - total / (count * n)
    return total, jnp.sum(squares, axis=0, keepdims=True) + count * jnp.sum(off * off, axis=0, keepdims=True)


def merge_kernel(parts, message):
    total, squares = merged(parts[...], L)
    message[...] = spread(jnp.concatenate([total, squares], axis=0), NX * NYL * NYH)


def one_hot(channels):
    rows = lax.broadcasted_iota(jnp.int32, (C, channels.shape[1]), 0)
    return jnp.where(rows == channels[...], 1.0, 0.0).astype(BF16)


def normalised(block, vectors):
    return (block - vectors[0:1]) * vectors[1:2]


def half_gate(v):
    return 0.5 * (1.0 + lax.erf(v * SQRT_HALF))


def terms_kernel(place, parts, gain, shift, source, inputs, mate, cot, outer, far, terms, vectors):
    total, squares = merged(parts[...], L * NZ * NC)
    mean = total / COUNT
    inv_std = lax.rsqrt(squares / COUNT + 1e-05)
    rows = jnp.concatenate([mean, inv_std, gain[...], shift[...]], axis=0)
    vectors[...] = rows
    pick = one_hot(source)
    chosen, rest = jnp.zeros((4, HALF), F32), rows
    for _ in range(3):
        part = rest.astype(BF16)
        chosen += jnp.dot(part, pick, preferred_element_type=F32)
        rest = rest - part.astype(F32)
    low = place[0] == 0
    both = jnp.concatenate([inputs[...], mate[L:]], axis=0)
    v = normalised(jnp.dot(both, pick, preferred_element_type=F32), chosen)
    v = chosen[2:3] * v + chosen[3:4]
    act = (v * half_gate(v)).astype(BF16)
    own, next_own, last_own = cot[...], mate[:L], outer[...]
    beyond = far[...]
    cots = (
        (jnp.where(low, next_own, last_own), jnp.where(low, beyond, own)),
        (own, next_own),
        (jnp.where(low, last_own, next_own), jnp.where(low, own, beyond)),
    )
    for tap, pair in enumerate(cots):
        block = lax.dot_general(act, jnp.concatenate(pair, axis=0), TN, preferred_element_type=F32)
        terms[:, tap * C : (tap + 1) * C] = (block * NORM).astype(BF16)


def by_tap(parts, tap):
    return jnp.concatenate([part[:, tap].reshape(-1, C) for part in parts], axis=0)


def back_kernel(place, vectors, inputs, mate, cot, outer, own, mine, theirs, channel, pre_grad, totals):
    low = place[0] == 0
    taps = (
        jnp.where(low, mate[:L], outer[...]),
        cot[...],
        jnp.where(low, outer[...], mate[:L]),
    )
    total = jnp.zeros((L, C), F32)
    for tap, q in enumerate(taps):
        total += lax.dot_general(q, by_tap((own, mine, theirs), tap), NT, preferred_element_type=F32)
    high = total.astype(BF16)
    rest = (total - high.astype(F32)).astype(BF16)
    pick = one_hot(channel)
    total = lax.dot_general(high, pick, NT, preferred_element_type=F32)
    total += lax.dot_general(rest, pick, NT, preferred_element_type=F32)
    rows = vectors[...]
    normed = normalised(inputs[...].astype(F32), rows)
    v = rows[2:3] * normed + rows[3:4]
    grad = total * (half_gate(v) + v * (INV_SQRT_2PI * jnp.exp(-0.5 * v * v)))
    pre_grad[...] = grad
    totals[...] = jnp.concatenate(
        [jnp.sum(grad, axis=0, keepdims=True), jnp.sum(grad * normed, axis=0, keepdims=True)], axis=0
    )


def put_totals(totals, held):
    high = totals.astype(BF16).astype(F32)
    rows = jnp.concatenate([high, totals - high], axis=0)
    for tile in range(6):
        held[4 * tile : 4 * tile + 4] = rows[:, 128 * tile : 128 * tile + 128]
    return held[:TOT].astype(BF16)


def get_totals(held):
    rows = jnp.concatenate([held[4 * tile : 4 * tile + 4] for tile in range(6)], axis=1)
    return rows[0:2] + rows[2:4]


def first_kernel(got, message):
    parts = got[...].astype(F32)
    total = jnp.sum(parts, axis=0)
    zero = jnp.zeros((8, 128), F32)
    for l in range(NYL):
        for h in range(NYH):
            tiles = []
            for piece in range(PIECE):
                sub, tile = divmod(l * PIECE + piece, 18)
                row = sub * OWNERS + h * NZ
                tiles.append(total[row : row + 8, 128 * tile : 128 * tile + 128])
            tiles.append(zero)
            message[l * NYH + h] = jnp.concatenate(tiles, axis=0).astype(BF16)


def second_kernel(got, totals, totals_y, message, held, line):
    total = jnp.sum(got[...].astype(F32), axis=0)
    packed = put_totals(totals[...] + totals_y[...], held).astype(F32)
    for piece in range(PIECE):
        line[:, TOT + piece, :] = total[piece * 8 : piece * 8 + 8]
    for z in range(NZ):
        line[z, :TOT] = packed
        line[z, TOT + PIECE :] = jnp.zeros((MSG - TOT - PIECE, 128), F32)
    message[...] = line[...].astype(BF16)


def third_kernel(got, message, held):
    total = jnp.sum(got[...].astype(F32), axis=0)
    held[...] = total[:32]
    packed = put_totals(get_totals(held), held)
    message[...] = spread(jnp.concatenate([packed, total[TOT:].astype(BF16)], axis=0), NX * NYL)


def last_kernel(got, vectors, inputs, cot, pre_grad, grad_in, scaled, held):
    total = jnp.zeros((32, 128), F32)
    for member in range(NX * NYL):
        total += got[member, :32].astype(F32)
    held[...] = total
    totals = get_totals(held)
    scaled[...] = totals * NORM
    rows = vectors[...]
    normed = normalised(inputs[...].astype(F32), rows)
    bn_grad = (rows[2:3] * rows[1:2]) * (
        pre_grad[...] - totals[0:1] / COUNT - normed * (totals[1:2] / COUNT)
    )
    grad_in[...] = (cot[...].astype(F32) + bn_grad).astype(BF16)


def forward_kernel(place, vectors, inputs, mate, outer, own, mine, theirs, channel, output):
    rows = vectors[...]

    def activate(block):
        v = rows[2:3] * normalised(block.astype(F32), rows) + rows[3:4]
        return v * half_gate(v)

    low = place[0] == 0
    here = activate(inputs[...]).astype(BF16)
    near = activate(mate[L:]).astype(BF16)
    away = jnp.where(place[1] == 1, activate(outer[...]), 0.0).astype(BF16)
    taps = (jnp.where(low, away, near), here, jnp.where(low, near, away))
    total = inputs[...].astype(F32)
    pick = one_hot(channel)
    for tap, a in enumerate(taps):
        chosen = jnp.dot(a, pick, preferred_element_type=F32).astype(BF16)
        total += jnp.dot(chosen, by_tap((own, mine, theirs), tap), preferred_element_type=F32)
    output[...] = total.astype(BF16)


def shape(*dims, kind=F32):
    return jax.ShapeDtypeStruct(dims, kind)


def exchange(value, axes):
    return lax.all_to_all(value, axes, 0, 0, tiled=True)


def from_side(value, distance):
    route = []
    for z in range(NZ):
        route.append((((z + distance) % NZ) * NC, z * NC))
        route.append((((z - distance) % NZ) * NC + 1, z * NC + 1))
    return lax.ppermute(value, ("z", "c"), route)


def body(inputs, gain, shift, kernel, cotangent):
    yh, zi, ci = lax.axis_index("yh"), lax.axis_index("z"), lax.axis_index("c")
    inputs, cotangent = inputs[0], cotangent[0]
    gain, shift = gain[None], shift[None]
    seq = (yh * NZ + zi) * NC + ci
    has_outer = jnp.logical_and(seq > 0, seq < SEQ_N - 1).astype(jnp.int32)
    place = jnp.stack([ci, has_outer])
    order = jnp.arange(HALF)
    quarter, row, owner = order // 96, (order // OWNERS) % SUB, order % OWNERS
    source = ((owner * NC + ci) * ROWS + quarter * SUB + row)[None]
    side = 1 - 2 * ci
    ones = [(1, 0), (1, 1), (2, 0), (2, 1), (3, 0), (3, 1)]
    steps = [(zi, 0), (zi, 1)] + [(zi + side * d, p) for d, p in ones] + [(zi + 4, ci)]
    steps += [(zi - side * d, p) for d, p in ones] + [(zi + 4, 1 - ci)]
    base = jnp.stack([(z % NZ) * NC + p for z, p in steps])
    inner = jnp.arange(NYH * ROWS)
    inner = (inner // ROWS) * (NZ * NC * ROWS) + inner % ROWS
    channel = (base[:, None] * ROWS + inner[None]).reshape(1, C)
    swap_c = [(0, 1), (1, 0)]
    swap_out = [(i, j) for i in range(1, SEQ_N - 1, 2) for i, j in ((i, i + 1), (i + 1, i))]
    swap_y = []
    for l in range(NYL):
        for h in range(NYH):
            y = 7 - (h * NYL + l)
            swap_y.append((l * NYH + h, (y % NYL) * NYH + y // NYL))

    stats = call(stats_kernel, shape(NZ * NC, 2, C), "stats", 8)(inputs)
    stats, held_cot, own = lax.optimization_barrier((stats, cotangent, kernel))
    own = own.transpose(1, 0, 2)
    same = lax.ppermute(own, "c", swap_c)
    outer = lax.ppermute(held_cot, SEQ, swap_out)
    low = ci == 0
    own = jnp.stack([jnp.where(low, own, same), jnp.where(low, same, own)])
    other = lax.ppermute(own, ("yl", "yh"), swap_y)
    stats = exchange(stats, ("z", "c"))

    first = yh == 0
    own = jnp.concatenate([jnp.where(first, own, other), jnp.where(first, other, own)], axis=2)
    stats, own, outer, held_in, held_cot = lax.optimization_barrier((stats, own, outer, inputs, cotangent))
    near = from_side(own, 1)
    mate = lax.ppermute(jnp.concatenate([held_cot, held_in], axis=0), "c", swap_c)
    far = lax.ppermute(outer, "c", swap_c)
    stats = call(merge_kernel, shape(NX * NYL * NYH, 2, C), "merge", 8)(stats)
    stats = exchange(stats, ("x", "yl", "yh"))
    stats, near = lax.optimization_barrier((stats, near))
    pair = from_side(jnp.concatenate([own, near], axis=0), 2)

    terms, vectors = call(
        terms_kernel, (shape(HALF, 3 * C, kind=BF16), shape(4, C)), "terms", 24, smem=10,
        flops=2 * 512 * HALF * C * 4, size=6 << 20,
    )(place, stats, gain, shift, source, inputs, mate, cotangent, outer, far)
    terms = exchange(terms.reshape(NX, HALF // NX, 3 * C), "x")

    across = from_side(jnp.where(low, pair[2], pair[3]), 1)
    mine = jnp.concatenate([near, pair, across[None]], axis=0)
    theirs = lax.ppermute(mine, "c", swap_c)
    pre_grad, totals = call(
        back_kernel, (shape(L, C), shape(2, C)), "back", 32, smem=10,
        flops=2 * L * C * C * 5, size=8 << 20,
    )(place, vectors, inputs, mate, cotangent, outer, own, mine, theirs, channel)
    totals = lax.psum(totals, "c")
    totals_y = lax.ppermute(totals, ("yl", "yh"), swap_y)

    held = pltpu.VMEM((32, 128), F32)
    message = call(first_kernel, shape(8, 224, 128, kind=BF16), "first", 12)(terms)
    message, late_in = lax.optimization_barrier((message, inputs))
    outer_in = lax.ppermute(late_in, SEQ, swap_out)
    got = exchange(message, ("yl", "yh"))
    message = call(
        second_kernel, shape(NZ, MSG, 128, kind=BF16), "second", 12,
        scratch=[held, pltpu.VMEM((NZ, MSG, 128), F32)],
    )(got, totals, totals_y)
    got = exchange(message, "z")
    message = call(third_kernel, shape(NX * NYL, MSG, 128, kind=BF16), "third", 12, scratch=[held])(got)
    got = exchange(message, ("x", "yl"))
    output = call(
        forward_kernel, shape(L, C, kind=BF16), "forward", 32, smem=9,
        flops=2 * L * C * C * 6, size=6 << 20,
    )(place, vectors, inputs, mate, outer_in, own, mine, theirs, channel)
    grad_in, scaled = call(
        last_kernel, (shape(L, C, kind=BF16), shape(2, C)), "last", 12, scratch=[held]
    )(got, vectors, inputs, cotangent, pre_grad)
    weight_grad = got[:, TOT : TOT + PIECE].astype(F32).reshape(ROWS, 3, C)
    return (output[None], grad_in[None], weight_grad, scaled[1], scaled[0])


def solution(mesh):
    split_mesh = Mesh(mesh.devices.reshape(NX, NYL, NYH, NZ, NC), AXES)
    rows = P(("x", "yl"), SEQ, None)
    return jax.shard_map(
        body,
        mesh=split_mesh,
        in_specs=(rows, P(), P(), P(SEQ, None, None), rows),
        out_specs=(rows, rows, P(SEQ, None, None), P(), P()),
        check_vma=False,
    )
```

time: 663 us -> 163 us (0.25)
  the two profiles are of different devices: /device:TPU:1 before, /device:TPU:48 now
where the time goes in v3:
time: 163 us; the launch traced here: 162 us
  starting transfers between devices  74.2 us (46%)
  waiting for transfers between devices  52.2 us (32%)
  Pallas kernels  18.3 us (11%)
  local copies, waits for them, and re-layouts  7.13 us (4%)
  other arithmetic  6.84 us (4%)
  blocking collectives  2.49 us (2%)
    all_to_all x6, starting transfers between devices, exchange(): return lax.all_to_all(value, axes, 0, 0, tiled=True)  34.5 us
    ppermute x3, waiting for transfers between devices, from_side(): return lax.ppermute(value, ('z', 'c'), route)  18.2 us
    all_to_all x6, waiting for transfers between devices, exchange(): return lax.all_to_all(value, axes, 0, 0, tiled=True)  17.2 us
    ppermute x1, starting transfers between devices, body(): outer = lax.ppermute(held_cot, SEQ, swap_out)  14.8 us
    ppermute x1, waiting for transfers between devices, body(): outer_in = lax.ppermute(late_in, SEQ, swap_out)  7.48 us
    unnamed x27, local copies, waits for them, and re-layouts  6.23 us
    ppermute x3, starting transfers between devices, from_side(): return lax.ppermute(value, ('z', 'c'), route)  5.74 us
    pallas_call x1, Pallas kernels, body(): call(forward_kernel, shape(L, C, kind=BF16), 'forward', 32, smem=9, flops...  5.29 us
  transfers between devices with their start and end apart: 17, of which 11 were waited for; matrix products, arithmetic and copies ran while one was open for 4% of the time, Pallas kernels for 9%

profile of v3, /device:TPU:48, one launch (start us, length us, event | category | flops | bytes accessed | tf_op | source)
XLA Modules:
  0.0 162.1 jit_solution(1803127964256862088)
XLA Ops:
  0.6 0.0 copy-start
  0.6 1.0 copy-done
  1.6 0.8 stats.1
  2.5 1.9 %collective-permute-start = (bf16[3,24,768]{2,1,0:T(8,128)(2,1)}, bf16[3,24,768]{2,1,0:T(8,128)(2,1)S(1)}, u32[]{:S(2)}, u32[]{:S(2)}) collective-permute-start(bf16[3,24,768]{2,1,0:T(8,128)(2,1)} %bitcast.47), channel_id=1, source_target_pairs={{0,1},{1,0},{2,3},{3,2},{4,5},{5,4},{6,7},{7,6},{8,9},{9,8},{10,11... | collective-permute-start | bytes 331784 | tf_op jit(solution)/shard_map/ppermute | solution.py:268
  4.4 1.5 collective-permute-done
  5.9 0.9 select_bitcast_fusion.1
  6.8 0.0 copy-start.1
  6.8 0.0 copy-start.3
  6.9 2.9 %collective-permute-start.1 = (bf16[2,3,24,768]{3,2,1,0:T(8,128)(2,1)S(1)}, bf16[2,3,24,768]{3,2,1,0:T(8,128)(2,1)S(1)}, u32[]{:S(2)}, u32[]{:S(2)}) collective-permute-start(bf16[2,3,24,768]{3,2,1,0:T(8,128)(2,1)S(1)} %pad_maximum_fusion.4), channel_id=1, source_target_pairs={{0,112},{16,96},{32,80},{48,64},{64,48},{80,32},{96,16},{112,0},{1... | collective-permute-start | bytes 663560 | tf_op jit(solution)/shard_map/ppermute | solution.py:272
  9.8 14.8 %collective-permute-start.2 = (bf16[256,768]{1,0:T(8,128)(2,1)}, bf16[256,768]{1,0:T(8,128)(2,1)S(1)}, u32[]{:S(2)}, u32[]{:S(2)}) collective-permute-start(bf16[256,768]{1,0:T(8,128)(2,1)} %bitcast.41), channel_id=1, source_target_pairs={{1,2},{2,1},{3,4},{4,3},{5,6},{6,5},{7,8},{8,7},{9,10},{10,9},{11,... | collective-permute-start | bytes 1179656 | tf_op jit(solution)/shard_map/ppermute | solution.py:269
  24.6 3.5 %all-to-all-start = ((f32[16,2,768]{2,1,0:T(2,128)}), f32[16,2,768]{2,1,0:T(2,128)S(1)}, u32[]{:S(2)}, u32[]{:S(2)}) async-start(f32[16,2,768]{2,1,0:T(2,128)} %stats.1), calls=%async_computation | async-start | bytes 196608 | tf_op jit(solution)/shard_map/all_to_all | solution.py:228
  28.1 0.1 broadcast_select_fusion.1
  28.2 8.8 %all-to-all-done.parts = f32[16,2,768]{2,1,0:T(2,128)S(1)} async-done(((f32[16,2,768]{2,1,0:T(2,128)}), f32[16,2,768]{2,1,0:T(2,128)S(1)}, u32[]{:S(2)}, u32[]{:S(2)}) %all-to-all-start) | async-done | bytes 98336 | tf_op jit(solution)/shard_map/all_to_all | solution.py:228
  37.0 1.2 collective-permute-done.2.outer
  38.2 1.9 %collective-permute-start.3 = (bf16[2,3,48,768]{3,2,1,0:T(8,128)(2,1)S(1)}, bf16[2,3,48,768]{3,2,1,0:T(8,128)(2,1)S(1)}, u32[]{:S(2)}, u32[]{:S(2)}) collective-permute-start(bf16[2,3,48,768]{3,2,1,0:T(8,128)(2,1)S(1)} %pad_maximum_fusion.3.own), channel_id=1, source_target_pairs={{2,0},{15,1},{4,2},{1,3},{6,4},{3,5},{8,6},{5,7},{10,8},{7,9},{12,... | collective-permute-start | bytes 1327112 | tf_op jit(solution)/shard_map/ppermute | solution.py:236
  40.1 0.8 merge.1
  40.9 11.3 %all-to-all-start.1 = ((f32[32,2,768]{2,1,0:T(2,128)}), f32[32,2,768]{2,1,0:T(2,128)S(1)}, u32[]{:S(2)}, u32[]{:S(2)}) async-start(f32[32,2,768]{2,1,0:T(2,128)} %merge.1), calls=%async_computation.1 | async-start | bytes 393216 | tf_op jit(solution)/shard_map/all_to_all | solution.py:228
  52.2 0.0 copy-start.11
  52.2 0.0 copy-start.12
  52.3 1.0 pad_maximum_fusion.2
  53.2 1.9 %collective-permute-start.4 = (bf16[512,768]{1,0:T(8,128)(2,1)}, bf16[512,768]{1,0:T(8,128)(2,1)S(1)}, u32[]{:S(2)}, u32[]{:S(2)}) collective-permute-start(bf16[512,768]{1,0:T(8,128)(2,1)} %pad_maximum_fusion.2), channel_id=1, source_target_pairs={{0,1},{1,0},{2,3},{3,2},{4,5},{5,4},{6,7},{7,6},{8,9},{9,8},{10,11... | collective-permute-start | bytes 2359304 | tf_op jit(solution)/shard_map/ppermute | solution.py:279
  55.1 4.5 %all-to-all-done.1.parts = f32[32,2,768]{2,1,0:T(2,128)S(1)} async-done(((f32[32,2,768]{2,1,0:T(2,128)}), f32[32,2,768]{2,1,0:T(2,128)S(1)}, u32[]{:S(2)}, u32[]{:S(2)}) %all-to-all-start.1) | async-done | bytes 196640 | tf_op jit(solution)/shard_map/all_to_all | solution.py:228
  59.6 0.0 collective-permute-done.3
  59.6 1.1 pad_maximum_fusion.1
  60.7 1.9 %collective-permute-start.7 = (bf16[4,3,48,768]{3,2,1,0:T(8,128)(2,1)}, bf16[4,3,48,768]{3,2,1,0:T(8,128)(2,1)}, u32[]{:S(2)}, u32[]{:S(2)}) collective-permute-start(bf16[4,3,48,768]{3,2,1,0:T(8,128)(2,1)} %pad_maximum_fusion.1), channel_id=1, source_target_pairs={{4,0},{13,1},{6,2},{15,3},{8,4},{1,5},{10,6},{3,7},{12,8},{5,9},{1... | collective-permute-start | bytes 2654216 | tf_op jit(solution)/shard_map/ppermute | solution.py:236
  62.6 1.9 %collective-permute-start.5 = (bf16[256,768]{1,0:T(8,128)(2,1)S(1)}, bf16[256,768]{1,0:T(8,128)(2,1)S(1)}, u32[]{:S(2)}, u32[]{:S(2)}) collective-permute-start(bf16[256,768]{1,0:T(8,128)(2,1)S(1)} %collective-permute-done.2.outer), channel_id=1, source_target_pairs={{0,1},{1,0},{2,3},{3,2},{4,5},{5,4},{6,7},{7,6},{8,9},{9,8},{10,11... | collective-permute-start | bytes 1179656 | tf_op jit(solution)/shard_map/ppermute | solution.py:280
  64.6 0.1 pad_add_fusion.place
  64.7 1.5 collective-permute-done.5.far
  66.3 0.0 collective-permute-done.4.mate
  66.3 2.7 %terms.1 = (bf16[384,2304]{1,0:T(8,128)(2,1)S(1)}, f32[4,768]{1,0:T(4,128)S(1)}) custom-call(s32[2]{0:T(128)S(1)} %pad_add_fusion.place, f32[32,2,768]{2,1,0:T(2,128)S(1)} %all-to-all-done.1.parts, f32[1,768]{1,0:T(1,128)S(1)} %broadcast_in_dim.18.gain, f32[1,768]{1,0:T(1,128)S(1)} %broadcast_in_dim.19.shift, s32[1,384]{1,0:T(1,128)S(1)} %fusion.1.source, ...), custom_call_target="tpu_custom_call" | custom-call | flops 1207959552 | bytes 6291456 | tf_op jit(solution)/shard_map/terms/pallas_call | solution.py:286
  69.0 1.2 copy-done.2
  70.3 3.7 %all-to-all-start.2 = ((bf16[4,96,2304]{2,1,0:T(8,128)(2,1)}), bf16[4,96,2304]{2,1,0:T(8,128)(2,1)S(1)}, u32[]{:S(2)}, u32[]{:S(2)}) async-start(bf16[4,96,2304]{2,1,0:T(8,128)(2,1)} %bitcast.40), calls=%async_computation.2 | async-start | bytes 3538944 | tf_op jit(solution)/shard_map/all_to_all | solution.py:228
  74.0 12.3 %collective-permute-done.7 = bf16[4,3,48,768]{3,2,1,0:T(8,128)(2,1)} collective-permute-done((bf16[4,3,48,768]{3,2,1,0:T(8,128)(2,1)}, bf16[4,3,48,768]{3,2,1,0:T(8,128)(2,1)}, u32[]{:S(2)}, u32[]{:S(2)}) %collective-permute-start.7) | collective-permute-done | bytes 884768 | tf_op jit(solution)/shard_map/ppermute | solution.py:236
  86.2 1.1 fusion
  87.3 1.9 %collective-permute-start.8 = (bf16[3,48,768]{2,1,0:T(8,128)(2,1)S(1)}, bf16[3,48,768]{2,1,0:T(8,128)(2,1)S(1)}, u32[]{:S(2)}, u32[]{:S(2)}) collective-permute-start(bf16[3,48,768]{2,1,0:T(8,128)(2,1)S(1)} %fusion), channel_id=1, source_target_pairs={{2,0},{15,1},{4,2},{1,3},{6,4},{3,5},{8,6},{5,7},{10,8},{7,9},{12,... | collective-permute-start | bytes 663560 | tf_op jit(solution)/shard_map/ppermute | solution.py:236
  89.2 5.9 %collective-permute-done.8 = bf16[3,48,768]{2,1,0:T(8,128)(2,1)S(1)} collective-permute-done((bf16[3,48,768]{2,1,0:T(8,128)(2,1)S(1)}, bf16[3,48,768]{2,1,0:T(8,128)(2,1)S(1)}, u32[]{:S(2)}, u32[]{:S(2)}) %collective-permute-start.8) | collective-permute-done | bytes 221216 | tf_op jit(solution)/shard_map/ppermute | solution.py:236
  95.1 2.5 %pad_maximum_fusion.mine = bf16[7,3,48,768]{3,2,1,0:T(8,128)(2,1)} fusion(bf16[1,3,48,768]{3,2,1,0:T(8,128)(2,1)S(1)} %bitcast.46, bf16[4,3,48,768]{3,2,1,0:T(8,128)(2,1)} %collective-permute-done.7, bf16[2,3,48,768]{3,2,1,0:T(8,128)(2,1)S(1)} %copy-done.10), kind=kLoop, calls=%fused_computation | loop fusion | flops 1548288 | bytes 3096576 | tf_op jit(solution)/shard_map/concatenate | solution.py:293
  97.7 1.9 %collective-permute-start.9 = (bf16[7,3,48,768]{3,2,1,0:T(8,128)(2,1)}, bf16[7,3,48,768]{3,2,1,0:T(8,128)(2,1)}, u32[]{:S(2)}, u32[]{:S(2)}) collective-permute-start(bf16[7,3,48,768]{3,2,1,0:T(8,128)(2,1)} %pad_maximum_fusion.mine), channel_id=1, source_target_pairs={{0,1},{1,0},{2,3},{3,2},{4,5},{5,4},{6,7},{7,6},{8,9},{9,8},{10,11... | collective-permute-start | bytes 4644872 | tf_op jit(solution)/shard_map/ppermute | solution.py:294
  99.6 0.0 all-to-all-done.2.got
  99.6 1.0 first.1
  100.6 7.1 %all-to-all-start.3 = ((bf16[8,224,128]{2,1,0:T(8,128)(2,1)}), bf16[8,224,128]{2,1,0:T(8,128)(2,1)S(1)}, u32[]{:S(2)}, u32[]{:S(2)}) async-start(bf16[8,224,128]{2,1,0:T(8,128)(2,1)} %first.1), calls=%async_computation.3 | async-start | bytes 917504 | tf_op jit(solution)/shard_map/all_to_all | solution.py:228
  107.7 0.1 stack.95
  107.8 0.1 broadcast_add_fusion
  107.9 0.1 add.236.channel
  108.0 1.1 copy-done.5
  109.1 1.0 copy-done.8
  110.1 4.8 %back.1 = (f32[256,768]{1,0:T(8,128)S(1)}, f32[2,768]{1,0:T(2,128)S(1)}) custom-call(s32[2]{0:T(128)S(1)} %pad_add_fusion.place, f32[4,768]{1,0:T(4,128)S(1)} %get-tuple-element.32.vectors, bf16[256,768]{1,0:T(8,128)(2,1)S(1)} %bitcast.36, bf16[512,768]{1,0:T(8,128)(2,1)S(1)} %copy-done.5, bf16[256,768]{1,0:T(8,128)(2,1)S(1)} %bitcast.44, ...), custom_call_target="tpu_custom_call" | custom-call | flops 1509949440 | bytes 8388608 | tf_op jit(solution)/shard_map/back/pallas_call | solution.py:295
  114.9 2.5 %psum.7.totals = f32[2,768]{1,0:T(2,128)S(1)} all-reduce(f32[2,768]{1,0:T(2,128)S(1)} %get-tuple-element.37), channel_id=1, replica_groups=mesh['x'=4,'yl'=4,'yh'=2,'z'=8,'c'=2] {'c'}, use_global_device_ids=true, to_apply=%region_0.1 | all-reduce | flops 1536 | bytes 12288 | tf_op jit(solution)/shard_map/psum | solution.py:299
  117.4 3.3 %collective-permute-start.10 = (f32[2,768]{1,0:T(2,128)S(1)}, f32[2,768]{1,0:T(2,128)S(1)}, u32[]{:S(2)}, u32[]{:S(2)}) collective-permute-start(f32[2,768]{1,0:T(2,128)S(1)} %psum.7.totals), channel_id=1, source_target_pairs={{0,112},{16,96},{32,80},{48,64},{64,48},{80,32},{96,16},{112,0},{1... | collective-permute-start | bytes 18440 | tf_op jit(solution)/shard_map/ppermute | solution.py:300
  120.7 0.1 all-to-all-done.3.got
  120.8 5.1 %collective-permute-done.10.totals_y = f32[2,768]{1,0:T(2,128)S(1)} collective-permute-done((f32[2,768]{1,0:T(2,128)S(1)}, f32[2,768]{1,0:T(2,128)S(1)}, u32[]{:S(2)}, u32[]{:S(2)}) %collective-permute-start.10) | collective-permute-done | bytes 6176 | tf_op jit(solution)/shard_map/ppermute | solution.py:300
  125.9 0.8 second.1
  126.7 3.4 %all-to-all-start.4 = ((bf16[8,64,128]{2,1,0:T(8,128)(2,1)}), bf16[8,64,128]{2,1,0:T(8,128)(2,1)S(1)}, u32[]{:S(2)}, u32[]{:S(2)}) async-start(bf16[8,64,128]{2,1,0:T(8,128)(2,1)} %second.1), calls=%async_computation.4 | async-start | bytes 262144 | tf_op jit(solution)/shard_map/all_to_all | solution.py:228
  130.1 5.3 %collective-permute-start.6 = (bf16[256,768]{1,0:T(8,128)(2,1)S(1)}, bf16[256,768]{1,0:T(8,128)(2,1)S(1)}, u32[]{:S(2)}, u32[]{:S(2)}) collective-permute-start(bf16[256,768]{1,0:T(8,128)(2,1)S(1)} %bitcast.37), channel_id=1, source_target_pairs={{1,2},{2,1},{3,4},{4,3},{5,6},{6,5},{7,8},{8,7},{9,10},{10,9},{11,... | collective-permute-start | bytes 1179656 | tf_op jit(solution)/shard_map/ppermute | solution.py:305
  135.4 3.9 %all-to-all-done.4.got = bf16[8,64,128]{2,1,0:T(8,128)(2,1)S(1)} async-done(((bf16[8,64,128]{2,1,0:T(8,128)(2,1)}), bf16[8,64,128]{2,1,0:T(8,128)(2,1)S(1)}, u32[]{:S(2)}, u32[]{:S(2)}) %all-to-all-start.4) | async-done | bytes 131104 | tf_op jit(solution)/shard_map/all_to_all | solution.py:228
  139.2 0.8 third.1
  140.0 5.4 %all-to-all-start.5 = ((bf16[16,64,128]{2,1,0:T(8,128)(2,1)}), bf16[16,64,128]{2,1,0:T(8,128)(2,1)S(1)}, u32[]{:S(2)}, u32[]{:S(2)}) async-start(bf16[16,64,128]{2,1,0:T(8,128)(2,1)} %third.1), calls=%async_computation.5 | async-start | bytes 524288 | tf_op jit(solution)/shard_map/all_to_all | solution.py:228
  145.5 7.5 %collective-permute-done.6.outer = bf16[256,768]{1,0:T(8,128)(2,1)S(1)} collective-permute-done((bf16[256,768]{1,0:T(8,128)(2,1)S(1)}, bf16[256,768]{1,0:T(8,128)(2,1)S(1)}, u32[]{:S(2)}, u32[]{:S(2)}) %collective-permute-start.6) | collective-permute-done | bytes 393248 | tf_op jit(solution)/shard_map/ppermute | solution.py:305
  152.9 1.1 copy-done.6
  154.1 5.3 %forward.1 = bf16[256,768]{1,0:T(8,128)(2,1)} custom-call(s32[2]{0:T(128)S(1)} %pad_add_fusion.place, f32[4,768]{1,0:T(4,128)S(1)} %get-tuple-element.32.vectors, bf16[256,768]{1,0:T(8,128)(2,1)S(1)} %bitcast.38, bf16[512,768]{1,0:T(8,128)(2,1)S(1)} %copy-done.6, bf16[256,768]{1,0:T(8,128)(2,1)S(1)} %collective-permute-done.6.outer, ...), custom_call_target="tpu_custom_call" | custom-call | flops 1811939328 | bytes 6291456 | tf_op jit(solution)/shard_map/forward/pallas_call | solution.py:314
  159.4 0.1 reshape.307
  159.5 0.7 copy.11
  160.2 1.2 last.1
  161.5 0.6 slice_reduce_fusion
  (27 shorter events, 0.2 us)
Async XLA Ops:
  0.6 1.0 copy-start
  2.5 3.4 %collective-permute-start = (bf16[3,24,768]{2,1,0:T(8,128)(2,1)}, bf16[3,24,768]{2,1,0:T(8,128)(2,1)S(1)}, u32[]{:S(2)}, u32[]{:S(2)}) collective-permute-start(bf16[3,24,768]{2,1,0:T(8,128)(2,1)} %bitcast.47), channel_id=1, source_target_pairs={{0,1},{1,0},{2,3},{3,2},{4,5},{5,4},{6,7},{7,6},{8,9},{9,8},{10,11... | collective-permute-start | bytes 331784 | tf_op jit(solution)/shard_map/ppermute | solution.py:268
  6.8 45.4 %copy-start.1 = (bf16[1,256,768]{2,1,0:T(8,128)(2,1)S(1)}, bf16[1,256,768]{2,1,0:T(8,128)(2,1)}, u32[]{:S(2)}) copy-start(bf16[1,256,768]{2,1,0:T(8,128)(2,1)} %param.5) | copy-start | bytes 1179652
  6.8 45.4 %copy-start.3 = (bf16[1,256,768]{2,1,0:T(8,128)(2,1)S(1)}, bf16[1,256,768]{2,1,0:T(8,128)(2,1)}, u32[]{:S(2)}) copy-start(bf16[1,256,768]{2,1,0:T(8,128)(2,1)} %param.9) | copy-start | bytes 1179652
  6.9 21.3 %collective-permute-start.1 = (bf16[2,3,24,768]{3,2,1,0:T(8,128)(2,1)S(1)}, bf16[2,3,24,768]{3,2,1,0:T(8,128)(2,1)S(1)}, u32[]{:S(2)}, u32[]{:S(2)}) collective-permute-start(bf16[2,3,24,768]{3,2,1,0:T(8,128)(2,1)S(1)} %pad_maximum_fusion.4), channel_id=1, source_target_pairs={{0,112},{16,96},{32,80},{48,64},{64,48},{80,32},{96,16},{112,0},{1... | collective-permute-start | bytes 663560 | tf_op jit(solution)/shard_map/ppermute | solution.py:272
  9.8 28.4 %collective-permute-start.2 = (bf16[256,768]{1,0:T(8,128)(2,1)}, bf16[256,768]{1,0:T(8,128)(2,1)S(1)}, u32[]{:S(2)}, u32[]{:S(2)}) collective-permute-start(bf16[256,768]{1,0:T(8,128)(2,1)} %bitcast.41), channel_id=1, source_target_pairs={{1,2},{2,1},{3,4},{4,3},{5,6},{6,5},{7,8},{8,7},{9,10},{10,9},{11,... | collective-permute-start | bytes 1179656 | tf_op jit(solution)/shard_map/ppermute | solution.py:269
  24.6 12.4 %all-to-all-start = ((f32[16,2,768]{2,1,0:T(2,128)}), f32[16,2,768]{2,1,0:T(2,128)S(1)}, u32[]{:S(2)}, u32[]{:S(2)}) async-start(f32[16,2,768]{2,1,0:T(2,128)} %stats.1), calls=%async_computation | async-start | bytes 196608 | tf_op jit(solution)/shard_map/all_to_all | solution.py:228
  38.2 28.1 %copy-start.7 = (bf16[256,768]{1,0:T(8,128)(2,1)}, bf16[256,768]{1,0:T(8,128)(2,1)S(1)}, u32[]{:S(2)}) copy-start(bf16[256,768]{1,0:T(8,128)(2,1)S(1)} %collective-permute-done.2.outer) | copy-start | bytes 1179652
  38.2 21.4 %collective-permute-start.3 = (bf16[2,3,48,768]{3,2,1,0:T(8,128)(2,1)S(1)}, bf16[2,3,48,768]{3,2,1,0:T(8,128)(2,1)S(1)}, u32[]{:S(2)}, u32[]{:S(2)}) collective-permute-start(bf16[2,3,48,768]{3,2,1,0:T(8,128)(2,1)S(1)} %pad_maximum_fusion.3.own), channel_id=1, source_target_pairs={{2,0},{15,1},{4,2},{1,3},{6,4},{3,5},{8,6},{5,7},{10,8},{7,9},{12,... | collective-permute-start | bytes 1327112 | tf_op jit(solution)/shard_map/ppermute | solution.py:236
  40.9 18.7 %all-to-all-start.1 = ((f32[32,2,768]{2,1,0:T(2,128)}), f32[32,2,768]{2,1,0:T(2,128)S(1)}, u32[]{:S(2)}, u32[]{:S(2)}) async-start(f32[32,2,768]{2,1,0:T(2,128)} %merge.1), calls=%async_computation.1 | async-start | bytes 393216 | tf_op jit(solution)/shard_map/all_to_all | solution.py:228
  52.2 12.4 %copy-start.11 = (f32[768]{0:T(1024)S(1)}, f32[768]{0:T(1024)}, u32[]{:S(2)}) copy-start(f32[768]{0:T(1024)} %param.6) | copy-start | bytes 9220
  52.2 12.4 %copy-start.12 = (f32[768]{0:T(1024)S(1)}, f32[768]{0:T(1024)}, u32[]{:S(2)}) copy-start(f32[768]{0:T(1024)} %param.7) | copy-start | bytes 9220
  53.2 13.0 %collective-permute-start.4 = (bf16[512,768]{1,0:T(8,128)(2,1)}, bf16[512,768]{1,0:T(8,128)(2,1)S(1)}, u32[]{:S(2)}, u32[]{:S(2)}) collective-permute-start(bf16[512,768]{1,0:T(8,128)(2,1)} %pad_maximum_fusion.2), channel_id=1, source_target_pairs={{0,1},{1,0},{2,3},{3,2},{4,5},{5,4},{6,7},{7,6},{8,9},{9,8},{10,11... | collective-permute-start | bytes 2359304 | tf_op jit(solution)/shard_map/ppermute | solution.py:279
  59.6 1.1 copy-start.9
  60.7 25.5 %collective-permute-start.7 = (bf16[4,3,48,768]{3,2,1,0:T(8,128)(2,1)}, bf16[4,3,48,768]{3,2,1,0:T(8,128)(2,1)}, u32[]{:S(2)}, u32[]{:S(2)}) collective-permute-start(bf16[4,3,48,768]{3,2,1,0:T(8,128)(2,1)} %pad_maximum_fusion.1), channel_id=1, source_target_pairs={{4,0},{13,1},{6,2},{15,3},{8,4},{1,5},{10,6},{3,7},{12,8},{5,9},{1... | collective-permute-start | bytes 2654216 | tf_op jit(solution)/shard_map/ppermute | solution.py:236
  62.6 3.6 %collective-permute-start.5 = (bf16[256,768]{1,0:T(8,128)(2,1)S(1)}, bf16[256,768]{1,0:T(8,128)(2,1)S(1)}, u32[]{:S(2)}, u32[]{:S(2)}) collective-permute-start(bf16[256,768]{1,0:T(8,128)(2,1)S(1)} %collective-permute-done.2.outer), channel_id=1, source_target_pairs={{0,1},{1,0},{2,3},{3,2},{4,5},{5,4},{6,7},{7,6},{8,9},{9,8},{10,11... | collective-permute-start | bytes 1179656 | tf_op jit(solution)/shard_map/ppermute | solution.py:280
  66.3 2.8 %copy-start.4 = (bf16[512,768]{1,0:T(8,128)(2,1)}, bf16[512,768]{1,0:T(8,128)(2,1)S(1)}, u32[]{:S(2)}) copy-start(bf16[512,768]{1,0:T(8,128)(2,1)S(1)} %collective-permute-done.4.mate) | copy-start | bytes 2359300
  69.0 1.2 copy-start.2
  70.2 24.9 %copy-start.10 = (bf16[2,3,48,768]{3,2,1,0:T(8,128)(2,1)S(1)}, bf16[2,3,48,768]{3,2,1,0:T(8,128)(2,1)}, u32[]{:S(2)}) copy-start(bf16[2,3,48,768]{3,2,1,0:T(8,128)(2,1)} %copy-done.9) | copy-start | bytes 1327108
  70.3 29.3 %all-to-all-start.2 = ((bf16[4,96,2304]{2,1,0:T(8,128)(2,1)}), bf16[4,96,2304]{2,1,0:T(8,128)(2,1)S(1)}, u32[]{:S(2)}, u32[]{:S(2)}) async-start(bf16[4,96,2304]{2,1,0:T(8,128)(2,1)} %bitcast.40), calls=%async_computation.2 | async-start | bytes 3538944 | tf_op jit(solution)/shard_map/all_to_all | solution.py:228
  87.3 7.8 %collective-permute-start.8 = (bf16[3,48,768]{2,1,0:T(8,128)(2,1)S(1)}, bf16[3,48,768]{2,1,0:T(8,128)(2,1)S(1)}, u32[]{:S(2)}, u32[]{:S(2)}) collective-permute-start(bf16[3,48,768]{2,1,0:T(8,128)(2,1)S(1)} %fusion), channel_id=1, source_target_pairs={{2,0},{15,1},{4,2},{1,3},{6,4},{3,5},{8,6},{5,7},{10,8},{7,9},{12,... | collective-permute-start | bytes 663560 | tf_op jit(solution)/shard_map/ppermute | solution.py:236
  97.7 10.3 %collective-permute-start.9 = (bf16[7,3,48,768]{3,2,1,0:T(8,128)(2,1)}, bf16[7,3,48,768]{3,2,1,0:T(8,128)(2,1)}, u32[]{:S(2)}, u32[]{:S(2)}) collective-permute-start(bf16[7,3,48,768]{3,2,1,0:T(8,128)(2,1)} %pad_maximum_fusion.mine), channel_id=1, source_target_pairs={{0,1},{1,0},{2,3},{3,2},{4,5},{5,4},{6,7},{7,6},{8,9},{9,8},{10,11... | collective-permute-start | bytes 4644872 | tf_op jit(solution)/shard_map/ppermute | solution.py:294
  100.6 20.3 %all-to-all-start.3 = ((bf16[8,224,128]{2,1,0:T(8,128)(2,1)}), bf16[8,224,128]{2,1,0:T(8,128)(2,1)S(1)}, u32[]{:S(2)}, u32[]{:S(2)}) async-start(bf16[8,224,128]{2,1,0:T(8,128)(2,1)} %first.1), calls=%async_computation.3 | async-start | bytes 917504 | tf_op jit(solution)/shard_map/all_to_all | solution.py:228
  108.0 1.1 copy-start.5
  109.1 1.0 copy-start.8
  117.4 8.5 %collective-permute-start.10 = (f32[2,768]{1,0:T(2,128)S(1)}, f32[2,768]{1,0:T(2,128)S(1)}, u32[]{:S(2)}, u32[]{:S(2)}) collective-permute-start(f32[2,768]{1,0:T(2,128)S(1)} %psum.7.totals), channel_id=1, source_target_pairs={{0,112},{16,96},{32,80},{48,64},{64,48},{80,32},{96,16},{112,0},{1... | collective-permute-start | bytes 18440 | tf_op jit(solution)/shard_map/ppermute | solution.py:300
  126.7 12.5 %all-to-all-start.4 = ((bf16[8,64,128]{2,1,0:T(8,128)(2,1)}), bf16[8,64,128]{2,1,0:T(8,128)(2,1)S(1)}, u32[]{:S(2)}, u32[]{:S(2)}) async-start(bf16[8,64,128]{2,1,0:T(8,128)(2,1)} %second.1), calls=%async_computation.4 | async-start | bytes 262144 | tf_op jit(solution)/shard_map/all_to_all | solution.py:228
  130.1 22.8 %collective-permute-start.6 = (bf16[256,768]{1,0:T(8,128)(2,1)S(1)}, bf16[256,768]{1,0:T(8,128)(2,1)S(1)}, u32[]{:S(2)}, u32[]{:S(2)}) collective-permute-start(bf16[256,768]{1,0:T(8,128)(2,1)S(1)} %bitcast.37), channel_id=1, source_target_pairs={{1,2},{2,1},{3,4},{4,3},{5,6},{6,5},{7,8},{8,7},{9,10},{10,9},{11,... | collective-permute-start | bytes 1179656 | tf_op jit(solution)/shard_map/ppermute | solution.py:305
  140.0 19.3 %all-to-all-start.5 = ((bf16[16,64,128]{2,1,0:T(8,128)(2,1)}), bf16[16,64,128]{2,1,0:T(8,128)(2,1)S(1)}, u32[]{:S(2)}, u32[]{:S(2)}) async-start(bf16[16,64,128]{2,1,0:T(8,128)(2,1)} %third.1), calls=%async_computation.5 | async-start | bytes 524288 | tf_op jit(solution)/shard_map/all_to_all | solution.py:228
  152.9 1.1 copy-start.6

commit v4 on v3

v4 whole, which is shorter than its diff:
```python
import jax
import jax.numpy as jnp
from jax import lax
from jax.experimental import pallas as pl
from jax.experimental.pallas import tpu as pltpu
from jax.sharding import Mesh, PartitionSpec as P

F32 = jnp.float32
BF16 = jnp.bfloat16
AXES = ("x", "ya", "yb", "yh", "z", "c")
DP = ("x", "ya", "yb")
Y = ("ya", "yb", "yh")
NX, NYA, NYB, NYH, NZ, NC = 4, 2, 2, 2, 8, 2
NYL = NYA * NYB
SEQ = ("yh", "z", "c")
SEQ_N = NYH * NZ * NC
C = 768
HALF = C // 2
L = 256
ROWS = 24
OWNERS = NYH * NZ
SUB = ROWS // (NX * NYB)
PIECE = 27
TOT = 24
MSG = 64
COUNT = L * SEQ_N * NX * NYL
NORM = float(COUNT) ** -0.5
SQRT_HALF = 0.7071067811865476
INV_SQRT_2PI = 0.3989422804014327
NT = (((1,), (1,)), ((), ()))
TN = (((0,), (0,)), ((), ()))
SPACES = {
    "s": pl.BlockSpec(memory_space=pltpu.SMEM),
    "v": pl.BlockSpec(memory_space=pltpu.VMEM),
    "a": pl.BlockSpec(memory_space=pl.ANY),
}


def call(kernel, out_shape, name, megabytes, spaces=None, out_specs=None, flops=0, size=1 << 20, scratch=()):
    params = pltpu.CompilerParams(vmem_limit_bytes=megabytes * 1024 * 1024)
    estimate = pl.CostEstimate(flops=flops, bytes_accessed=size, transcendentals=0)
    extra = {}
    if spaces is not None:
        extra["in_specs"] = [SPACES[letter] for letter in spaces]
    if out_specs is not None:
        extra["out_specs"] = out_specs
    return pl.pallas_call(
        kernel, out_shape=out_shape, compiler_params=params, cost_estimate=estimate, name=name,
        scratch_shapes=list(scratch), **extra,
    )


def fetch(sources, targets, sems):
    copies = [
        pltpu.make_async_copy(source, target, sems.at[i])
        for i, (source, target) in enumerate(zip(sources, targets))
    ]
    for copy in copies:
        copy.start()
    return copies


def spread(value, n):
    return jnp.broadcast_to(value[None], (n,) + value.shape)


def stats_kernel(inputs, message, block, sems):
    fetch([inputs], [block], sems)[0].wait()
    values = block[...].astype(F32)
    total = jnp.sum(values, axis=0, keepdims=True)
    off = values - total / L
    squares = jnp.sum(off * off, axis=0, keepdims=True)
    message[...] = spread(jnp.concatenate([total, squares], axis=0), NZ * NC)


def merged(parts, count):
    sums, squares = parts[:, 0, :], parts[:, 1, :]
    n = sums.shape[0]
    total = jnp.sum(sums, axis=0, keepdims=True)
    off = sums / count - total / (count * n)
    return total, jnp.sum(squares, axis=0, keepdims=True) + count * jnp.sum(off * off, axis=0, keepdims=True)


def merge_kernel(parts, message):
    total, squares = merged(parts[...], L)
    message[...] = spread(jnp.concatenate([total, squares], axis=0), NX * NYL * NYH)


def one_hot(channels):
    rows = lax.broadcasted_iota(jnp.int32, (C, channels.shape[1]), 0)
    return jnp.where(rows == channels[...], 1.0, 0.0).astype(BF16)


def normalised(block, vectors):
    return (block - vectors[0:1]) * vectors[1:2]


def half_gate(v):
    return 0.5 * (1.0 + lax.erf(v * SQRT_HALF))


def terms_kernel(place, parts, gain, shift, source, inputs, mate, cot, outer, terms, vectors):
    total, squares = merged(parts[...], L * NZ * NC)
    mean = total / COUNT
    inv_std = lax.rsqrt(squares / COUNT + 1e-05)
    rows = jnp.concatenate([mean, inv_std, gain[...], shift[...]], axis=0)
    vectors[...] = rows
    pick = one_hot(source)
    chosen, rest = jnp.zeros((4, HALF), F32), rows
    for _ in range(3):
        part = rest.astype(BF16)
        chosen += jnp.dot(part, pick, preferred_element_type=F32)
        rest = rest - part.astype(F32)
    low = place[0] == 0
    both = jnp.concatenate([inputs[...], mate[L : 2 * L]], axis=0)
    v = normalised(jnp.dot(both, pick, preferred_element_type=F32), chosen)
    v = chosen[2:3] * v + chosen[3:4]
    act = (v * half_gate(v)).astype(BF16)
    own, next_own, last_own = cot[...], mate[:L], outer[:L]
    beyond = mate[2 * L :]
    cots = (
        (jnp.where(low, next_own, last_own), jnp.where(low, beyond, own)),
        (own, next_own),
        (jnp.where(low, last_own, next_own), jnp.where(low, own, beyond)),
    )
    for tap, pair in enumerate(cots):
        block = lax.dot_general(act, jnp.concatenate(pair, axis=0), TN, preferred_element_type=F32)
        terms[:, tap * C : (tap + 1) * C] = (block * NORM).astype(BF16)


def by_tap(kern, tap):
    return kern[:, tap].reshape(C, C)


def back_kernel(
    place, vectors, inputs_h, mate_h, cot_h, outer_h, kc, ko, channel, pre_grad, totals,
    inputs, mate, cot, outer, kern, sems,
):
    sources = [inputs_h, mate_h.at[:L], cot_h, outer_h.at[:L], kc, ko]
    copies = fetch(sources, [inputs, mate, cot, outer, kern.at[:NZ], kern.at[NZ:]], sems)
    low = place[0] == 0
    pick = one_hot(channel)
    copies[0].wait()
    rows = vectors[...]
    normed = normalised(inputs[...].astype(F32), rows)
    v = rows[2:3] * normed + rows[3:4]
    slope = half_gate(v) + v * (INV_SQRT_2PI * jnp.exp(-0.5 * v * v))
    for copy in copies[1:]:
        copy.wait()
    taps = (
        jnp.where(low, mate[...], outer[...]),
        cot[...],
        jnp.where(low, outer[...], mate[...]),
    )
    total = jnp.zeros((L, C), F32)
    for tap, q in enumerate(taps):
        total += lax.dot_general(q, by_tap(kern, tap), NT, preferred_element_type=F32)
    high = total.astype(BF16)
    rest = (total - high.astype(F32)).astype(BF16)
    total = lax.dot_general(high, pick, NT, preferred_element_type=F32)
    total += lax.dot_general(rest, pick, NT, preferred_element_type=F32)
    grad = total * slope
    pre_grad[...] = grad
    totals[...] = jnp.concatenate(
        [jnp.sum(grad, axis=0, keepdims=True), jnp.sum(grad * normed, axis=0, keepdims=True)], axis=0
    )


def put_totals(totals, held):
    high = totals.astype(BF16).astype(F32)
    rows = jnp.concatenate([high, totals - high], axis=0)
    for tile in range(6):
        held[4 * tile : 4 * tile + 4] = rows[:, 128 * tile : 128 * tile + 128]
    return held[:TOT].astype(BF16)


def get_totals(held):
    rows = jnp.concatenate([held[4 * tile : 4 * tile + 4] for tile in range(6)], axis=1)
    return rows[0:2] + rows[2:4]


def first_kernel(got, message):
    parts = got[...].astype(F32)
    total = jnp.sum(parts, axis=0)
    zero = jnp.zeros((8, 128), F32)
    for l in range(NYA):
        for h in range(NYH):
            tiles = []
            for piece in range(PIECE):
                sub, tile = divmod(l * PIECE + piece, 18)
                row = sub * OWNERS + h * NZ
                tiles.append(total[row : row + 8, 128 * tile : 128 * tile + 128])
            tiles.append(zero)
            message[l * NYH + h] = jnp.concatenate(tiles, axis=0).astype(BF16)


def second_kernel(got, totals, totals_y, message, held, line):
    total = jnp.sum(got[...].astype(F32), axis=0)
    packed = put_totals(totals[...] + totals_y[...], held).astype(F32)
    for piece in range(PIECE):
        line[:, TOT + piece, :] = total[piece * 8 : piece * 8 + 8]
    for z in range(NZ):
        line[z, :TOT] = packed
        line[z, TOT + PIECE :] = jnp.zeros((MSG - TOT - PIECE, 128), F32)
    message[...] = line[...].astype(BF16)


def third_kernel(got, message, held):
    total = jnp.sum(got[...].astype(F32), axis=0)
    held[...] = total[:32]
    packed = put_totals(get_totals(held), held)
    message[...] = spread(jnp.concatenate([packed, total[TOT:].astype(BF16)], axis=0), NX * NYL)


def last_kernel(
    got, vectors, inputs_h, cot_h, pre_h, grad_in, weights, gain_grad, shift_grad,
    inputs, cot, pre_grad, held, line, sems,
):
    copies = fetch([inputs_h, cot_h, pre_h], [inputs, cot, pre_grad], sems)
    total = jnp.zeros((32, 128), F32)
    for member in range(NX * NYL):
        part = got[member].astype(F32)
        total += part[:32]
        line[...] = part
        x, l = divmod(member, NYL)
        a, b = divmod(l, NYB)
        for piece in range(PIECE):
            sub, tile = divmod(a * PIECE + piece, 18)
            row = (x * NYB + b) * SUB + sub
            tap, lane = divmod(tile, 6)
            weights[tap, row : row + 1, 128 * lane : 128 * lane + 128] = line[TOT + piece : TOT + piece + 1]
    held[...] = total
    totals = get_totals(held)
    shift_grad[...] = (totals[0:1] * NORM).reshape(C)
    gain_grad[...] = (totals[1:2] * NORM).reshape(C)
    for copy in copies:
        copy.wait()
    rows = vectors[...]
    normed = normalised(inputs[...].astype(F32), rows)
    bn_grad = (rows[2:3] * rows[1:2]) * (
        pre_grad[...] - totals[0:1] / COUNT - normed * (totals[1:2] / COUNT)
    )
    grad_in[...] = (cot[...].astype(F32) + bn_grad).astype(BF16)


def acts_kernel(place, vectors, inputs, mate_h, outer_h, channel, acts, mate, outer, sems):
    copies = fetch([outer_h.at[L:], mate_h.at[L : 2 * L]], [outer, mate], sems)
    rows = vectors[...]

    def activate(block):
        v = rows[2:3] * normalised(block.astype(F32), rows) + rows[3:4]
        return v * half_gate(v)

    low = place[0] == 0
    pick = one_hot(channel)
    here = activate(inputs[...]).astype(BF16)
    copies[0].wait()
    away = jnp.where(place[1] == 1, activate(outer[...]), 0.0).astype(BF16)
    copies[1].wait()
    near = activate(mate[...]).astype(BF16)
    for tap, a in enumerate((jnp.where(low, away, near), here, jnp.where(low, near, away))):
        acts[tap] = jnp.dot(a, pick, preferred_element_type=F32).astype(BF16)


def forward_kernel(acts, inputs, kc, ko, output, kern, sems):
    copies = fetch([kc, ko], [kern.at[:NZ], kern.at[NZ:]], sems)
    total = inputs[...].astype(F32)
    for copy in copies:
        copy.wait()
    for tap in range(3):
        total += jnp.dot(acts[tap], by_tap(kern, tap), preferred_element_type=F32)
    output[...] = total.astype(BF16)


def shape(*dims, kind=F32):
    return jax.ShapeDtypeStruct(dims, kind)


def exchange(value, axes):
    return lax.all_to_all(value, axes, 0, 0, tiled=True)


def body(inputs, gain, shift, kernel, cotangent):
    yh, zi, ci = lax.axis_index("yh"), lax.axis_index("z"), lax.axis_index("c")
    inputs, cotangent = inputs[0], cotangent[0]
    gain, shift = gain[None], shift[None]
    seq = (yh * NZ + zi) * NC + ci
    has_outer = jnp.logical_and(seq > 0, seq < SEQ_N - 1).astype(jnp.int32)
    place = jnp.stack([ci, has_outer])
    order = jnp.arange(HALF)
    part, row, owner = order // (SUB * OWNERS), (order // OWNERS) % SUB, order % OWNERS
    source = ((owner * NC + ci) * ROWS + part * SUB + row)[None]
    order = jnp.arange(C)
    gp, gz = order // (NZ * NYH * ROWS), (order // (NYH * ROWS)) % NZ
    gy, gr = (order // ROWS) % NYH, order % ROWS
    channel = ((((gy + yh) % NYH * NZ + gz) * NC + (gp + ci) % NC) * ROWS + gr)[None]
    swap_c = [(0, 1), (1, 0)]
    swap_out = [(i, j) for i in range(1, SEQ_N - 1, 2) for i, j in ((i, i + 1), (i + 1, i))]
    swap_y = []
    for l in range(NYL):
        for h in range(NYH):
            y = 7 - (h * NYL + l)
            swap_y.append((l * NYH + h, (y % NYL) * NYH + y // NYL))

    own = kernel.transpose(1, 0, 2)
    other = lax.ppermute(own, Y, swap_y)
    pair = jnp.concatenate([cotangent, inputs], axis=0)
    stats = call(stats_kernel, shape(NZ * NC, 2, C), "stats", 56, "a", scratch=[
        pltpu.VMEM((L, C), BF16), pltpu.SemaphoreType.DMA((1,)),
    ])(inputs)
    stats, other, pair = lax.optimization_barrier((stats, other, pair))
    outer = lax.ppermute(pair, SEQ, swap_out)
    kernel_c = lax.all_gather(jnp.concatenate([own, other], axis=1), "z", axis=0, tiled=False)
    stats = exchange(stats, ("z", "c"))
    stats, outer, pair = lax.optimization_barrier((stats, outer, pair))
    stats = call(merge_kernel, shape(NX * NYL * NYH, 2, C), "merge", 8)(stats)
    mate = lax.ppermute(jnp.concatenate([pair, outer[:L]], axis=0), "c", swap_c)
    stats = exchange(stats, ("x",) + Y)

    terms, vectors = call(
        terms_kernel, (shape(HALF, 3 * C, kind=BF16), shape(4, C)), "terms", 24, "svvvvvvvv", flops=2 * 512 * HALF * C * 4, size=6 << 20,
    )(place, stats, gain, shift, source, inputs, mate, cotangent, outer)
    terms = exchange(terms.reshape(NX * NYB, HALF // (NX * NYB), 3 * C), ("x", "yb"))

    kernel_o = lax.ppermute(kernel_c, "c", swap_c)
    kern = pltpu.VMEM((2 * NZ, 3, NYH * ROWS, C), BF16)
    pre_grad, totals = call(
        back_kernel, (shape(L, C), shape(2, C)), "back", 56, "svaaaaaav",
        flops=2 * L * C * C * 5, size=8 << 20,
        scratch=[
            pltpu.VMEM((L, C), BF16), pltpu.VMEM((L, C), BF16), pltpu.VMEM((L, C), BF16),
            pltpu.VMEM((L, C), BF16), kern, pltpu.SemaphoreType.DMA((6,)),
        ],
    )(place, vectors, inputs, mate, cotangent, outer, kernel_c, kernel_o, channel)
    totals = lax.psum(totals, "c")

    held = pltpu.VMEM((32, 128), F32)
    terms, totals = lax.optimization_barrier((terms, totals))
    totals_y = lax.ppermute(totals, Y, swap_y)
    message = call(first_kernel, shape(NYA * NYH, 224, 128, kind=BF16), "first", 12)(terms)
    got = exchange(message, ("ya", "yh"))
    message = call(
        second_kernel, shape(NZ, MSG, 128, kind=BF16), "second", 12,
        scratch=[held, pltpu.VMEM((NZ, MSG, 128), F32)],
    )(got, totals, totals_y)
    got = exchange(message, "z")
    acts = call(
        acts_kernel, shape(3, L, C, kind=BF16), "acts", 56, "svvaav", flops=2 * L * C * C * 3, size=2 << 20,
        scratch=[pltpu.VMEM((L, C), BF16), pltpu.VMEM((L, C), BF16), pltpu.SemaphoreType.DMA((2,))],
    )(place, vectors, inputs, mate, outer, channel)
    got, acts = lax.optimization_barrier((got, acts))
    message = call(third_kernel, shape(NX * NYL, MSG, 128, kind=BF16), "third", 12, scratch=[held])(got)
    got = exchange(message, DP)
    output = call(
        forward_kernel, shape(L, C, kind=BF16), "forward", 56, "vvaa", flops=2 * L * C * C * 3, size=6 << 20,
        scratch=[kern, pltpu.SemaphoreType.DMA((2,))],
    )(acts, inputs, kernel_c, kernel_o)
    got, output = lax.optimization_barrier((got, output))
    grad_in, weights, gain_grad, shift_grad = call(
        last_kernel,
        (shape(L, C, kind=BF16), shape(3, ROWS, C), shape(C), shape(C)), "last", 12, "vvaaa",
        scratch=[
            pltpu.VMEM((L, C), BF16), pltpu.VMEM((L, C), BF16), pltpu.VMEM((L, C), F32),
            held, pltpu.VMEM((MSG, 128), F32), pltpu.SemaphoreType.DMA((3,)),
        ],
    )(got, vectors, inputs, cotangent, pre_grad)
    return (output[None], grad_in[None], weights.transpose(1, 0, 2), gain_grad, shift_grad)


def solution(mesh):
    split_mesh = Mesh(mesh.devices.reshape(NX, NYA, NYB, NYH, NZ, NC), AXES)
    rows = P(DP, SEQ, None)
    return jax.shard_map(
        body,
        mesh=split_mesh,
        in_specs=(rows, P(), P(), P(SEQ, None, None), rows),
        out_specs=(rows, rows, P(SEQ, None, None), P(), P()),
        check_vma=False,
    )
```

time: 163 us -> 155 us (0.951)
  the two profiles are of different devices: /device:TPU:48 before, /device:TPU:8 now
where the time goes in v4:
time: 155 us
  starting transfers between devices  52.2 us (34%)
  waiting for transfers between devices  29.5 us (19%)
  Pallas kernels  26.6 us (17%)
  blocking collectives  25 us (16%)
  between operations  14.4 us (9%)
  other arithmetic  3.74 us (2%)
  local copies, waits for them, and re-layouts  3.12 us (2%)
    all_to_all x5, starting transfers between devices, exchange(): return lax.all_to_all(value, axes, 0, 0, tiled=True)  35 us
    all_to_all x5, waiting for transfers between devices, exchange(): return lax.all_to_all(value, axes, 0, 0, tiled=True)  23.6 us
    all_to_all x1, blocking collectives, exchange(): return lax.all_to_all(value, axes, 0, 0, tiled=True)  22.3 us
    pallas_call x1, Pallas kernels, body(): call(back_kernel, (shape(L, C), shape(2, C)), 'back', 56, 'svaaaaaav', fl...  7.02 us
    ppermute x1, starting transfers between devices, body(): totals_y = lax.ppermute(totals, Y, swap_y)  6.69 us
    ppermute x1, starting transfers between devices, body(): other = lax.ppermute(own, Y, swap_y)  6.05 us
    pallas_call x1, Pallas kernels, body(): call(forward_kernel, shape(L, C, kind=BF16), 'forward', 56, 'vvaa', flops...  5.33 us
    pallas_call x1, Pallas kernels, body(): call(acts_kernel, shape(3, L, C, kind=BF16), 'acts', 56, 'svvaav', flops=...  4.83 us
  transfers between devices with their start and end apart: 11, of which 8 were waited for; matrix products, arithmetic and copies ran while one was open for 2% of the time, Pallas kernels for 15%

profile of v4, /device:TPU:8, one launch (start us, length us, event | category | flops | bytes accessed | tf_op | source)
XLA Modules:
  0.0 154.6 jit_solution(1518774269202582925)
XLA Ops:
  7.2 0.0 copy-start.13
  7.2 0.0 all-gather.3.cloned.1.call-start
  7.2 6.0 %collective-permute-start = (bf16[3,24,768]{2,1,0:T(8,128)(2,1)}, bf16[3,24,768]{2,1,0:T(8,128)(2,1)S(1)}, u32[]{:S(2)}, u32[]{:S(2)}) collective-permute-start(bf16[3,24,768]{2,1,0:T(8,128)(2,1)} %bitcast.26), channel_id=1, source_target_pairs={{0,112},{16,96},{32,80},{48,64},{64,48},{80,32},{96,16},{112,0},{1... | collective-permute-start | bytes 331784 | tf_op jit(solution)/shard_map/ppermute | solution.py:306
  13.3 1.8 %stats.1 = f32[16,2,768]{2,1,0:T(2,128)} custom-call(bf16[256,768]{1,0:T(8,128)(2,1)} %bitcast.10), custom_call_target="tpu_custom_call" | custom-call | bytes 1048576 | tf_op jit(solution)/shard_map/stats/pallas_call | solution.py:308
  15.1 0.0 copy-start.12
  15.1 1.2 pad_maximum_fusion.1
  16.3 0.8 collective-permute-done
  17.1 0.7 collective-permute-start.1
  17.8 0.0 copy-done.13
  17.8 0.7 pad_maximum_fusion.2
  18.5 0.0 all-gather.3.cloned.1.call-update
  18.6 0.0 copy-done.12
  18.6 22.3 %all_to_all.30.parts = f32[16,2,768]{2,1,0:T(2,128)S(1)} all-to-all(f32[16,2,768]{2,1,0:T(2,128)S(1)} %copy-done.12), channel_id=1, replica_groups=mesh['x'=4,'ya'=2,'yb'=2,'yh'=2,'z'=8,'c'=2] {'z','c'}, dimensions={0} | all-to-all | bytes 196608 | tf_op jit(solution)/shard_map/all_to_all | solution.py:280
  40.9 0.0 collective-permute-done.1.outer.outer_h
  41.0 0.0 copy-start.14
  41.0 0.0 copy-start.15
  41.0 0.0 copy-start
  41.0 0.0 copy-start.4
  41.0 1.1 pad_maximum_fusion
  42.1 1.9 %collective-permute-start.2 = (bf16[768,768]{1,0:T(8,128)(2,1)}, bf16[768,768]{1,0:T(8,128)(2,1)S(1)}, u32[]{:S(2)}, u32[]{:S(2)}) collective-permute-start(bf16[768,768]{1,0:T(8,128)(2,1)} %pad_maximum_fusion), channel_id=1, source_target_pairs={{0,1},{1,0},{2,3},{3,2},{4,5},{5,4},{6,7},{7,6},{8,9},{9,8},{10,11... | collective-permute-start | bytes 3538952 | tf_op jit(solution)/shard_map/ppermute | solution.py:317
  44.0 0.8 merge.1
  44.8 14.9 %all-to-all-start.1 = ((f32[32,2,768]{2,1,0:T(2,128)}), f32[32,2,768]{2,1,0:T(2,128)S(1)}, u32[]{:S(2)}, u32[]{:S(2)}) async-start(f32[32,2,768]{2,1,0:T(2,128)} %merge.1), calls=%async_computation.1 | async-start | bytes 393216 | tf_op jit(solution)/shard_map/all_to_all | solution.py:280
  59.7 0.0 copy-done.14
  59.7 0.0 copy-done.15
  59.8 0.1 pad_add_fusion.place
  59.9 11.1 %all-to-all-done.1.parts = f32[32,2,768]{2,1,0:T(2,128)S(1)} async-done(((f32[32,2,768]{2,1,0:T(2,128)}), f32[32,2,768]{2,1,0:T(2,128)S(1)}, u32[]{:S(2)}, u32[]{:S(2)}) %all-to-all-start.1) | async-done | bytes 196640 | tf_op jit(solution)/shard_map/all_to_all | solution.py:280
  71.0 0.0 collective-permute-done.2.mate.mate_h
  71.0 0.0 copy-done.2
  71.0 0.0 copy-done
  71.0 0.0 copy-done.4
  71.0 0.0 copy-start.3
  71.0 2.7 %terms.1 = (bf16[384,2304]{1,0:T(8,128)(2,1)S(1)}, f32[4,768]{1,0:T(4,128)S(1)}) custom-call(s32[2]{0:T(128)S(1)} %pad_add_fusion.place, f32[32,2,768]{2,1,0:T(2,128)S(1)} %all-to-all-done.1.parts, f32[1,768]{1,0:T(1,128)S(1)} %broadcast_in_dim.14.gain, f32[1,768]{1,0:T(1,128)S(1)} %broadcast_in_dim.15.shift, s32[1,384]{1,0:T(1,128)S(1)} %fusion.13.source, ...), custom_call_target="tpu_custom_call" | custom-call | flops 1207959552 | bytes 6291456 | tf_op jit(solution)/shard_map/terms/pallas_call | solution.py:320
  73.7 0.0 copy-done.10
  73.7 0.0 copy-done.3
  73.7 0.0 copy-start.6
  73.7 1.2 copy-done.6
  75.0 0.6 copy-done.8
  75.6 4.9 %all-to-all-start.2 = ((bf16[8,48,2304]{2,1,0:T(8,128)(2,1)}), bf16[8,48,2304]{2,1,0:T(8,128)(2,1)S(1)}, u32[]{:S(2)}, u32[]{:S(2)}) async-start(bf16[8,48,2304]{2,1,0:T(8,128)(2,1)} %bitcast.21), calls=%async_computation.2 | async-start | bytes 3538944 | tf_op jit(solution)/shard_map/all_to_all | solution.py:280
  80.4 1.9 %collective-permute-start.3 = (bf16[8,3,48,768]{3,2,1,0:T(8,128)(2,1)}, bf16[8,3,48,768]{3,2,1,0:T(8,128)(2,1)S(1)}, u32[]{:S(2)}, u32[]{:S(2)}) collective-permute-start(bf16[8,3,48,768]{3,2,1,0:T(8,128)(2,1)} %bitcast.22), channel_id=1, source_target_pairs={{0,1},{1,0},{2,3},{3,2},{4,5},{5,4},{6,7},{7,6},{8,9},{9,8},{10,11... | collective-permute-start | bytes 5308424 | tf_op jit(solution)/shard_map/ppermute | solution.py:325
  82.4 0.6 fusion.channel
  83.0 3.2 %collective-permute-done.3.ko = bf16[8,3,48,768]{3,2,1,0:T(8,128)(2,1)S(1)} collective-permute-done((bf16[8,3,48,768]{3,2,1,0:T(8,128)(2,1)}, bf16[8,3,48,768]{3,2,1,0:T(8,128)(2,1)S(1)}, u32[]{:S(2)}, u32[]{:S(2)}) %collective-permute-start.3) | collective-permute-done | bytes 1769504 | tf_op jit(solution)/shard_map/ppermute | solution.py:325
  86.2 1.2 copy-done.11
  87.4 7.0 %back.1 = (f32[256,768]{1,0:T(8,128)}, f32[2,768]{1,0:T(2,128)}) custom-call(s32[2]{0:T(128)} %copy-done.10, f32[4,768]{1,0:T(4,128)} %copy-done.8, bf16[256,768]{1,0:T(8,128)(2,1)} %bitcast.12, bf16[768,768]{1,0:T(8,128)(2,1)} %copy-done.3, bf16[256,768]{1,0:T(8,128)(2,1)} %bitcast.18, bf16[512,768]{1,0:T(8,128)(2,1)} %copy-done.2, ...), custom_call_target="tpu_custom_call" | custom-call | flops 1509949440 | bytes 8388608 | tf_op jit(solution)/shard_map/back/pallas_call | solution.py:327
  94.4 2.6 %psum.7.totals = f32[2,768]{1,0:T(2,128)S(1)} all-reduce(f32[2,768]{1,0:T(2,128)} %get-tuple-element.33), channel_id=1, replica_groups=mesh['x'=4,'ya'=2,'yb'=2,'yh'=2,'z'=8,'c'=2] {'c'}, use_global_device_ids=true, to_apply=%region_0.1 | all-reduce | flops 1536 | bytes 12288 | tf_op jit(solution)/shard_map/psum | solution.py:335
  97.1 3.9 %all-to-all-done.2.got = bf16[8,48,2304]{2,1,0:T(8,128)(2,1)S(1)} async-done(((bf16[8,48,2304]{2,1,0:T(8,128)(2,1)}), bf16[8,48,2304]{2,1,0:T(8,128)(2,1)S(1)}, u32[]{:S(2)}, u32[]{:S(2)}) %all-to-all-start.2) | async-done | bytes 1769504 | tf_op jit(solution)/shard_map/all_to_all | solution.py:280
  101.0 0.9 first.1
  101.9 4.3 %all-to-all-start.3 = ((bf16[4,224,128]{2,1,0:T(8,128)(2,1)}), bf16[4,224,128]{2,1,0:T(8,128)(2,1)S(1)}, u32[]{:S(2)}, u32[]{:S(2)}) async-start(bf16[4,224,128]{2,1,0:T(8,128)(2,1)} %first.1), calls=%async_computation.3 | async-start | bytes 458752 | tf_op jit(solution)/shard_map/all_to_all | solution.py:280
  106.2 6.7 %collective-permute-start.4 = (f32[2,768]{1,0:T(2,128)S(1)}, f32[2,768]{1,0:T(2,128)S(1)}, u32[]{:S(2)}, u32[]{:S(2)}) collective-permute-start(f32[2,768]{1,0:T(2,128)S(1)} %psum.7.totals), channel_id=1, source_target_pairs={{0,112},{16,96},{32,80},{48,64},{64,48},{80,32},{96,16},{112,0},{1... | collective-permute-start | bytes 18440 | tf_op jit(solution)/shard_map/ppermute | solution.py:339
  112.9 1.9 %collective-permute-done.4.totals_y = f32[2,768]{1,0:T(2,128)S(1)} collective-permute-done((f32[2,768]{1,0:T(2,128)S(1)}, f32[2,768]{1,0:T(2,128)S(1)}, u32[]{:S(2)}, u32[]{:S(2)}) %collective-permute-start.4) | collective-permute-done | bytes 6176 | tf_op jit(solution)/shard_map/ppermute | solution.py:339
  114.8 1.4 all-to-all-done.3.got
  116.2 0.8 second.1
  117.0 6.2 %all-to-all-start.4 = ((bf16[8,64,128]{2,1,0:T(8,128)(2,1)}), bf16[8,64,128]{2,1,0:T(8,128)(2,1)S(1)}, u32[]{:S(2)}, u32[]{:S(2)}) async-start(bf16[8,64,128]{2,1,0:T(8,128)(2,1)} %second.1), calls=%async_computation.4 | async-start | bytes 262144 | tf_op jit(solution)/shard_map/all_to_all | solution.py:280
  123.1 4.8 %acts.1 = bf16[3,256,768]{2,1,0:T(8,128)(2,1)} custom-call(s32[2]{0:T(128)} %copy-done.10, f32[4,768]{1,0:T(4,128)} %copy-done.8, bf16[256,768]{1,0:T(8,128)(2,1)} %bitcast.13, bf16[768,768]{1,0:T(8,128)(2,1)} %copy-done.3, bf16[512,768]{1,0:T(8,128)(2,1)} %copy-done.2, s32[1,768]{1,0:T(1,128)} %fusion.channel), custom_call_target="tpu_custom_call" | custom-call | flops 905969664 | bytes 2097152 | tf_op jit(solution)/shard_map/acts/pallas_call | solution.py:347
  128.0 4.2 %all-to-all-done.4.got = bf16[8,64,128]{2,1,0:T(8,128)(2,1)S(1)} async-done(((bf16[8,64,128]{2,1,0:T(8,128)(2,1)}), bf16[8,64,128]{2,1,0:T(8,128)(2,1)S(1)}, u32[]{:S(2)}, u32[]{:S(2)}) %all-to-all-start.4) | async-done | bytes 131104 | tf_op jit(solution)/shard_map/all_to_all | solution.py:280
  132.2 0.8 third.1
  133.0 4.8 %all-to-all-start.5 = ((bf16[16,64,128]{2,1,0:T(8,128)(2,1)}), bf16[16,64,128]{2,1,0:T(8,128)(2,1)S(1)}, u32[]{:S(2)}, u32[]{:S(2)}) async-start(bf16[16,64,128]{2,1,0:T(8,128)(2,1)} %third.1), calls=%async_computation.5 | async-start | bytes 524288 | tf_op jit(solution)/shard_map/all_to_all | solution.py:280
  137.8 0.0 copy-start.5
  137.8 0.0 copy-start.7
  137.8 0.0 copy-start.9
  137.8 5.3 %forward.1 = bf16[256,768]{1,0:T(8,128)(2,1)} custom-call(bf16[3,256,768]{2,1,0:T(8,128)(2,1)} %acts.1, bf16[256,768]{1,0:T(8,128)(2,1)} %bitcast.14, bf16[8,3,48,768]{3,2,1,0:T(8,128)(2,1)} %bitcast.24, bf16[8,3,48,768]{3,2,1,0:T(8,128)(2,1)} %copy-done.11), custom_call_target="tpu_custom_call" | custom-call | flops 905969664 | bytes 6291456 | tf_op jit(solution)/shard_map/forward/pallas_call | solution.py:354
  143.1 2.9 %all-to-all-done.5.got = bf16[16,64,128]{2,1,0:T(8,128)(2,1)S(1)} async-done(((bf16[16,64,128]{2,1,0:T(8,128)(2,1)}), bf16[16,64,128]{2,1,0:T(8,128)(2,1)S(1)}, u32[]{:S(2)}, u32[]{:S(2)}) %all-to-all-start.5) | async-done | bytes 262176 | tf_op jit(solution)/shard_map/all_to_all | solution.py:280
  146.1 0.0 copy-done.1
  146.1 0.0 copy-done.5
  146.1 1.6 %last.1 = (bf16[256,768]{1,0:T(8,128)(2,1)}, f32[3,24,768]{2,1,0:T(8,128)}, f32[768]{0:T(1024)}, f32[768]{0:T(1024)}) custom-call(bf16[16,64,128]{2,1,0:T(8,128)(2,1)S(1)} %all-to-all-done.5.got, f32[4,768]{1,0:T(4,128)S(1)} %copy-done.9, bf16[256,768]{1,0:T(8,128)(2,1)S(1)} %bitcast.16, bf16[256,768]{1,0:T(8,128)(2,1)S(1)} %bitcast.20, f32[256,768]{1,0:T(8,128)S(1)} %copy-done.7), custom_call_target="tpu_custom_call" | custom-call | bytes 1048576 | tf_op jit(solution)/shard_map/last/pallas_call | solution.py:359
  (12 shorter events, 0.1 us)
Async XLA Ops:
  7.2 10.7 %copy-start.13 = (bf16[24,3,768]{2,0,1:T(8,128)(2,1)S(1)}, bf16[24,3,768]{2,0,1:T(8,128)(2,1)}, u32[]{:S(2)}) copy-start(bf16[24,3,768]{2,0,1:T(8,128)(2,1)} %param.8) | copy-start | bytes 331780
  7.2 73.3 %all-gather.3.cloned.1.call-start = ((), (), s32[]{:S(2)}) async-start(), calls=%async_computation.6 | async-start | bytes 1990656 | tf_op jit(solution)/shard_map/all_gather | solution.py:313
  7.2 9.9 %collective-permute-start = (bf16[3,24,768]{2,1,0:T(8,128)(2,1)}, bf16[3,24,768]{2,1,0:T(8,128)(2,1)S(1)}, u32[]{:S(2)}, u32[]{:S(2)}) collective-permute-start(bf16[3,24,768]{2,1,0:T(8,128)(2,1)} %bitcast.26), channel_id=1, source_target_pairs={{0,112},{16,96},{32,80},{48,64},{64,48},{80,32},{96,16},{112,0},{1... | collective-permute-start | bytes 331784 | tf_op jit(solution)/shard_map/ppermute | solution.py:306
  15.1 3.5 %copy-start.12 = (f32[16,2,768]{2,1,0:T(2,128)S(1)}, f32[16,2,768]{2,1,0:T(2,128)}, u32[]{:S(2)}) copy-start(f32[16,2,768]{2,1,0:T(2,128)} %stats.1) | copy-start | bytes 294916
  17.1 23.8 %collective-permute-start.1 = (bf16[512,768]{1,0:T(8,128)(2,1)S(1)}, bf16[512,768]{1,0:T(8,128)(2,1)S(1)}, u32[]{:S(2)}, u32[]{:S(2)}) collective-permute-start(bf16[512,768]{1,0:T(8,128)(2,1)S(1)} %pad_maximum_fusion.1), channel_id=1, source_target_pairs={{1,2},{2,1},{3,4},{4,3},{5,6},{6,5},{7,8},{8,7},{9,10},{10,9},{11,... | collective-permute-start | bytes 2359304 | tf_op jit(solution)/shard_map/ppermute | solution.py:312
  40.9 30.0 %copy-start.2 = (bf16[512,768]{1,0:T(8,128)(2,1)}, bf16[512,768]{1,0:T(8,128)(2,1)S(1)}, u32[]{:S(2)}) copy-start(bf16[512,768]{1,0:T(8,128)(2,1)S(1)} %collective-permute-done.1.outer.outer_h) | copy-start | bytes 2359300
  41.0 18.8 %copy-start.14 = (f32[768]{0:T(1024)S(1)}, f32[768]{0:T(1024)}, u32[]{:S(2)}) copy-start(f32[768]{0:T(1024)} %param.6) | copy-start | bytes 9220
  41.0 18.8 %copy-start.15 = (f32[768]{0:T(1024)S(1)}, f32[768]{0:T(1024)}, u32[]{:S(2)}) copy-start(f32[768]{0:T(1024)} %param.7) | copy-start | bytes 9220
  41.0 30.0 %copy-start = (bf16[1,256,768]{2,1,0:T(8,128)(2,1)S(1)}, bf16[1,256,768]{2,1,0:T(8,128)(2,1)}, u32[]{:S(2)}) copy-start(bf16[1,256,768]{2,1,0:T(8,128)(2,1)} %param.5) | copy-start | bytes 1179652
  41.0 30.0 %copy-start.4 = (bf16[1,256,768]{2,1,0:T(8,128)(2,1)S(1)}, bf16[1,256,768]{2,1,0:T(8,128)(2,1)}, u32[]{:S(2)}) copy-start(bf16[1,256,768]{2,1,0:T(8,128)(2,1)} %param.9) | copy-start | bytes 1179652
  42.1 28.8 %collective-permute-start.2 = (bf16[768,768]{1,0:T(8,128)(2,1)}, bf16[768,768]{1,0:T(8,128)(2,1)S(1)}, u32[]{:S(2)}, u32[]{:S(2)}) collective-permute-start(bf16[768,768]{1,0:T(8,128)(2,1)} %pad_maximum_fusion), channel_id=1, source_target_pairs={{0,1},{1,0},{2,3},{3,2},{4,5},{5,4},{6,7},{7,6},{8,9},{9,8},{10,11... | collective-permute-start | bytes 3538952 | tf_op jit(solution)/shard_map/ppermute | solution.py:317
  44.8 26.2 %all-to-all-start.1 = ((f32[32,2,768]{2,1,0:T(2,128)}), f32[32,2,768]{2,1,0:T(2,128)S(1)}, u32[]{:S(2)}, u32[]{:S(2)}) async-start(f32[32,2,768]{2,1,0:T(2,128)} %merge.1), calls=%async_computation.1 | async-start | bytes 393216 | tf_op jit(solution)/shard_map/all_to_all | solution.py:280
  59.8 13.9 %copy-start.10 = (s32[2]{0:T(128)}, s32[2]{0:T(128)S(1)}, u32[]{:S(2)}) copy-start(s32[2]{0:T(128)S(1)} %pad_add_fusion.place) | copy-start | bytes 28
  71.0 2.8 %copy-start.3 = (bf16[768,768]{1,0:T(8,128)(2,1)}, bf16[768,768]{1,0:T(8,128)(2,1)S(1)}, u32[]{:S(2)}) copy-start(bf16[768,768]{1,0:T(8,128)(2,1)S(1)} %collective-permute-done.2.mate.mate_h) | copy-start | bytes 3538948
  73.7 1.2 copy-start.6
  75.0 0.6 copy-start.8
  75.6 25.4 %all-to-all-start.2 = ((bf16[8,48,2304]{2,1,0:T(8,128)(2,1)}), bf16[8,48,2304]{2,1,0:T(8,128)(2,1)S(1)}, u32[]{:S(2)}, u32[]{:S(2)}) async-start(bf16[8,48,2304]{2,1,0:T(8,128)(2,1)} %bitcast.21), calls=%async_computation.2 | async-start | bytes 3538944 | tf_op jit(solution)/shard_map/all_to_all | solution.py:280
  80.4 5.8 %collective-permute-start.3 = (bf16[8,3,48,768]{3,2,1,0:T(8,128)(2,1)}, bf16[8,3,48,768]{3,2,1,0:T(8,128)(2,1)S(1)}, u32[]{:S(2)}, u32[]{:S(2)}) collective-permute-start(bf16[8,3,48,768]{3,2,1,0:T(8,128)(2,1)} %bitcast.22), channel_id=1, source_target_pairs={{0,1},{1,0},{2,3},{3,2},{4,5},{5,4},{6,7},{7,6},{8,9},{9,8},{10,11... | collective-permute-start | bytes 5308424 | tf_op jit(solution)/shard_map/ppermute | solution.py:325
  86.2 1.2 copy-start.11
  101.9 14.3 %all-to-all-start.3 = ((bf16[4,224,128]{2,1,0:T(8,128)(2,1)}), bf16[4,224,128]{2,1,0:T(8,128)(2,1)S(1)}, u32[]{:S(2)}, u32[]{:S(2)}) async-start(bf16[4,224,128]{2,1,0:T(8,128)(2,1)} %first.1), calls=%async_computation.3 | async-start | bytes 458752 | tf_op jit(solution)/shard_map/all_to_all | solution.py:280
  106.2 8.6 %collective-permute-start.4 = (f32[2,768]{1,0:T(2,128)S(1)}, f32[2,768]{1,0:T(2,128)S(1)}, u32[]{:S(2)}, u32[]{:S(2)}) collective-permute-start(f32[2,768]{1,0:T(2,128)S(1)} %psum.7.totals), channel_id=1, source_target_pairs={{0,112},{16,96},{32,80},{48,64},{64,48},{80,32},{96,16},{112,0},{1... | collective-permute-start | bytes 18440 | tf_op jit(solution)/shard_map/ppermute | solution.py:339
  117.0 15.2 %all-to-all-start.4 = ((bf16[8,64,128]{2,1,0:T(8,128)(2,1)}), bf16[8,64,128]{2,1,0:T(8,128)(2,1)S(1)}, u32[]{:S(2)}, u32[]{:S(2)}) async-start(bf16[8,64,128]{2,1,0:T(8,128)(2,1)} %second.1), calls=%async_computation.4 | async-start | bytes 262144 | tf_op jit(solution)/shard_map/all_to_all | solution.py:280
  133.0 13.1 %all-to-all-start.5 = ((bf16[16,64,128]{2,1,0:T(8,128)(2,1)}), bf16[16,64,128]{2,1,0:T(8,128)(2,1)S(1)}, u32[]{:S(2)}, u32[]{:S(2)}) async-start(bf16[16,64,128]{2,1,0:T(8,128)(2,1)} %third.1), calls=%async_computation.5 | async-start | bytes 524288 | tf_op jit(solution)/shard_map/all_to_all | solution.py:280
  137.7 8.3 %copy-start.1 = (bf16[1,256,768]{2,1,0:T(8,128)(2,1)S(1)}, bf16[1,256,768]{2,1,0:T(8,128)(2,1)}, u32[]{:S(2)}) copy-start(bf16[1,256,768]{2,1,0:T(8,128)(2,1)} %param.5) | copy-start | bytes 1179652
  137.8 8.3 %copy-start.5 = (bf16[1,256,768]{2,1,0:T(8,128)(2,1)S(1)}, bf16[1,256,768]{2,1,0:T(8,128)(2,1)}, u32[]{:S(2)}) copy-start(bf16[1,256,768]{2,1,0:T(8,128)(2,1)} %param.9) | copy-start | bytes 1179652
  137.8 8.3 %copy-start.7 = (f32[256,768]{1,0:T(8,128)S(1)}, f32[256,768]{1,0:T(8,128)}, u32[]{:S(2)}) copy-start(f32[256,768]{1,0:T(8,128)} %get-tuple-element.40.pre_h) | copy-start | bytes 2359300
  137.8 8.3 %copy-start.9 = (f32[4,768]{1,0:T(4,128)S(1)}, f32[4,768]{1,0:T(4,128)}, u32[]{:S(2)}) copy-start(f32[4,768]{1,0:T(4,128)} %copy-done.8) | copy-start | bytes 36868
Sparse Core Ops, SparseCore 0:
  18.7 54.8 all-gather.2

commit v5 on v4

--- a/solution.py
+++ b/solution.py
@@ -116,7 +116,7 @@
     v = normalised(jnp.dot(both, pick, preferred_element_type=F32), chosen)
     v = chosen[2:3] * v + chosen[3:4]
     act = (v * half_gate(v)).astype(BF16)
-    own, next_own, last_own = cot[...], mate[:L], outer[:L]
+    own, next_own, last_own = cot[...], mate[:L], outer[...]
     beyond = mate[2 * L :]
     cots = (
         (jnp.where(low, next_own, last_own), jnp.where(low, beyond, own)),
@@ -136,7 +136,7 @@
     place, vectors, inputs_h, mate_h, cot_h, outer_h, kc, ko, channel, pre_grad, totals,
     inputs, mate, cot, outer, kern, sems,
 ):
-    sources = [inputs_h, mate_h.at[:L], cot_h, outer_h.at[:L], kc, ko]
+    sources = [inputs_h, mate_h.at[:L], cot_h, outer_h, kc, ko]
     copies = fetch(sources, [inputs, mate, cot, outer, kern.at[:NZ], kern.at[NZ:]], sems)
     low = place[0] == 0
     pick = one_hot(channel)
@@ -179,7 +179,8 @@
     return rows[0:2] + rows[2:4]
 
 
-def first_kernel(got, message):
+def first_kernel(got, totals, message, held):
+    packed = put_totals(totals[...], held).astype(F32)
     parts = got[...].astype(F32)
     total = jnp.sum(parts, axis=0)
     zero = jnp.zeros((8, 128), F32)
@@ -190,13 +191,14 @@
                 sub, tile = divmod(l * PIECE + piece, 18)
                 row = sub * OWNERS + h * NZ
                 tiles.append(total[row : row + 8, 128 * tile : 128 * tile + 128])
-            tiles.append(zero)
+            tiles += [packed, zero, zero]
             message[l * NYH + h] = jnp.concatenate(tiles, axis=0).astype(BF16)
 
 
-def second_kernel(got, totals, totals_y, message, held, line):
+def second_kernel(got, message, held, line):
     total = jnp.sum(got[...].astype(F32), axis=0)
-    packed = put_totals(totals[...] + totals_y[...], held).astype(F32)
+    held[...] = total[PIECE * 8 : PIECE * 8 + 32]
+    packed = put_totals(get_totals(held), held).astype(F32)
     for piece in range(PIECE):
         line[:, TOT + piece, :] = total[piece * 8 : piece * 8 + 8]
     for z in range(NZ):
@@ -220,10 +222,11 @@
     total = jnp.zeros((32, 128), F32)
     for member in range(NX * NYL):
         part = got[member].astype(F32)
-        total += part[:32]
         line[...] = part
         x, l = divmod(member, NYL)
         a, b = divmod(l, NYB)
+        if a == 0:
+            total += part[:32]
         for piece in range(PIECE):
             sub, tile = divmod(a * PIECE + piece, 18)
             row = (x * NYB + b) * SUB + sub
@@ -243,32 +246,33 @@
     grad_in[...] = (cot[...].astype(F32) + bn_grad).astype(BF16)
 
 
-def acts_kernel(place, vectors, inputs, mate_h, outer_h, channel, acts, mate, outer, sems):
-    copies = fetch([outer_h.at[L:], mate_h.at[L : 2 * L]], [outer, mate], sems)
+def activated(block, rows):
+    v = rows[2:3] * normalised(block.astype(F32), rows) + rows[3:4]
+    return v * half_gate(v)
+
+
+def acts_kernel(vectors, inputs, mate_h, channel, acts, mate, sems):
+    copies = fetch([mate_h.at[L : 2 * L]], [mate], sems)
     rows = vectors[...]
-
-    def activate(block):
-        v = rows[2:3] * normalised(block.astype(F32), rows) + rows[3:4]
-        return v * half_gate(v)
-
+    pick = one_hot(channel)
+    here = activated(inputs[...], rows).astype(BF16)
+    acts[0] = jnp.dot(here, pick, preferred_element_type=F32).astype(BF16)
+    copies[0].wait()
+    near = activated(mate[...], rows).astype(BF16)
+    acts[1] = jnp.dot(near, pick, preferred_element_type=F32).astype(BF16)
+
+
+def forward_kernel(place, vectors, acts, inputs, outer, channel, kc, ko, output, kern, sems):
+    copies = fetch([kc, ko], [kern.at[:NZ], kern.at[NZ:]], sems)
     low = place[0] == 0
-    pick = one_hot(channel)
-    here = activate(inputs[...]).astype(BF16)
-    copies[0].wait()
-    away = jnp.where(place[1] == 1, activate(outer[...]), 0.0).astype(BF16)
-    copies[1].wait()
-    near = activate(mate[...]).astype(BF16)
-    for tap, a in enumerate((jnp.where(low, away, near), here, jnp.where(low, near, away))):
-        acts[tap] = jnp.dot(a, pick, preferred_element_type=F32).astype(BF16)
-
-
-def forward_kernel(acts, inputs, kc, ko, output, kern, sems):
-    copies = fetch([kc, ko], [kern.at[:NZ], kern.at[NZ:]], sems)
+    away = jnp.where(place[1] == 1, activated(outer[...], vectors[...]), 0.0).astype(BF16)
+    away = jnp.dot(away, one_hot(channel), preferred_element_type=F32).astype(BF16)
+    near = acts[1]
     total = inputs[...].astype(F32)
     for copy in copies:
         copy.wait()
-    for tap in range(3):
-        total += jnp.dot(acts[tap], by_tap(kern, tap), preferred_element_type=F32)
+    for tap, a in enumerate((jnp.where(low, away, near), acts[0], jnp.where(low, near, away))):
+        total += jnp.dot(a, by_tap(kern, tap), preferred_element_type=F32)
     output[...] = total.astype(BF16)
 
 
@@ -304,17 +308,16 @@
 
     own = kernel.transpose(1, 0, 2)
     other = lax.ppermute(own, Y, swap_y)
-    pair = jnp.concatenate([cotangent, inputs], axis=0)
-    stats = call(stats_kernel, shape(NZ * NC, 2, C), "stats", 56, "a", scratch=[
+    stats = call(stats_kernel, shape(NZ * NC, 2, C), "stats", 8, "a", scratch=[
         pltpu.VMEM((L, C), BF16), pltpu.SemaphoreType.DMA((1,)),
     ])(inputs)
-    stats, other, pair = lax.optimization_barrier((stats, other, pair))
-    outer = lax.ppermute(pair, SEQ, swap_out)
+    stats, other, held_cot = lax.optimization_barrier((stats, other, cotangent))
+    outer = lax.ppermute(held_cot, SEQ, swap_out)
     kernel_c = lax.all_gather(jnp.concatenate([own, other], axis=1), "z", axis=0, tiled=False)
     stats = exchange(stats, ("z", "c"))
-    stats, outer, pair = lax.optimization_barrier((stats, outer, pair))
+    stats, outer, held_cot, held_in = lax.optimization_barrier((stats, outer, cotangent, inputs))
     stats = call(merge_kernel, shape(NX * NYL * NYH, 2, C), "merge", 8)(stats)
-    mate = lax.ppermute(jnp.concatenate([pair, outer[:L]], axis=0), "c", swap_c)
+    mate = lax.ppermute(jnp.concatenate([held_cot, held_in, outer], axis=0), "c", swap_c)
     stats = exchange(stats, ("x",) + Y)
 
     terms, vectors = call(
@@ -335,26 +338,28 @@
     totals = lax.psum(totals, "c")
 
     held = pltpu.VMEM((32, 128), F32)
-    terms, totals = lax.optimization_barrier((terms, totals))
-    totals_y = lax.ppermute(totals, Y, swap_y)
-    message = call(first_kernel, shape(NYA * NYH, 224, 128, kind=BF16), "first", 12)(terms)
+    message = call(
+        first_kernel, shape(NYA * NYH, 256, 128, kind=BF16), "first", 12, scratch=[held]
+    )(terms, totals)
     got = exchange(message, ("ya", "yh"))
     message = call(
         second_kernel, shape(NZ, MSG, 128, kind=BF16), "second", 12,
         scratch=[held, pltpu.VMEM((NZ, MSG, 128), F32)],
-    )(got, totals, totals_y)
+    )(got)
+    message, late_in = lax.optimization_barrier((message, inputs))
+    outer_in = lax.ppermute(late_in, SEQ, swap_out)
     got = exchange(message, "z")
     acts = call(
-        acts_kernel, shape(3, L, C, kind=BF16), "acts", 56, "svvaav", flops=2 * L * C * C * 3, size=2 << 20,
-        scratch=[pltpu.VMEM((L, C), BF16), pltpu.VMEM((L, C), BF16), pltpu.SemaphoreType.DMA((2,))],
-    )(place, vectors, inputs, mate, outer, channel)
+        acts_kernel, shape(2, L, C, kind=BF16), "acts", 56, "vvav", flops=2 * L * C * C * 2, size=2 << 20,
+        scratch=[pltpu.VMEM((L, C), BF16), pltpu.SemaphoreType.DMA((1,))],
+    )(vectors, inputs, mate, channel)
     got, acts = lax.optimization_barrier((got, acts))
     message = call(third_kernel, shape(NX * NYL, MSG, 128, kind=BF16), "third", 12, scratch=[held])(got)
     got = exchange(message, DP)
     output = call(
-        forward_kernel, shape(L, C, kind=BF16), "forward", 56, "vvaa", flops=2 * L * C * C * 3, size=6 << 20,
+        forward_kernel, shape(L, C, kind=BF16), "forward", 56, "svvvvvaa", flops=2 * L * C * C * 4, size=6 << 20,
         scratch=[kern, pltpu.SemaphoreType.DMA((2,))],
-    )(acts, inputs, kernel_c, kernel_o)
+    )(place, vectors, acts, inputs, outer_in, channel, kernel_c, kernel_o)
     got, output = lax.optimization_barrier((got, output))
     grad_in, weights, gain_grad, shift_grad = call(
         last_kernel,

time: 155 us -> 153 us (0.987)
  the two profiles are of different devices: /device:TPU:8 before, /device:TPU:1 now
where the time goes in v5:
time: 153 us; the launch traced here: 152 us
  starting transfers between devices  48.7 us (32%)
  blocking collectives  34.5 us (23%)
  Pallas kernels  26.7 us (17%)
  waiting for transfers between devices  21.1 us (14%)
  between operations  14.3 us (9%)
  other arithmetic  3.67 us (2%)
  local copies, waits for them, and re-layouts  2.57 us (2%)
    all_to_all x2, blocking collectives, exchange(): return lax.all_to_all(value, axes, 0, 0, tiled=True)  31.9 us
    all_to_all x4, starting transfers between devices, exchange(): return lax.all_to_all(value, axes, 0, 0, tiled=True)  20.5 us
    all_to_all x4, waiting for transfers between devices, exchange(): return lax.all_to_all(value, axes, 0, 0, tiled=True)  17.1 us
    ppermute x1, starting transfers between devices, body(): outer = lax.ppermute(held_cot, SEQ, swap_out)  8.26 us
    ppermute x1, starting transfers between devices, body(): outer_in = lax.ppermute(late_in, SEQ, swap_out)  7.2 us
    pallas_call x1, Pallas kernels, body(): call(back_kernel, (shape(L, C), shape(2, C)), 'back', 56, 'svaaaaaav', fl...  6.96 us
    ppermute x1, starting transfers between devices, body(): other = lax.ppermute(own, Y, swap_y)  5.93 us
    pallas_call x1, Pallas kernels, body(): call(forward_kernel, shape(L, C, kind=BF16), 'forward', 56, 'svvvvvaa', f...  5.53 us
  transfers between devices with their start and end apart: 10, of which 5 were waited for; matrix products, arithmetic and copies ran while one was open for 1% of the time, Pallas kernels for 16%

profile of v5, /device:TPU:1, one launch (start us, length us, event | category | flops | bytes accessed | tf_op | source)
XLA Modules:
  0.0 151.6 jit_solution(13264318315875054222)
XLA Ops:
  7.2 0.0 all-gather.3.cloned.1.call-start
  7.2 5.9 %collective-permute-start = (bf16[3,24,768]{2,1,0:T(8,128)(2,1)}, bf16[3,24,768]{2,1,0:T(8,128)(2,1)S(1)}, u32[]{:S(2)}, u32[]{:S(2)}) collective-permute-start(bf16[3,24,768]{2,1,0:T(8,128)(2,1)} %bitcast.19), channel_id=1, source_target_pairs={{0,112},{16,96},{32,80},{48,64},{64,48},{80,32},{96,16},{112,0},{1... | collective-permute-start | bytes 331784 | tf_op jit(solution)/shard_map/ppermute | solution.py:310
  13.1 1.2 stats.1
  14.4 1.1 collective-permute-done
  15.5 1.6 %pad_maximum_fusion.1 = bf16[3,48,768]{2,1,0:T(8,128)(2,1)} fusion(bf16[3,24,768]{2,1,0:T(8,128)(2,1)S(1)} %collective-permute-done, bf16[3,24,768]{2,1,0:T(8,128)(2,1)} %bitcast.20), kind=kLoop, calls=%fused_computation.1 | loop fusion | flops 442368 | bytes 442368 | tf_op jit(solution)/shard_map/concatenate | solution.py:316
  17.1 0.0 copy-start.10
  17.1 0.0 copy-start.11
  17.1 0.0 copy-start.1
  17.1 0.0 all-gather.3.cloned.1.call-update
  17.1 8.3 %collective-permute-start.1 = (bf16[256,768]{1,0:T(8,128)(2,1)}, bf16[256,768]{1,0:T(8,128)(2,1)S(1)}, u32[]{:S(2)}, u32[]{:S(2)}) collective-permute-start(bf16[256,768]{1,0:T(8,128)(2,1)} %bitcast.10), channel_id=1, source_target_pairs={{1,2},{2,1},{3,4},{4,3},{5,6},{6,5},{7,8},{8,7},{9,10},{10,9},{11,... | collective-permute-start | bytes 1179656 | tf_op jit(solution)/shard_map/ppermute | solution.py:315
  25.4 17.8 %all_to_all.30.parts = f32[16,2,768]{2,1,0:T(2,128)S(1)} all-to-all(f32[16,2,768]{2,1,0:T(2,128)S(1)} %stats.1), channel_id=1, replica_groups=mesh['x'=4,'ya'=2,'yb'=2,'yh'=2,'z'=8,'c'=2] {'z','c'}, dimensions={0} | all-to-all | bytes 196608 | tf_op jit(solution)/shard_map/all_to_all | solution.py:284
  43.2 0.0 collective-permute-done.1.outer.outer_h
  43.2 0.0 copy-start.3
  43.2 1.3 pad_maximum_fusion
  44.5 1.9 %collective-permute-start.2 = (bf16[768,768]{1,0:T(8,128)(2,1)S(1)}, bf16[768,768]{1,0:T(8,128)(2,1)S(1)}, u32[]{:S(2)}, u32[]{:S(2)}) collective-permute-start(bf16[768,768]{1,0:T(8,128)(2,1)S(1)} %pad_maximum_fusion), channel_id=1, source_target_pairs={{0,1},{1,0},{2,3},{3,2},{4,5},{5,4},{6,7},{7,6},{8,9},{9,8},{10,11... | collective-permute-start | bytes 3538952 | tf_op jit(solution)/shard_map/ppermute | solution.py:320
  46.5 0.8 merge.1
  47.2 9.1 %all-to-all-start.1 = ((f32[32,2,768]{2,1,0:T(2,128)}), f32[32,2,768]{2,1,0:T(2,128)S(1)}, u32[]{:S(2)}, u32[]{:S(2)}) async-start(f32[32,2,768]{2,1,0:T(2,128)} %merge.1), calls=%async_computation.1 | async-start | bytes 393216 | tf_op jit(solution)/shard_map/all_to_all | solution.py:284
  56.4 0.0 copy-done.10
  56.4 0.0 copy-done.11
  56.5 0.1 pad_add_fusion.place
  56.5 0.0 copy-start.7
  56.6 9.6 %all-to-all-done.1.parts = f32[32,2,768]{2,1,0:T(2,128)S(1)} async-done(((f32[32,2,768]{2,1,0:T(2,128)}), f32[32,2,768]{2,1,0:T(2,128)S(1)}, u32[]{:S(2)}, u32[]{:S(2)}) %all-to-all-start.1) | async-done | bytes 196640 | tf_op jit(solution)/shard_map/all_to_all | solution.py:284
  66.2 0.0 collective-permute-done.2.mate.mate_h
  66.2 0.0 copy-done.1
  66.2 0.0 copy-start
  66.2 4.7 %terms.1 = (bf16[384,2304]{1,0:T(8,128)(2,1)}, f32[4,768]{1,0:T(4,128)S(1)}) custom-call(s32[2]{0:T(128)S(1)} %pad_add_fusion.place, f32[32,2,768]{2,1,0:T(2,128)S(1)} %all-to-all-done.1.parts, f32[1,768]{1,0:T(1,128)S(1)} %broadcast_in_dim.14.gain, f32[1,768]{1,0:T(1,128)S(1)} %broadcast_in_dim.15.shift, s32[1,384]{1,0:T(1,128)S(1)} %fusion.13.source, ...), custom_call_target="tpu_custom_call" | custom-call | flops 1207959552 | bytes 6291456 | tf_op jit(solution)/shard_map/terms/pallas_call | solution.py:323
  70.9 0.0 copy-done.3
  70.9 0.0 copy-done.7
  70.9 0.0 copy-done
  70.9 0.0 copy-start.5
  70.9 0.6 copy-done.5
  71.5 3.6 %all-to-all-start.2 = ((bf16[8,48,2304]{2,1,0:T(8,128)(2,1)}), bf16[8,48,2304]{2,1,0:T(8,128)(2,1)S(1)}, u32[]{:S(2)}, u32[]{:S(2)}) async-start(bf16[8,48,2304]{2,1,0:T(8,128)(2,1)} %bitcast.5), calls=%async_computation.2 | async-start | bytes 3538944 | tf_op jit(solution)/shard_map/all_to_all | solution.py:284
  75.1 0.0 all-gather.3.cloned.1.call-done
  75.2 4.9 %collective-permute-start.3 = (bf16[8,3,48,768]{3,2,1,0:T(8,128)(2,1)}, bf16[8,3,48,768]{3,2,1,0:T(8,128)(2,1)S(1)}, u32[]{:S(2)}, u32[]{:S(2)}) collective-permute-start(bf16[8,3,48,768]{3,2,1,0:T(8,128)(2,1)} %bitcast.15), channel_id=1, source_target_pairs={{0,1},{1,0},{2,3},{3,2},{4,5},{5,4},{6,7},{7,6},{8,9},{9,8},{10,11... | collective-permute-start | bytes 5308424 | tf_op jit(solution)/shard_map/ppermute | solution.py:328
  80.0 0.6 fusion.channel
  80.7 2.9 %collective-permute-done.3.ko = bf16[8,3,48,768]{3,2,1,0:T(8,128)(2,1)S(1)} collective-permute-done((bf16[8,3,48,768]{3,2,1,0:T(8,128)(2,1)}, bf16[8,3,48,768]{3,2,1,0:T(8,128)(2,1)S(1)}, u32[]{:S(2)}, u32[]{:S(2)}) %collective-permute-start.3) | collective-permute-done | bytes 1769504 | tf_op jit(solution)/shard_map/ppermute | solution.py:328
  83.5 0.0 copy-start.8
  83.5 1.2 copy-done.8
  84.7 7.0 %back.1 = (f32[256,768]{1,0:T(8,128)}, f32[2,768]{1,0:T(2,128)}) custom-call(s32[2]{0:T(128)} %copy-done.7, f32[4,768]{1,0:T(4,128)} %copy-done.5, bf16[256,768]{1,0:T(8,128)(2,1)} %bitcast.2.inputs.inputs_h, bf16[768,768]{1,0:T(8,128)(2,1)} %copy-done, bf16[256,768]{1,0:T(8,128)(2,1)} %bitcast.12, bf16[256,768]{1,0:T(8,128)(2,1)} %copy-done.3, ...), custom_call_target="tpu_custom_call" | custom-call | flops 1509949440 | bytes 8388608 | tf_op jit(solution)/shard_map/back/pallas_call | solution.py:330
  91.7 2.6 %psum.7.totals = f32[2,768]{1,0:T(2,128)S(1)} all-reduce(f32[2,768]{1,0:T(2,128)} %get-tuple-element.35), channel_id=1, replica_groups=mesh['x'=4,'ya'=2,'yb'=2,'yh'=2,'z'=8,'c'=2] {'c'}, use_global_device_ids=true, to_apply=%region_0.1 | all-reduce | flops 1536 | bytes 12288 | tf_op jit(solution)/shard_map/psum | solution.py:338
  94.3 1.3 all-to-all-done.2.got
  95.7 0.3 first.1
  96.0 14.1 %all_to_all.31.got = bf16[4,256,128]{2,1,0:T(8,128)(2,1)S(1)} all-to-all(bf16[4,256,128]{2,1,0:T(8,128)(2,1)S(1)} %first.1), channel_id=1, replica_groups=mesh['x'=4,'ya'=2,'yb'=2,'yh'=2,'z'=8,'c'=2] {'ya','yh'}, dimensions={0} | all-to-all | bytes 524288 | tf_op jit(solution)/shard_map/all_to_all | solution.py:284
  110.0 0.8 second.1
  110.8 3.4 %all-to-all-start.4 = ((bf16[8,64,128]{2,1,0:T(8,128)(2,1)}), bf16[8,64,128]{2,1,0:T(8,128)(2,1)S(1)}, u32[]{:S(2)}, u32[]{:S(2)}) async-start(bf16[8,64,128]{2,1,0:T(8,128)(2,1)} %second.1), calls=%async_computation.4 | async-start | bytes 262144 | tf_op jit(solution)/shard_map/all_to_all | solution.py:284
  114.2 7.2 %collective-permute-start.4 = (bf16[256,768]{1,0:T(8,128)(2,1)}, bf16[256,768]{1,0:T(8,128)(2,1)S(1)}, u32[]{:S(2)}, u32[]{:S(2)}) collective-permute-start(bf16[256,768]{1,0:T(8,128)(2,1)} %bitcast.2.inputs.inputs_h), channel_id=1, source_target_pairs={{1,2},{2,1},{3,4},{4,3},{5,6},{6,5},{7,8},{8,7},{9,10},{10,9},{11,... | collective-permute-start | bytes 1179656 | tf_op jit(solution)/shard_map/ppermute | solution.py:350
  121.4 3.6 %acts.1 = bf16[2,256,768]{2,1,0:T(8,128)(2,1)} custom-call(f32[4,768]{1,0:T(4,128)} %copy-done.5, bf16[256,768]{1,0:T(8,128)(2,1)} %bitcast.2.inputs.inputs_h, bf16[768,768]{1,0:T(8,128)(2,1)} %copy-done, s32[1,768]{1,0:T(1,128)} %fusion.channel), custom_call_target="tpu_custom_call" | custom-call | flops 603979776 | bytes 2097152 | tf_op jit(solution)/shard_map/acts/pallas_call | solution.py:352
  125.0 0.0 all-to-all-done.4.got
  125.0 0.8 third.1
  125.8 4.4 %all-to-all-start.5 = ((bf16[16,64,128]{2,1,0:T(8,128)(2,1)}), bf16[16,64,128]{2,1,0:T(8,128)(2,1)S(1)}, u32[]{:S(2)}, u32[]{:S(2)}) async-start(bf16[16,64,128]{2,1,0:T(8,128)(2,1)} %third.1), calls=%async_computation.5 | async-start | bytes 524288 | tf_op jit(solution)/shard_map/all_to_all | solution.py:284
  130.2 0.0 copy-start.2
  130.2 0.0 copy-start.4
  130.2 0.0 copy-start.6
  130.2 0.0 collective-permute-done.4.outer
  130.3 0.0 copy-start.9
  130.3 0.7 copy-done.9
  131.0 5.5 %forward.1 = bf16[256,768]{1,0:T(8,128)(2,1)} custom-call(s32[2]{0:T(128)} %copy-done.7, f32[4,768]{1,0:T(4,128)} %copy-done.5, bf16[2,256,768]{2,1,0:T(8,128)(2,1)} %acts.1, bf16[256,768]{1,0:T(8,128)(2,1)} %bitcast.2.inputs.inputs_h, bf16[256,768]{1,0:T(8,128)(2,1)} %copy-done.9, s32[1,768]{1,0:T(1,128)} %fusion.channel, bf16[8,3,48,768]{3,2,1,0:T(8,128)(2,1)} %bitcast.17, ...), custom_call_target="tpu_custom_call" | custom-call | flops 1207959552 | bytes 6291456 | tf_op jit(solution)/shard_map/forward/pallas_call | solution.py:359
  136.5 6.2 %all-to-all-done.5.got = bf16[16,64,128]{2,1,0:T(8,128)(2,1)S(1)} async-done(((bf16[16,64,128]{2,1,0:T(8,128)(2,1)}), bf16[16,64,128]{2,1,0:T(8,128)(2,1)S(1)}, u32[]{:S(2)}, u32[]{:S(2)}) %all-to-all-start.5) | async-done | bytes 262176 | tf_op jit(solution)/shard_map/all_to_all | solution.py:284
  142.7 0.0 copy-done.2
  142.7 0.0 copy-done.4
  142.7 0.0 copy-done.6
  142.7 2.0 %last.1 = (bf16[256,768]{1,0:T(8,128)(2,1)}, f32[3,24,768]{2,1,0:T(8,128)}, f32[768]{0:T(1024)}, f32[768]{0:T(1024)}) custom-call(bf16[16,64,128]{2,1,0:T(8,128)(2,1)S(1)} %all-to-all-done.5.got, f32[4,768]{1,0:T(4,128)S(1)} %copy-done.6, bf16[256,768]{1,0:T(8,128)(2,1)} %bitcast.2.inputs.inputs_h, bf16[256,768]{1,0:T(8,128)(2,1)S(1)} %bitcast.14, ...), custom_call_target="tpu_custom_call" | custom-call | bytes 1048576 | tf_op jit(solution)/shard_map/last/pallas_call | solution.py:364
  (3 shorter events, 0.0 us)
Async XLA Ops:
  7.2 68.0 %all-gather.3.cloned.1.call-start = ((), (), s32[]{:S(2)}) async-start(), calls=%async_computation.6 | async-start | bytes 1990656 | tf_op jit(solution)/shard_map/all_gather | solution.py:316
  7.2 8.3 %collective-permute-start = (bf16[3,24,768]{2,1,0:T(8,128)(2,1)}, bf16[3,24,768]{2,1,0:T(8,128)(2,1)S(1)}, u32[]{:S(2)}, u32[]{:S(2)}) collective-permute-start(bf16[3,24,768]{2,1,0:T(8,128)(2,1)} %bitcast.19), channel_id=1, source_target_pairs={{0,112},{16,96},{32,80},{48,64},{64,48},{80,32},{96,16},{112,0},{1... | collective-permute-start | bytes 331784 | tf_op jit(solution)/shard_map/ppermute | solution.py:310
  17.1 39.3 %copy-start.10 = (f32[768]{0:T(1024)S(1)}, f32[768]{0:T(1024)}, u32[]{:S(2)}) copy-start(f32[768]{0:T(1024)} %param.6) | copy-start | bytes 9220
  17.1 39.4 %copy-start.11 = (f32[768]{0:T(1024)S(1)}, f32[768]{0:T(1024)}, u32[]{:S(2)}) copy-start(f32[768]{0:T(1024)} %param.7) | copy-start | bytes 9220
  17.1 49.1 %copy-start.1 = (bf16[1,256,768]{2,1,0:T(8,128)(2,1)S(1)}, bf16[1,256,768]{2,1,0:T(8,128)(2,1)}, u32[]{:S(2)}) copy-start(bf16[1,256,768]{2,1,0:T(8,128)(2,1)} %param.9) | copy-start | bytes 1179652
  17.1 26.1 %collective-permute-start.1 = (bf16[256,768]{1,0:T(8,128)(2,1)}, bf16[256,768]{1,0:T(8,128)(2,1)S(1)}, u32[]{:S(2)}, u32[]{:S(2)}) collective-permute-start(bf16[256,768]{1,0:T(8,128)(2,1)} %bitcast.10), channel_id=1, source_target_pairs={{1,2},{2,1},{3,4},{4,3},{5,6},{6,5},{7,8},{8,7},{9,10},{10,9},{11,... | collective-permute-start | bytes 1179656 | tf_op jit(solution)/shard_map/ppermute | solution.py:315
  43.2 27.7 %copy-start.3 = (bf16[256,768]{1,0:T(8,128)(2,1)}, bf16[256,768]{1,0:T(8,128)(2,1)S(1)}, u32[]{:S(2)}) copy-start(bf16[256,768]{1,0:T(8,128)(2,1)S(1)} %collective-permute-done.1.outer.outer_h) | copy-start | bytes 1179652
  44.5 21.7 %collective-permute-start.2 = (bf16[768,768]{1,0:T(8,128)(2,1)S(1)}, bf16[768,768]{1,0:T(8,128)(2,1)S(1)}, u32[]{:S(2)}, u32[]{:S(2)}) collective-permute-start(bf16[768,768]{1,0:T(8,128)(2,1)S(1)} %pad_maximum_fusion), channel_id=1, source_target_pairs={{0,1},{1,0},{2,3},{3,2},{4,5},{5,4},{6,7},{7,6},{8,9},{9,8},{10,11... | collective-permute-start | bytes 3538952 | tf_op jit(solution)/shard_map/ppermute | solution.py:320
  47.2 18.9 %all-to-all-start.1 = ((f32[32,2,768]{2,1,0:T(2,128)}), f32[32,2,768]{2,1,0:T(2,128)S(1)}, u32[]{:S(2)}, u32[]{:S(2)}) async-start(f32[32,2,768]{2,1,0:T(2,128)} %merge.1), calls=%async_computation.1 | async-start | bytes 393216 | tf_op jit(solution)/shard_map/all_to_all | solution.py:284
  56.5 14.4 %copy-start.7 = (s32[2]{0:T(128)}, s32[2]{0:T(128)S(1)}, u32[]{:S(2)}) copy-start(s32[2]{0:T(128)S(1)} %pad_add_fusion.place) | copy-start | bytes 28
  66.2 4.7 %copy-start = (bf16[768,768]{1,0:T(8,128)(2,1)}, bf16[768,768]{1,0:T(8,128)(2,1)S(1)}, u32[]{:S(2)}) copy-start(bf16[768,768]{1,0:T(8,128)(2,1)S(1)} %collective-permute-done.2.mate.mate_h) | copy-start | bytes 3538948
  70.9 0.6 copy-start.5
  71.5 24.1 %all-to-all-start.2 = ((bf16[8,48,2304]{2,1,0:T(8,128)(2,1)}), bf16[8,48,2304]{2,1,0:T(8,128)(2,1)S(1)}, u32[]{:S(2)}, u32[]{:S(2)}) async-start(bf16[8,48,2304]{2,1,0:T(8,128)(2,1)} %bitcast.5), calls=%async_computation.2 | async-start | bytes 3538944 | tf_op jit(solution)/shard_map/all_to_all | solution.py:284
  75.2 8.4 %collective-permute-start.3 = (bf16[8,3,48,768]{3,2,1,0:T(8,128)(2,1)}, bf16[8,3,48,768]{3,2,1,0:T(8,128)(2,1)S(1)}, u32[]{:S(2)}, u32[]{:S(2)}) collective-permute-start(bf16[8,3,48,768]{3,2,1,0:T(8,128)(2,1)} %bitcast.15), channel_id=1, source_target_pairs={{0,1},{1,0},{2,3},{3,2},{4,5},{5,4},{6,7},{7,6},{8,9},{9,8},{10,11... | collective-permute-start | bytes 5308424 | tf_op jit(solution)/shard_map/ppermute | solution.py:328
  83.5 1.2 copy-start.8
  110.8 14.2 %all-to-all-start.4 = ((bf16[8,64,128]{2,1,0:T(8,128)(2,1)}), bf16[8,64,128]{2,1,0:T(8,128)(2,1)S(1)}, u32[]{:S(2)}, u32[]{:S(2)}) async-start(bf16[8,64,128]{2,1,0:T(8,128)(2,1)} %second.1), calls=%async_computation.4 | async-start | bytes 262144 | tf_op jit(solution)/shard_map/all_to_all | solution.py:284
  114.2 16.0 %collective-permute-start.4 = (bf16[256,768]{1,0:T(8,128)(2,1)}, bf16[256,768]{1,0:T(8,128)(2,1)S(1)}, u32[]{:S(2)}, u32[]{:S(2)}) collective-permute-start(bf16[256,768]{1,0:T(8,128)(2,1)} %bitcast.2.inputs.inputs_h), channel_id=1, source_target_pairs={{1,2},{2,1},{3,4},{4,3},{5,6},{6,5},{7,8},{8,7},{9,10},{10,9},{11,... | collective-permute-start | bytes 1179656 | tf_op jit(solution)/shard_map/ppermute | solution.py:350
  125.8 16.9 %all-to-all-start.5 = ((bf16[16,64,128]{2,1,0:T(8,128)(2,1)}), bf16[16,64,128]{2,1,0:T(8,128)(2,1)S(1)}, u32[]{:S(2)}, u32[]{:S(2)}) async-start(bf16[16,64,128]{2,1,0:T(8,128)(2,1)} %third.1), calls=%async_computation.5 | async-start | bytes 524288 | tf_op jit(solution)/shard_map/all_to_all | solution.py:284
  130.2 12.5 %copy-start.2 = (bf16[1,256,768]{2,1,0:T(8,128)(2,1)S(1)}, bf16[1,256,768]{2,1,0:T(8,128)(2,1)}, u32[]{:S(2)}) copy-start(bf16[1,256,768]{2,1,0:T(8,128)(2,1)} %param.9) | copy-start | bytes 1179652
  130.2 12.5 %copy-start.4 = (f32[256,768]{1,0:T(8,128)S(1)}, f32[256,768]{1,0:T(8,128)}, u32[]{:S(2)}) copy-start(f32[256,768]{1,0:T(8,128)} %get-tuple-element.42.pre_h) | copy-start | bytes 2359300
  130.2 12.5 %copy-start.6 = (f32[4,768]{1,0:T(4,128)S(1)}, f32[4,768]{1,0:T(4,128)}, u32[]{:S(2)}) copy-start(f32[4,768]{1,0:T(4,128)} %copy-done.5) | copy-start | bytes 36868
  130.3 0.7 copy-start.9
Sparse Core Ops, SparseCore 0:
  17.2 48.4 all-gather.2

commit v6 on v5

--- a/solution.py
+++ b/solution.py
@@ -99,23 +99,26 @@
     return 0.5 * (1.0 + lax.erf(v * SQRT_HALF))
 
 
-def terms_kernel(place, parts, gain, shift, source, inputs, mate, cot, outer, terms, vectors):
+def prepare_kernel(parts, gain, shift, source, inputs, vectors, chosen, act):
     total, squares = merged(parts[...], L * NZ * NC)
     mean = total / COUNT
     inv_std = lax.rsqrt(squares / COUNT + 1e-05)
     rows = jnp.concatenate([mean, inv_std, gain[...], shift[...]], axis=0)
     vectors[...] = rows
     pick = one_hot(source)
-    chosen, rest = jnp.zeros((4, HALF), F32), rows
+    some, rest = jnp.zeros((4, HALF), F32), rows
     for _ in range(3):
         part = rest.astype(BF16)
-        chosen += jnp.dot(part, pick, preferred_element_type=F32)
+        some += jnp.dot(part, pick, preferred_element_type=F32)
         rest = rest - part.astype(F32)
+    chosen[...] = some
+    act[...] = activated(jnp.dot(inputs[...], pick, preferred_element_type=F32), some).astype(BF16)
+
+
+def terms_kernel(place, chosen, act_own, source, mate, cot, outer, terms):
     low = place[0] == 0
-    both = jnp.concatenate([inputs[...], mate[L : 2 * L]], axis=0)
-    v = normalised(jnp.dot(both, pick, preferred_element_type=F32), chosen)
-    v = chosen[2:3] * v + chosen[3:4]
-    act = (v * half_gate(v)).astype(BF16)
+    near = jnp.dot(mate[L : 2 * L], one_hot(source), preferred_element_type=F32)
+    act = jnp.concatenate([act_own[...], activated(near, chosen[...]).astype(BF16)], axis=0)
     own, next_own, last_own = cot[...], mate[:L], outer[...]
     beyond = mate[2 * L :]
     cots = (
@@ -251,28 +254,26 @@
     return v * half_gate(v)
 
 
-def acts_kernel(vectors, inputs, mate_h, channel, acts, mate, sems):
+def acts_kernel(place, vectors, inputs, mate_h, outer, channel, acts, mate, sems):
     copies = fetch([mate_h.at[L : 2 * L]], [mate], sems)
     rows = vectors[...]
     pick = one_hot(channel)
+    low = place[0] == 0
     here = activated(inputs[...], rows).astype(BF16)
-    acts[0] = jnp.dot(here, pick, preferred_element_type=F32).astype(BF16)
+    away = jnp.where(place[1] == 1, activated(outer[...], rows), 0.0).astype(BF16)
     copies[0].wait()
     near = activated(mate[...], rows).astype(BF16)
-    acts[1] = jnp.dot(near, pick, preferred_element_type=F32).astype(BF16)
-
-
-def forward_kernel(place, vectors, acts, inputs, outer, channel, kc, ko, output, kern, sems):
+    for tap, a in enumerate((jnp.where(low, away, near), here, jnp.where(low, near, away))):
+        acts[tap] = jnp.dot(a, pick, preferred_element_type=F32).astype(BF16)
+
+
+def forward_kernel(acts, inputs, kc, ko, output, kern, sems):
     copies = fetch([kc, ko], [kern.at[:NZ], kern.at[NZ:]], sems)
-    low = place[0] == 0
-    away = jnp.where(place[1] == 1, activated(outer[...], vectors[...]), 0.0).astype(BF16)
-    away = jnp.dot(away, one_hot(channel), preferred_element_type=F32).astype(BF16)
-    near = acts[1]
     total = inputs[...].astype(F32)
     for copy in copies:
         copy.wait()
-    for tap, a in enumerate((jnp.where(low, away, near), acts[0], jnp.where(low, near, away))):
-        total += jnp.dot(a, by_tap(kern, tap), preferred_element_type=F32)
+    for tap in range(3):
+        total += jnp.dot(acts[tap], by_tap(kern, tap), preferred_element_type=F32)
     output[...] = total.astype(BF16)
 
 
@@ -320,9 +321,13 @@
     mate = lax.ppermute(jnp.concatenate([held_cot, held_in, outer], axis=0), "c", swap_c)
     stats = exchange(stats, ("x",) + Y)
 
-    terms, vectors = call(
-        terms_kernel, (shape(HALF, 3 * C, kind=BF16), shape(4, C)), "terms", 24, "svvvvvvvv", flops=2 * 512 * HALF * C * 4, size=6 << 20,
-    )(place, stats, gain, shift, source, inputs, mate, cotangent, outer)
+    vectors, chosen, act_own = call(
+        prepare_kernel, (shape(4, C), shape(4, HALF), shape(L, HALF, kind=BF16)), "prepare", 24,
+    )(stats, gain, shift, source, inputs)
+    terms = call(
+        terms_kernel, shape(HALF, 3 * C, kind=BF16), "terms", 24, "svvvvvv",
+        flops=2 * 512 * HALF * C * 4, size=6 << 20,
+    )(place, chosen, act_own, source, mate, cotangent, outer)
     terms = exchange(terms.reshape(NX * NYB, HALF // (NX * NYB), 3 * C), ("x", "yb"))
 
     kernel_o = lax.ppermute(kernel_c, "c", swap_c)
@@ -341,25 +346,25 @@
     message = call(
         first_kernel, shape(NYA * NYH, 256, 128, kind=BF16), "first", 12, scratch=[held]
     )(terms, totals)
+    message, late_in = lax.optimization_barrier((message, inputs))
+    outer_in = lax.ppermute(late_in, SEQ, swap_out)
     got = exchange(message, ("ya", "yh"))
     message = call(
         second_kernel, shape(NZ, MSG, 128, kind=BF16), "second", 12,
         scratch=[held, pltpu.VMEM((NZ, MSG, 128), F32)],
     )(got)
-    message, late_in = lax.optimization_barrier((message, inputs))
-    outer_in = lax.ppermute(late_in, SEQ, swap_out)
     got = exchange(message, "z")
     acts = call(
-        acts_kernel, shape(2, L, C, kind=BF16), "acts", 56, "vvav", flops=2 * L * C * C * 2, size=2 << 20,
+        acts_kernel, shape(3, L, C, kind=BF16), "acts", 56, "svvavv", flops=2 * L * C * C * 3, size=2 << 20,
         scratch=[pltpu.VMEM((L, C), BF16), pltpu.SemaphoreType.DMA((1,))],
-    )(vectors, inputs, mate, channel)
+    )(place, vectors, inputs, mate, outer_in, channel)
     got, acts = lax.optimization_barrier((got, acts))
     message = call(third_kernel, shape(NX * NYL, MSG, 128, kind=BF16), "third", 12, scratch=[held])(got)
     got = exchange(message, DP)
     output = call(
-        forward_kernel, shape(L, C, kind=BF16), "forward", 56, "svvvvvaa", flops=2 * L * C * C * 4, size=6 << 20,
+        forward_kernel, shape(L, C, kind=BF16), "forward", 56, "vvaa", flops=2 * L * C * C * 3, size=6 << 20,
         scratch=[kern, pltpu.SemaphoreType.DMA((2,))],
-    )(place, vectors, acts, inputs, outer_in, channel, kernel_c, kernel_o)
+    )(acts, inputs, kernel_c, kernel_o)
     got, output = lax.optimization_barrier((got, output))
     grad_in, weights, gain_grad, shift_grad = call(
         last_kernel,

time: 153 us -> 152 us (level)
  the two profiles are of different devices: /device:TPU:1 before, /device:TPU:40 now
where the time goes in v6:
time: 152 us; the launch traced here: 151 us
  starting transfers between devices  48.5 us (32%)
  waiting for transfers between devices  39.3 us (26%)
  Pallas kernels  25.2 us (17%)
  blocking collectives  14.3 us (9%)
  between operations  14.3 us (9%)
  local copies, waits for them, and re-layouts  4.8 us (3%)
  other arithmetic  4.72 us (3%)
    all_to_all x5, starting transfers between devices, exchange(): return lax.all_to_all(value, axes, 0, 0, tiled=True)  29.1 us
    all_to_all x5, waiting for transfers between devices, exchange(): return lax.all_to_all(value, axes, 0, 0, tiled=True)  20.1 us
    all_to_all x1, blocking collectives, exchange(): return lax.all_to_all(value, axes, 0, 0, tiled=True)  11.7 us
    ppermute x1, waiting for transfers between devices, body(): outer_in = lax.ppermute(late_in, SEQ, swap_out)  10.4 us
    ppermute x1, starting transfers between devices, body(): outer = lax.ppermute(held_cot, SEQ, swap_out)  10.1 us
    pallas_call x1, Pallas kernels, body(): call(back_kernel, (shape(L, C), shape(2, C)), 'back', 56, 'svaaaaaav', fl...  6.96 us
    ppermute x1, waiting for transfers between devices, body(): other = lax.ppermute(own, Y, swap_y)  5.59 us
    pallas_call x1, Pallas kernels, body(): call(forward_kernel, shape(L, C, kind=BF16), 'forward', 56, 'vvaa', flops...  5.33 us
  transfers between devices with their start and end apart: 11, of which 7 were waited for; matrix products, arithmetic and copies ran while one was open for 2% of the time, Pallas kernels for 14%

profile of v6, /device:TPU:40, one launch (start us, length us, event | category | flops | bytes accessed | tf_op | source)
XLA Modules:
  0.0 151.2 jit_solution(10483468235093334017)
XLA Ops:
  7.2 0.0 all-gather.3.cloned.1.call-start
  7.2 3.0 %collective-permute-start = (bf16[3,24,768]{2,1,0:T(8,128)(2,1)}, bf16[3,24,768]{2,1,0:T(8,128)(2,1)S(1)}, u32[]{:S(2)}, u32[]{:S(2)}) collective-permute-start(bf16[3,24,768]{2,1,0:T(8,128)(2,1)} %bitcast.28), channel_id=1, source_target_pairs={{0,112},{16,96},{32,80},{48,64},{64,48},{80,32},{96,16},{112,0},{1... | collective-permute-start | bytes 331784 | tf_op jit(solution)/shard_map/ppermute | solution.py:311
  10.2 0.0 copy-start
  10.3 1.0 copy-done
  11.2 0.4 stats.1
  11.6 5.6 %collective-permute-done = bf16[3,24,768]{2,1,0:T(8,128)(2,1)S(1)} collective-permute-done((bf16[3,24,768]{2,1,0:T(8,128)(2,1)}, bf16[3,24,768]{2,1,0:T(8,128)(2,1)S(1)}, u32[]{:S(2)}, u32[]{:S(2)}) %collective-permute-start) | collective-permute-done | bytes 110624 | tf_op jit(solution)/shard_map/ppermute | solution.py:311
  17.2 1.6 %pad_maximum_fusion.1 = bf16[3,48,768]{2,1,0:T(8,128)(2,1)} fusion(bf16[3,24,768]{2,1,0:T(8,128)(2,1)S(1)} %collective-permute-done, bf16[3,24,768]{2,1,0:T(8,128)(2,1)} %bitcast.29), kind=kLoop, calls=%fused_computation.1 | loop fusion | flops 442368 | bytes 442368 | tf_op jit(solution)/shard_map/concatenate | solution.py:317
  18.8 0.0 copy-start.14
  18.8 0.0 all-gather.3.cloned.1.call-update
  18.9 10.1 %collective-permute-start.1 = (bf16[256,768]{1,0:T(8,128)(2,1)}, bf16[256,768]{1,0:T(8,128)(2,1)S(1)}, u32[]{:S(2)}, u32[]{:S(2)}) collective-permute-start(bf16[256,768]{1,0:T(8,128)(2,1)} %bitcast.18), channel_id=1, source_target_pairs={{1,2},{2,1},{3,4},{4,3},{5,6},{6,5},{7,8},{8,7},{9,10},{10,9},{11,... | collective-permute-start | bytes 1179656 | tf_op jit(solution)/shard_map/ppermute | solution.py:316
  28.9 11.7 %all_to_all.30.parts = f32[16,2,768]{2,1,0:T(2,128)S(1)} all-to-all(f32[16,2,768]{2,1,0:T(2,128)S(1)} %stats.1), channel_id=1, replica_groups=mesh['x'=4,'ya'=2,'yb'=2,'yh'=2,'z'=8,'c'=2] {'z','c'}, dimensions={0} | all-to-all | bytes 196608 | tf_op jit(solution)/shard_map/all_to_all | solution.py:285
  40.6 0.0 collective-permute-done.1.outer.outer_h
  40.6 2.4 %pad_maximum_fusion = bf16[768,768]{1,0:T(8,128)(2,1)} fusion(bf16[256,768]{1,0:T(8,128)(2,1)S(1)} %collective-permute-done.1.outer.outer_h, bf16[256,768]{1,0:T(8,128)(2,1)} %bitcast.10, bf16[256,768]{1,0:T(8,128)(2,1)} %bitcast.19), kind=kLoop, calls=%fused_computation | loop fusion | flops 3538944 | bytes 2359296 | tf_op jit(solution)/shard_map/concatenate | solution.py:321
  43.0 2.5 %collective-permute-start.2 = (bf16[768,768]{1,0:T(8,128)(2,1)}, bf16[768,768]{1,0:T(8,128)(2,1)S(1)}, u32[]{:S(2)}, u32[]{:S(2)}) collective-permute-start(bf16[768,768]{1,0:T(8,128)(2,1)} %pad_maximum_fusion), channel_id=1, source_target_pairs={{0,1},{1,0},{2,3},{3,2},{4,5},{5,4},{6,7},{7,6},{8,9},{9,8},{10,11... | collective-permute-start | bytes 3538952 | tf_op jit(solution)/shard_map/ppermute | solution.py:321
  45.5 0.8 merge.1
  46.3 10.2 %all-to-all-start.1 = ((f32[32,2,768]{2,1,0:T(2,128)}), f32[32,2,768]{2,1,0:T(2,128)S(1)}, u32[]{:S(2)}, u32[]{:S(2)}) async-start(f32[32,2,768]{2,1,0:T(2,128)} %merge.1), calls=%async_computation.1 | async-start | bytes 393216 | tf_op jit(solution)/shard_map/all_to_all | solution.py:285
  56.5 0.0 copy-done.14
  56.5 0.0 copy-done.15
  56.5 0.1 pad_add_fusion.place
  56.6 8.2 %all-to-all-done.1.parts = f32[32,2,768]{2,1,0:T(2,128)S(1)} async-done(((f32[32,2,768]{2,1,0:T(2,128)}), f32[32,2,768]{2,1,0:T(2,128)S(1)}, u32[]{:S(2)}, u32[]{:S(2)}) %all-to-all-start.1) | async-done | bytes 196640 | tf_op jit(solution)/shard_map/all_to_all | solution.py:285
  64.8 0.0 copy-done.1
  64.8 0.9 prepare.1
  65.7 0.0 copy-start.10
  65.7 0.6 copy-done.10
  66.3 0.0 collective-permute-done.2.mate.mate_h
  66.3 0.0 copy-done.7
  66.3 0.0 copy-done.4
  66.3 2.0 %terms.1 = bf16[384,2304]{1,0:T(8,128)(2,1)S(1)} custom-call(s32[2]{0:T(128)S(1)} %pad_add_fusion.place, f32[4,384]{1,0:T(4,128)S(1)} %get-tuple-element.30.chosen, bf16[256,384]{1,0:T(8,128)(2,1)S(1)} %get-tuple-element.31.act_own, s32[1,384]{1,0:T(1,128)S(1)} %fusion.13.source, bf16[768,768]{1,0:T(8,128)(2,1)S(1)} %collective-permute-done.2.mate.mate_h, ...), custom_call_target="tpu_custom_call" | custom-call | flops 1207959552 | bytes 6291456 | tf_op jit(solution)/shard_map/terms/pallas_call | solution.py:327
  68.3 0.0 copy-done.12
  68.3 0.0 copy-done.8
  68.3 0.0 copy-start.6
  68.3 1.2 copy-done.6
  69.5 4.1 %all-to-all-start.2 = ((bf16[8,48,2304]{2,1,0:T(8,128)(2,1)}), bf16[8,48,2304]{2,1,0:T(8,128)(2,1)S(1)}, u32[]{:S(2)}, u32[]{:S(2)}) async-start(bf16[8,48,2304]{2,1,0:T(8,128)(2,1)} %bitcast.23), calls=%async_computation.2 | async-start | bytes 3538944 | tf_op jit(solution)/shard_map/all_to_all | solution.py:285
  73.6 1.9 %collective-permute-start.3 = (bf16[8,3,48,768]{3,2,1,0:T(8,128)(2,1)}, bf16[8,3,48,768]{3,2,1,0:T(8,128)(2,1)S(1)}, u32[]{:S(2)}, u32[]{:S(2)}) collective-permute-start(bf16[8,3,48,768]{3,2,1,0:T(8,128)(2,1)} %bitcast.24), channel_id=1, source_target_pairs={{0,1},{1,0},{2,3},{3,2},{4,5},{5,4},{6,7},{7,6},{8,9},{9,8},{10,11... | collective-permute-start | bytes 5308424 | tf_op jit(solution)/shard_map/ppermute | solution.py:333
  75.5 0.6 fusion.channel
  76.2 3.2 %collective-permute-done.3.ko = bf16[8,3,48,768]{3,2,1,0:T(8,128)(2,1)S(1)} collective-permute-done((bf16[8,3,48,768]{3,2,1,0:T(8,128)(2,1)}, bf16[8,3,48,768]{3,2,1,0:T(8,128)(2,1)S(1)}, u32[]{:S(2)}, u32[]{:S(2)}) %collective-permute-start.3) | collective-permute-done | bytes 1769504 | tf_op jit(solution)/shard_map/ppermute | solution.py:333
  79.4 1.2 copy-done.13
  80.6 7.0 %back.1 = (f32[256,768]{1,0:T(8,128)}, f32[2,768]{1,0:T(2,128)}) custom-call(s32[2]{0:T(128)} %copy-done.12, f32[4,768]{1,0:T(4,128)} %copy-done.10, bf16[256,768]{1,0:T(8,128)(2,1)} %bitcast.11, bf16[768,768]{1,0:T(8,128)(2,1)} %copy-done.8, bf16[256,768]{1,0:T(8,128)(2,1)} %bitcast.20, bf16[256,768]{1,0:T(8,128)(2,1)} %copy-done.7, ...), custom_call_target="tpu_custom_call" | custom-call | flops 1509949440 | bytes 8388608 | tf_op jit(solution)/shard_map/back/pallas_call | solution.py:335
  87.5 0.0 copy-start.2
  87.6 2.6 %psum.7.totals = f32[2,768]{1,0:T(2,128)S(1)} all-reduce(f32[2,768]{1,0:T(2,128)} %get-tuple-element.37), channel_id=1, replica_groups=mesh['x'=4,'ya'=2,'yb'=2,'yh'=2,'z'=8,'c'=2] {'c'}, use_global_device_ids=true, to_apply=%region_0.1 | all-reduce | flops 1536 | bytes 12288 | tf_op jit(solution)/shard_map/psum | solution.py:343
  90.2 5.5 %all-to-all-done.2.got = bf16[8,48,2304]{2,1,0:T(8,128)(2,1)S(1)} async-done(((bf16[8,48,2304]{2,1,0:T(8,128)(2,1)}), bf16[8,48,2304]{2,1,0:T(8,128)(2,1)S(1)}, u32[]{:S(2)}, u32[]{:S(2)}) %all-to-all-start.2) | async-done | bytes 1769504 | tf_op jit(solution)/shard_map/all_to_all | solution.py:285
  95.7 1.0 first.1
  96.7 7.2 %all-to-all-start.3 = ((bf16[4,256,128]{2,1,0:T(8,128)(2,1)}), bf16[4,256,128]{2,1,0:T(8,128)(2,1)S(1)}, u32[]{:S(2)}, u32[]{:S(2)}) async-start(bf16[4,256,128]{2,1,0:T(8,128)(2,1)} %first.1), calls=%async_computation.3 | async-start | bytes 524288 | tf_op jit(solution)/shard_map/all_to_all | solution.py:285
  103.9 0.0 copy-done.2
  103.9 1.9 %collective-permute-start.4 = (bf16[256,768]{1,0:T(8,128)(2,1)S(1)}, bf16[256,768]{1,0:T(8,128)(2,1)S(1)}, u32[]{:S(2)}, u32[]{:S(2)}) collective-permute-start(bf16[256,768]{1,0:T(8,128)(2,1)S(1)} %bitcast.16), channel_id=1, source_target_pairs={{1,2},{2,1},{3,4},{4,3},{5,6},{6,5},{7,8},{8,7},{9,10},{10,9},{11,... | collective-permute-start | bytes 1179656 | tf_op jit(solution)/shard_map/ppermute | solution.py:350
  105.8 3.5 %all-to-all-done.3.got = bf16[4,256,128]{2,1,0:T(8,128)(2,1)S(1)} async-done(((bf16[4,256,128]{2,1,0:T(8,128)(2,1)}), bf16[4,256,128]{2,1,0:T(8,128)(2,1)S(1)}, u32[]{:S(2)}, u32[]{:S(2)}) %all-to-all-start.3) | async-done | bytes 262176 | tf_op jit(solution)/shard_map/all_to_all | solution.py:285
  109.3 0.8 second.1
  110.1 3.8 %all-to-all-start.4 = ((bf16[8,64,128]{2,1,0:T(8,128)(2,1)}), bf16[8,64,128]{2,1,0:T(8,128)(2,1)S(1)}, u32[]{:S(2)}, u32[]{:S(2)}) async-start(bf16[8,64,128]{2,1,0:T(8,128)(2,1)} %second.1), calls=%async_computation.4 | async-start | bytes 262144 | tf_op jit(solution)/shard_map/all_to_all | solution.py:285
  113.9 10.4 %collective-permute-done.4.outer = bf16[256,768]{1,0:T(8,128)(2,1)S(1)} collective-permute-done((bf16[256,768]{1,0:T(8,128)(2,1)S(1)}, bf16[256,768]{1,0:T(8,128)(2,1)S(1)}, u32[]{:S(2)}, u32[]{:S(2)}) %collective-permute-start.4) | collective-permute-done | bytes 393248 | tf_op jit(solution)/shard_map/ppermute | solution.py:350
  124.2 0.7 copy-done.16
  125.0 4.7 %acts.1 = bf16[3,256,768]{2,1,0:T(8,128)(2,1)} custom-call(s32[2]{0:T(128)} %copy-done.12, f32[4,768]{1,0:T(4,128)} %copy-done.10, bf16[256,768]{1,0:T(8,128)(2,1)} %bitcast.12, bf16[768,768]{1,0:T(8,128)(2,1)} %copy-done.8, bf16[256,768]{1,0:T(8,128)(2,1)} %copy-done.16, s32[1,768]{1,0:T(1,128)} %fusion.channel), custom_call_target="tpu_custom_call" | custom-call | flops 905969664 | bytes 2097152 | tf_op jit(solution)/shard_map/acts/pallas_call | solution.py:357
  129.7 0.0 all-to-all-done.4.got
  129.7 0.8 third.1
  130.5 3.9 %all-to-all-start.5 = ((bf16[16,64,128]{2,1,0:T(8,128)(2,1)}), bf16[16,64,128]{2,1,0:T(8,128)(2,1)S(1)}, u32[]{:S(2)}, u32[]{:S(2)}) async-start(bf16[16,64,128]{2,1,0:T(8,128)(2,1)} %third.1), calls=%async_computation.5 | async-start | bytes 524288 | tf_op jit(solution)/shard_map/all_to_all | solution.py:285
  134.3 0.0 copy-start.5
  134.3 0.0 copy-start.9
  134.4 0.0 copy-start.11
  134.4 5.3 %forward.1 = bf16[256,768]{1,0:T(8,128)(2,1)} custom-call(bf16[3,256,768]{2,1,0:T(8,128)(2,1)} %acts.1, bf16[256,768]{1,0:T(8,128)(2,1)} %bitcast.13, bf16[8,3,48,768]{3,2,1,0:T(8,128)(2,1)} %bitcast.26, bf16[8,3,48,768]{3,2,1,0:T(8,128)(2,1)} %copy-done.13), custom_call_target="tpu_custom_call" | custom-call | flops 905969664 | bytes 6291456 | tf_op jit(solution)/shard_map/forward/pallas_call | solution.py:364
  139.7 3.0 %all-to-all-done.5.got = bf16[16,64,128]{2,1,0:T(8,128)(2,1)S(1)} async-done(((bf16[16,64,128]{2,1,0:T(8,128)(2,1)}), bf16[16,64,128]{2,1,0:T(8,128)(2,1)S(1)}, u32[]{:S(2)}, u32[]{:S(2)}) %all-to-all-start.5) | async-done | bytes 262176 | tf_op jit(solution)/shard_map/all_to_all | solution.py:285
  142.6 0.0 copy-done.3
  142.7 0.0 copy-done.5
  142.7 0.0 copy-done.9
  142.7 0.0 copy-done.11
  142.7 1.6 %last.1 = (bf16[256,768]{1,0:T(8,128)(2,1)}, f32[3,24,768]{2,1,0:T(8,128)}, f32[768]{0:T(1024)}, f32[768]{0:T(1024)}) custom-call(bf16[16,64,128]{2,1,0:T(8,128)(2,1)S(1)} %all-to-all-done.5.got, f32[4,768]{1,0:T(4,128)S(1)} %copy-done.11, bf16[256,768]{1,0:T(8,128)(2,1)S(1)} %bitcast.17, bf16[256,768]{1,0:T(8,128)(2,1)S(1)} %bitcast.22, ...), custom_call_target="tpu_custom_call" | custom-call | bytes 1048576 | tf_op jit(solution)/shard_map/last/pallas_call | solution.py:369
  (13 shorter events, 0.0 us)
Async XLA Ops:
  7.2 66.4 %all-gather.3.cloned.1.call-start = ((), (), s32[]{:S(2)}) async-start(), calls=%async_computation.6 | async-start | bytes 1990656 | tf_op jit(solution)/shard_map/all_gather | solution.py:317
  7.2 10.0 %collective-permute-start = (bf16[3,24,768]{2,1,0:T(8,128)(2,1)}, bf16[3,24,768]{2,1,0:T(8,128)(2,1)S(1)}, u32[]{:S(2)}, u32[]{:S(2)}) collective-permute-start(bf16[3,24,768]{2,1,0:T(8,128)(2,1)} %bitcast.28), channel_id=1, source_target_pairs={{0,112},{16,96},{32,80},{48,64},{64,48},{80,32},{96,16},{112,0},{1... | collective-permute-start | bytes 331784 | tf_op jit(solution)/shard_map/ppermute | solution.py:311
  10.2 1.0 copy-start
  18.8 37.7 %copy-start.14 = (f32[768]{0:T(1024)S(1)}, f32[768]{0:T(1024)}, u32[]{:S(2)}) copy-start(f32[768]{0:T(1024)} %param.6) | copy-start | bytes 9220
  18.8 37.7 %copy-start.15 = (f32[768]{0:T(1024)S(1)}, f32[768]{0:T(1024)}, u32[]{:S(2)}) copy-start(f32[768]{0:T(1024)} %param.7) | copy-start | bytes 9220
  18.8 46.0 %copy-start.1 = (bf16[1,256,768]{2,1,0:T(8,128)(2,1)S(1)}, bf16[1,256,768]{2,1,0:T(8,128)(2,1)}, u32[]{:S(2)}) copy-start(bf16[1,256,768]{2,1,0:T(8,128)(2,1)} %param.5) | copy-start | bytes 1179652
  18.9 21.8 %collective-permute-start.1 = (bf16[256,768]{1,0:T(8,128)(2,1)}, bf16[256,768]{1,0:T(8,128)(2,1)S(1)}, u32[]{:S(2)}, u32[]{:S(2)}) collective-permute-start(bf16[256,768]{1,0:T(8,128)(2,1)} %bitcast.18), channel_id=1, source_target_pairs={{1,2},{2,1},{3,4},{4,3},{5,6},{6,5},{7,8},{8,7},{9,10},{10,9},{11,... | collective-permute-start | bytes 1179656 | tf_op jit(solution)/shard_map/ppermute | solution.py:316
  40.6 25.7 %copy-start.4 = (bf16[1,256,768]{2,1,0:T(8,128)(2,1)S(1)}, bf16[1,256,768]{2,1,0:T(8,128)(2,1)}, u32[]{:S(2)}) copy-start(bf16[1,256,768]{2,1,0:T(8,128)(2,1)} %param.9) | copy-start | bytes 1179652
  40.6 25.7 %copy-start.7 = (bf16[256,768]{1,0:T(8,128)(2,1)}, bf16[256,768]{1,0:T(8,128)(2,1)S(1)}, u32[]{:S(2)}) copy-start(bf16[256,768]{1,0:T(8,128)(2,1)S(1)} %collective-permute-done.1.outer.outer_h) | copy-start | bytes 1179652
  43.0 23.3 %collective-permute-start.2 = (bf16[768,768]{1,0:T(8,128)(2,1)}, bf16[768,768]{1,0:T(8,128)(2,1)S(1)}, u32[]{:S(2)}, u32[]{:S(2)}) collective-permute-start(bf16[768,768]{1,0:T(8,128)(2,1)} %pad_maximum_fusion), channel_id=1, source_target_pairs={{0,1},{1,0},{2,3},{3,2},{4,5},{5,4},{6,7},{7,6},{8,9},{9,8},{10,11... | collective-permute-start | bytes 3538952 | tf_op jit(solution)/shard_map/ppermute | solution.py:321
  46.3 18.5 %all-to-all-start.1 = ((f32[32,2,768]{2,1,0:T(2,128)}), f32[32,2,768]{2,1,0:T(2,128)S(1)}, u32[]{:S(2)}, u32[]{:S(2)}) async-start(f32[32,2,768]{2,1,0:T(2,128)} %merge.1), calls=%async_computation.1 | async-start | bytes 393216 | tf_op jit(solution)/shard_map/all_to_all | solution.py:285
  56.6 11.7 %copy-start.12 = (s32[2]{0:T(128)}, s32[2]{0:T(128)S(1)}, u32[]{:S(2)}) copy-start(s32[2]{0:T(128)S(1)} %pad_add_fusion.place) | copy-start | bytes 28
  65.7 0.6 copy-start.10
  66.3 2.0 %copy-start.8 = (bf16[768,768]{1,0:T(8,128)(2,1)}, bf16[768,768]{1,0:T(8,128)(2,1)S(1)}, u32[]{:S(2)}) copy-start(bf16[768,768]{1,0:T(8,128)(2,1)S(1)} %collective-permute-done.2.mate.mate_h) | copy-start | bytes 3538948
  68.3 1.2 copy-start.6
  69.5 26.2 %all-to-all-start.2 = ((bf16[8,48,2304]{2,1,0:T(8,128)(2,1)}), bf16[8,48,2304]{2,1,0:T(8,128)(2,1)S(1)}, u32[]{:S(2)}, u32[]{:S(2)}) async-start(bf16[8,48,2304]{2,1,0:T(8,128)(2,1)} %bitcast.23), calls=%async_computation.2 | async-start | bytes 3538944 | tf_op jit(solution)/shard_map/all_to_all | solution.py:285
  73.6 5.8 %collective-permute-start.3 = (bf16[8,3,48,768]{3,2,1,0:T(8,128)(2,1)}, bf16[8,3,48,768]{3,2,1,0:T(8,128)(2,1)S(1)}, u32[]{:S(2)}, u32[]{:S(2)}) collective-permute-start(bf16[8,3,48,768]{3,2,1,0:T(8,128)(2,1)} %bitcast.24), channel_id=1, source_target_pairs={{0,1},{1,0},{2,3},{3,2},{4,5},{5,4},{6,7},{7,6},{8,9},{9,8},{10,11... | collective-permute-start | bytes 5308424 | tf_op jit(solution)/shard_map/ppermute | solution.py:333
  79.4 1.2 copy-start.13
  87.5 16.4 %copy-start.2 = (bf16[1,256,768]{2,1,0:T(8,128)(2,1)S(1)}, bf16[1,256,768]{2,1,0:T(8,128)(2,1)}, u32[]{:S(2)}) copy-start(bf16[1,256,768]{2,1,0:T(8,128)(2,1)} %param.5) | copy-start | bytes 1179652
  96.7 12.6 %all-to-all-start.3 = ((bf16[4,256,128]{2,1,0:T(8,128)(2,1)}), bf16[4,256,128]{2,1,0:T(8,128)(2,1)S(1)}, u32[]{:S(2)}, u32[]{:S(2)}) async-start(bf16[4,256,128]{2,1,0:T(8,128)(2,1)} %first.1), calls=%async_computation.3 | async-start | bytes 524288 | tf_op jit(solution)/shard_map/all_to_all | solution.py:285
  103.9 20.3 %collective-permute-start.4 = (bf16[256,768]{1,0:T(8,128)(2,1)S(1)}, bf16[256,768]{1,0:T(8,128)(2,1)S(1)}, u32[]{:S(2)}, u32[]{:S(2)}) collective-permute-start(bf16[256,768]{1,0:T(8,128)(2,1)S(1)} %bitcast.16), channel_id=1, source_target_pairs={{1,2},{2,1},{3,4},{4,3},{5,6},{6,5},{7,8},{8,7},{9,10},{10,9},{11,... | collective-permute-start | bytes 1179656 | tf_op jit(solution)/shard_map/ppermute | solution.py:350
  110.1 19.6 %all-to-all-start.4 = ((bf16[8,64,128]{2,1,0:T(8,128)(2,1)}), bf16[8,64,128]{2,1,0:T(8,128)(2,1)S(1)}, u32[]{:S(2)}, u32[]{:S(2)}) async-start(bf16[8,64,128]{2,1,0:T(8,128)(2,1)} %second.1), calls=%async_computation.4 | async-start | bytes 262144 | tf_op jit(solution)/shard_map/all_to_all | solution.py:285
  124.2 0.7 copy-start.16
  130.5 12.2 %all-to-all-start.5 = ((bf16[16,64,128]{2,1,0:T(8,128)(2,1)}), bf16[16,64,128]{2,1,0:T(8,128)(2,1)S(1)}, u32[]{:S(2)}, u32[]{:S(2)}) async-start(bf16[16,64,128]{2,1,0:T(8,128)(2,1)} %third.1), calls=%async_computation.5 | async-start | bytes 524288 | tf_op jit(solution)/shard_map/all_to_all | solution.py:285
  134.3 8.3 %copy-start.3 = (bf16[1,256,768]{2,1,0:T(8,128)(2,1)S(1)}, bf16[1,256,768]{2,1,0:T(8,128)(2,1)}, u32[]{:S(2)}) copy-start(bf16[1,256,768]{2,1,0:T(8,128)(2,1)} %param.5) | copy-start | bytes 1179652
  134.3 8.3 %copy-start.5 = (bf16[1,256,768]{2,1,0:T(8,128)(2,1)S(1)}, bf16[1,256,768]{2,1,0:T(8,128)(2,1)}, u32[]{:S(2)}) copy-start(bf16[1,256,768]{2,1,0:T(8,128)(2,1)} %param.9) | copy-start | bytes 1179652
  134.3 8.3 %copy-start.9 = (f32[256,768]{1,0:T(8,128)S(1)}, f32[256,768]{1,0:T(8,128)}, u32[]{:S(2)}) copy-start(f32[256,768]{1,0:T(8,128)} %get-tuple-element.44.pre_h) | copy-start | bytes 2359300
  134.4 8.3 %copy-start.11 = (f32[4,768]{1,0:T(4,128)S(1)}, f32[4,768]{1,0:T(4,128)}, u32[]{:S(2)}) copy-start(f32[4,768]{1,0:T(4,128)} %copy-done.10) | copy-start | bytes 36868
Sparse Core Ops, SparseCore 0:
  19.0 48.4 all-gather.2

commit v7 on v6

--- a/solution.py
+++ b/solution.py
@@ -355,7 +355,7 @@
     )(got)
     got = exchange(message, "z")
     acts = call(
-        acts_kernel, shape(3, L, C, kind=BF16), "acts", 56, "svvavv", flops=2 * L * C * C * 3, size=2 << 20,
+        acts_kernel, shape(3, L, C, kind=BF16), "acts", 24, "svvavv", flops=2 * L * C * C * 3, size=2 << 20,
         scratch=[pltpu.VMEM((L, C), BF16), pltpu.SemaphoreType.DMA((1,))],
     )(place, vectors, inputs, mate, outer_in, channel)
     got, acts = lax.optimization_barrier((got, acts))

time: 152 us -> 151 us (level)
  Pallas kernels: 25.2 us -> 23.1 us
    unnamed x34 -> x42, local copies, waits for them, and re-layouts: 4.79 us -> 5.77 us
where the time goes in v7:
time: 151 us
  starting transfers between devices  49.1 us (33%)
  waiting for transfers between devices  39.2 us (26%)
  Pallas kernels  23.1 us (15%)
  blocking collectives  14.3 us (9%)
  between operations  14.3 us (9%)
  local copies, waits for them, and re-layouts  5.78 us (4%)
  other arithmetic  4.74 us (3%)
    all_to_all x5, starting transfers between devices, exchange(): return lax.all_to_all(value, axes, 0, 0, tiled=True)  29.7 us
    all_to_all x5, waiting for transfers between devices, exchange(): return lax.all_to_all(value, axes, 0, 0, tiled=True)  20 us
    all_to_all x1, blocking collectives, exchange(): return lax.all_to_all(value, axes, 0, 0, tiled=True)  11.7 us
    ppermute x1, waiting for transfers between devices, body(): outer_in = lax.ppermute(late_in, SEQ, swap_out)  10.4 us
    ppermute x1, starting transfers between devices, body(): outer = lax.ppermute(held_cot, SEQ, swap_out)  10.1 us
    pallas_call x1, Pallas kernels, body(): call(back_kernel, (shape(L, C), shape(2, C)), 'back', 56, 'svaaaaaav', fl...  6.96 us
    unnamed x42, local copies, waits for them, and re-layouts  5.77 us
    ppermute x1, waiting for transfers between devices, body(): other = lax.ppermute(own, Y, swap_y)  5.59 us
  transfers between devices with their start and end apart: 11, of which 7 were waited for; matrix products, arithmetic and copies ran while one was open for 2% of the time, Pallas kernels for 14%

profile of v7, /device:TPU:40, one launch (start us, length us, event | category | flops | bytes accessed | tf_op | source)
XLA Modules:
  0.0 150.7 jit_solution(11217331146548854368)
XLA Ops:
  7.2 0.0 all-gather.3.cloned.1.call-start
  7.2 3.0 %collective-permute-start = (bf16[3,24,768]{2,1,0:T(8,128)(2,1)}, bf16[3,24,768]{2,1,0:T(8,128)(2,1)S(1)}, u32[]{:S(2)}, u32[]{:S(2)}) collective-permute-start(bf16[3,24,768]{2,1,0:T(8,128)(2,1)} %bitcast.28), channel_id=1, source_target_pairs={{0,112},{16,96},{32,80},{48,64},{64,48},{80,32},{96,16},{112,0},{1... | collective-permute-start | bytes 331784 | tf_op jit(solution)/shard_map/ppermute | solution.py:311
  10.2 0.0 copy-start
  10.3 1.0 copy-done
  11.2 0.4 stats.1
  11.6 5.6 %collective-permute-done = bf16[3,24,768]{2,1,0:T(8,128)(2,1)S(1)} collective-permute-done((bf16[3,24,768]{2,1,0:T(8,128)(2,1)}, bf16[3,24,768]{2,1,0:T(8,128)(2,1)S(1)}, u32[]{:S(2)}, u32[]{:S(2)}) %collective-permute-start) | collective-permute-done | bytes 110624 | tf_op jit(solution)/shard_map/ppermute | solution.py:311
  17.2 1.6 %pad_maximum_fusion.1 = bf16[3,48,768]{2,1,0:T(8,128)(2,1)} fusion(bf16[3,24,768]{2,1,0:T(8,128)(2,1)S(1)} %collective-permute-done, bf16[3,24,768]{2,1,0:T(8,128)(2,1)} %bitcast.29), kind=kLoop, calls=%fused_computation.1 | loop fusion | flops 442368 | bytes 442368 | tf_op jit(solution)/shard_map/concatenate | solution.py:317
  18.8 0.0 all-gather.3.cloned.1.call-update
  18.9 10.1 %collective-permute-start.1 = (bf16[256,768]{1,0:T(8,128)(2,1)}, bf16[256,768]{1,0:T(8,128)(2,1)S(1)}, u32[]{:S(2)}, u32[]{:S(2)}) collective-permute-start(bf16[256,768]{1,0:T(8,128)(2,1)} %bitcast.18), channel_id=1, source_target_pairs={{1,2},{2,1},{3,4},{4,3},{5,6},{6,5},{7,8},{8,7},{9,10},{10,9},{11,... | collective-permute-start | bytes 1179656 | tf_op jit(solution)/shard_map/ppermute | solution.py:316
  28.9 11.7 %all_to_all.30.parts = f32[16,2,768]{2,1,0:T(2,128)S(1)} all-to-all(f32[16,2,768]{2,1,0:T(2,128)S(1)} %stats.1), channel_id=1, replica_groups=mesh['x'=4,'ya'=2,'yb'=2,'yh'=2,'z'=8,'c'=2] {'z','c'}, dimensions={0} | all-to-all | bytes 196608 | tf_op jit(solution)/shard_map/all_to_all | solution.py:285
  40.6 0.0 collective-permute-done.1.outer.outer_h
  40.6 2.4 %pad_maximum_fusion = bf16[768,768]{1,0:T(8,128)(2,1)} fusion(bf16[256,768]{1,0:T(8,128)(2,1)S(1)} %collective-permute-done.1.outer.outer_h, bf16[256,768]{1,0:T(8,128)(2,1)} %bitcast.10, bf16[256,768]{1,0:T(8,128)(2,1)} %bitcast.19), kind=kLoop, calls=%fused_computation | loop fusion | flops 3538944 | bytes 2359296 | tf_op jit(solution)/shard_map/concatenate | solution.py:321
  43.0 2.5 %collective-permute-start.2 = (bf16[768,768]{1,0:T(8,128)(2,1)}, bf16[768,768]{1,0:T(8,128)(2,1)S(1)}, u32[]{:S(2)}, u32[]{:S(2)}) collective-permute-start(bf16[768,768]{1,0:T(8,128)(2,1)} %pad_maximum_fusion), channel_id=1, source_target_pairs={{0,1},{1,0},{2,3},{3,2},{4,5},{5,4},{6,7},{7,6},{8,9},{9,8},{10,11... | collective-permute-start | bytes 3538952 | tf_op jit(solution)/shard_map/ppermute | solution.py:321
  45.5 0.8 merge.1
  46.3 10.2 %all-to-all-start.1 = ((f32[32,2,768]{2,1,0:T(2,128)}), f32[32,2,768]{2,1,0:T(2,128)S(1)}, u32[]{:S(2)}, u32[]{:S(2)}) async-start(f32[32,2,768]{2,1,0:T(2,128)} %merge.1), calls=%async_computation.1 | async-start | bytes 393216 | tf_op jit(solution)/shard_map/all_to_all | solution.py:285
  56.5 0.0 copy-done.19
  56.5 0.0 copy-done.20
  56.5 0.1 pad_add_fusion.place
  56.6 8.2 %all-to-all-done.1.parts = f32[32,2,768]{2,1,0:T(2,128)S(1)} async-done(((f32[32,2,768]{2,1,0:T(2,128)}), f32[32,2,768]{2,1,0:T(2,128)S(1)}, u32[]{:S(2)}, u32[]{:S(2)}) %all-to-all-start.1) | async-done | bytes 196640 | tf_op jit(solution)/shard_map/all_to_all | solution.py:285
  64.8 0.0 copy-done.1
  64.8 0.9 prepare.1
  65.7 0.0 copy-start.13
  65.7 0.6 copy-done.13
  66.3 0.0 collective-permute-done.2.mate.mate_h
  66.3 0.0 copy-done.7
  66.3 0.0 copy-done.4
  66.3 2.0 %terms.1 = bf16[384,2304]{1,0:T(8,128)(2,1)S(1)} custom-call(s32[2]{0:T(128)S(1)} %pad_add_fusion.place, f32[4,384]{1,0:T(4,128)S(1)} %get-tuple-element.30.chosen, bf16[256,384]{1,0:T(8,128)(2,1)S(1)} %get-tuple-element.31.act_own, s32[1,384]{1,0:T(1,128)S(1)} %fusion.13.source, bf16[768,768]{1,0:T(8,128)(2,1)S(1)} %collective-permute-done.2.mate.mate_h, ...), custom_call_target="tpu_custom_call" | custom-call | flops 1207959552 | bytes 6291456 | tf_op jit(solution)/shard_map/terms/pallas_call | solution.py:327
  68.3 0.0 copy-done.16
  68.3 0.0 copy-done.8
  68.3 0.0 copy-start.6
  68.3 1.2 copy-done.6
  69.5 4.1 %all-to-all-start.2 = ((bf16[8,48,2304]{2,1,0:T(8,128)(2,1)}), bf16[8,48,2304]{2,1,0:T(8,128)(2,1)S(1)}, u32[]{:S(2)}, u32[]{:S(2)}) async-start(bf16[8,48,2304]{2,1,0:T(8,128)(2,1)} %bitcast.23), calls=%async_computation.2 | async-start | bytes 3538944 | tf_op jit(solution)/shard_map/all_to_all | solution.py:285
  73.6 1.9 %collective-permute-start.3 = (bf16[8,3,48,768]{3,2,1,0:T(8,128)(2,1)}, bf16[8,3,48,768]{3,2,1,0:T(8,128)(2,1)S(1)}, u32[]{:S(2)}, u32[]{:S(2)}) collective-permute-start(bf16[8,3,48,768]{3,2,1,0:T(8,128)(2,1)} %bitcast.24), channel_id=1, source_target_pairs={{0,1},{1,0},{2,3},{3,2},{4,5},{5,4},{6,7},{7,6},{8,9},{9,8},{10,11... | collective-permute-start | bytes 5308424 | tf_op jit(solution)/shard_map/ppermute | solution.py:333
  75.5 0.6 fusion.channel
  76.2 3.2 %collective-permute-done.3.ko = bf16[8,3,48,768]{3,2,1,0:T(8,128)(2,1)S(1)} collective-permute-done((bf16[8,3,48,768]{3,2,1,0:T(8,128)(2,1)}, bf16[8,3,48,768]{3,2,1,0:T(8,128)(2,1)S(1)}, u32[]{:S(2)}, u32[]{:S(2)}) %collective-permute-start.3) | collective-permute-done | bytes 1769504 | tf_op jit(solution)/shard_map/ppermute | solution.py:333
  79.4 1.2 copy-done.18
  80.6 7.0 %back.1 = (f32[256,768]{1,0:T(8,128)}, f32[2,768]{1,0:T(2,128)}) custom-call(s32[2]{0:T(128)} %copy-done.16, f32[4,768]{1,0:T(4,128)} %copy-done.13, bf16[256,768]{1,0:T(8,128)(2,1)} %bitcast.11, bf16[768,768]{1,0:T(8,128)(2,1)} %copy-done.8, bf16[256,768]{1,0:T(8,128)(2,1)} %bitcast.20, bf16[256,768]{1,0:T(8,128)(2,1)} %copy-done.7, ...), custom_call_target="tpu_custom_call" | custom-call | flops 1509949440 | bytes 8388608 | tf_op jit(solution)/shard_map/back/pallas_call | solution.py:335
  87.6 0.0 copy-start.2
  87.6 0.0 copy-start.9
  87.6 0.0 copy-start.14
  87.6 0.0 copy-start.15
  87.6 0.0 copy-start.17
  87.6 2.6 %psum.7.totals = f32[2,768]{1,0:T(2,128)S(1)} all-reduce(f32[2,768]{1,0:T(2,128)} %get-tuple-element.37), channel_id=1, replica_groups=mesh['x'=4,'ya'=2,'yb'=2,'yh'=2,'z'=8,'c'=2] {'c'}, use_global_device_ids=true, to_apply=%region_0.1 | all-reduce | flops 1536 | bytes 12288 | tf_op jit(solution)/shard_map/psum | solution.py:343
  90.3 5.4 %all-to-all-done.2.got = bf16[8,48,2304]{2,1,0:T(8,128)(2,1)S(1)} async-done(((bf16[8,48,2304]{2,1,0:T(8,128)(2,1)}), bf16[8,48,2304]{2,1,0:T(8,128)(2,1)S(1)}, u32[]{:S(2)}, u32[]{:S(2)}) %all-to-all-start.2) | async-done | bytes 1769504 | tf_op jit(solution)/shard_map/all_to_all | solution.py:285
  95.7 0.3 first.1
  96.0 0.0 copy-start.11
  96.0 0.7 copy-done.11
  96.7 7.2 %all-to-all-start.3 = ((bf16[4,256,128]{2,1,0:T(8,128)(2,1)}), bf16[4,256,128]{2,1,0:T(8,128)(2,1)S(1)}, u32[]{:S(2)}, u32[]{:S(2)}) async-start(bf16[4,256,128]{2,1,0:T(8,128)(2,1)} %copy-done.11), calls=%async_computation.3 | async-start | bytes 524288 | tf_op jit(solution)/shard_map/all_to_all | solution.py:285
  103.9 0.0 copy-done.2
  103.9 1.9 %collective-permute-start.4 = (bf16[256,768]{1,0:T(8,128)(2,1)S(1)}, bf16[256,768]{1,0:T(8,128)(2,1)S(1)}, u32[]{:S(2)}, u32[]{:S(2)}) collective-permute-start(bf16[256,768]{1,0:T(8,128)(2,1)S(1)} %bitcast.15), channel_id=1, source_target_pairs={{1,2},{2,1},{3,4},{4,3},{5,6},{6,5},{7,8},{8,7},{9,10},{10,9},{11,... | collective-permute-start | bytes 1179656 | tf_op jit(solution)/shard_map/ppermute | solution.py:350
  105.9 3.5 %all-to-all-done.3.got = bf16[4,256,128]{2,1,0:T(8,128)(2,1)S(1)} async-done(((bf16[4,256,128]{2,1,0:T(8,128)(2,1)}), bf16[4,256,128]{2,1,0:T(8,128)(2,1)S(1)}, u32[]{:S(2)}, u32[]{:S(2)}) %all-to-all-start.3) | async-done | bytes 262176 | tf_op jit(solution)/shard_map/all_to_all | solution.py:285
  109.3 0.8 second.1
  110.1 3.8 %all-to-all-start.4 = ((bf16[8,64,128]{2,1,0:T(8,128)(2,1)}), bf16[8,64,128]{2,1,0:T(8,128)(2,1)S(1)}, u32[]{:S(2)}, u32[]{:S(2)}) async-start(bf16[8,64,128]{2,1,0:T(8,128)(2,1)} %second.1), calls=%async_computation.4 | async-start | bytes 262144 | tf_op jit(solution)/shard_map/all_to_all | solution.py:285
  113.9 10.4 %collective-permute-done.4.outer = bf16[256,768]{1,0:T(8,128)(2,1)S(1)} collective-permute-done((bf16[256,768]{1,0:T(8,128)(2,1)S(1)}, bf16[256,768]{1,0:T(8,128)(2,1)S(1)}, u32[]{:S(2)}, u32[]{:S(2)}) %collective-permute-start.4) | collective-permute-done | bytes 393248 | tf_op jit(solution)/shard_map/ppermute | solution.py:350
  124.3 3.3 %acts.1 = bf16[3,256,768]{2,1,0:T(8,128)(2,1)S(1)} custom-call(s32[2]{0:T(128)S(1)} %copy-done.17, f32[4,768]{1,0:T(4,128)S(1)} %copy-done.14, bf16[256,768]{1,0:T(8,128)(2,1)S(1)} %bitcast.16, bf16[768,768]{1,0:T(8,128)(2,1)S(1)} %copy-done.9, bf16[256,768]{1,0:T(8,128)(2,1)S(1)} %collective-permute-done.4.outer, s32[1,768]{1,0:T(1,128)S(1)} %copy-done.15), custom_call_target="tpu_custom_call" | custom-call | flops 905969664 | bytes 2097152 | tf_op jit(solution)/shard_map/acts/pallas_call | solution.py:357
  127.6 0.0 copy-start.10
  127.6 1.0 copy-done.10
  128.6 0.0 all-to-all-done.4.got
  128.6 0.8 third.1
  129.4 4.4 %all-to-all-start.5 = ((bf16[16,64,128]{2,1,0:T(8,128)(2,1)}), bf16[16,64,128]{2,1,0:T(8,128)(2,1)S(1)}, u32[]{:S(2)}, u32[]{:S(2)}) async-start(bf16[16,64,128]{2,1,0:T(8,128)(2,1)} %third.1), calls=%async_computation.5 | async-start | bytes 524288 | tf_op jit(solution)/shard_map/all_to_all | solution.py:285
  133.8 0.0 copy-start.5
  133.8 5.3 %forward.1 = bf16[256,768]{1,0:T(8,128)(2,1)} custom-call(bf16[3,256,768]{2,1,0:T(8,128)(2,1)} %copy-done.10, bf16[256,768]{1,0:T(8,128)(2,1)} %bitcast.12, bf16[8,3,48,768]{3,2,1,0:T(8,128)(2,1)} %bitcast.26, bf16[8,3,48,768]{3,2,1,0:T(8,128)(2,1)} %copy-done.18), custom_call_target="tpu_custom_call" | custom-call | flops 905969664 | bytes 6291456 | tf_op jit(solution)/shard_map/forward/pallas_call | solution.py:364
  139.2 3.0 %all-to-all-done.5.got = bf16[16,64,128]{2,1,0:T(8,128)(2,1)S(1)} async-done(((bf16[16,64,128]{2,1,0:T(8,128)(2,1)}), bf16[16,64,128]{2,1,0:T(8,128)(2,1)S(1)}, u32[]{:S(2)}, u32[]{:S(2)}) %all-to-all-start.5) | async-done | bytes 262176 | tf_op jit(solution)/shard_map/all_to_all | solution.py:285
  142.1 1.6 %last.1 = (bf16[256,768]{1,0:T(8,128)(2,1)}, f32[3,24,768]{2,1,0:T(8,128)}, f32[768]{0:T(1024)}, f32[768]{0:T(1024)}) custom-call(bf16[16,64,128]{2,1,0:T(8,128)(2,1)S(1)} %all-to-all-done.5.got, f32[4,768]{1,0:T(4,128)S(1)} %copy-done.14, bf16[256,768]{1,0:T(8,128)(2,1)S(1)} %bitcast.17, bf16[256,768]{1,0:T(8,128)(2,1)S(1)} %bitcast.22, ...), custom_call_target="tpu_custom_call" | custom-call | bytes 1048576 | tf_op jit(solution)/shard_map/last/pallas_call | solution.py:369
  (21 shorter events, 0.1 us)
Async XLA Ops:
  7.2 66.5 %all-gather.3.cloned.1.call-start = ((), (), s32[]{:S(2)}) async-start(), calls=%async_computation.6 | async-start | bytes 1990656 | tf_op jit(solution)/shard_map/all_gather | solution.py:317
  7.2 10.0 %collective-permute-start = (bf16[3,24,768]{2,1,0:T(8,128)(2,1)}, bf16[3,24,768]{2,1,0:T(8,128)(2,1)S(1)}, u32[]{:S(2)}, u32[]{:S(2)}) collective-permute-start(bf16[3,24,768]{2,1,0:T(8,128)(2,1)} %bitcast.28), channel_id=1, source_target_pairs={{0,112},{16,96},{32,80},{48,64},{64,48},{80,32},{96,16},{112,0},{1... | collective-permute-start | bytes 331784 | tf_op jit(solution)/shard_map/ppermute | solution.py:311
  10.2 1.0 copy-start
  18.8 37.7 %copy-start.19 = (f32[768]{0:T(1024)S(1)}, f32[768]{0:T(1024)}, u32[]{:S(2)}) copy-start(f32[768]{0:T(1024)} %param.6) | copy-start | bytes 9220
  18.8 37.7 %copy-start.20 = (f32[768]{0:T(1024)S(1)}, f32[768]{0:T(1024)}, u32[]{:S(2)}) copy-start(f32[768]{0:T(1024)} %param.7) | copy-start | bytes 9220
  18.8 46.0 %copy-start.1 = (bf16[1,256,768]{2,1,0:T(8,128)(2,1)S(1)}, bf16[1,256,768]{2,1,0:T(8,128)(2,1)}, u32[]{:S(2)}) copy-start(bf16[1,256,768]{2,1,0:T(8,128)(2,1)} %param.5) | copy-start | bytes 1179652
  18.9 21.8 %collective-permute-start.1 = (bf16[256,768]{1,0:T(8,128)(2,1)}, bf16[256,768]{1,0:T(8,128)(2,1)S(1)}, u32[]{:S(2)}, u32[]{:S(2)}) collective-permute-start(bf16[256,768]{1,0:T(8,128)(2,1)} %bitcast.18), channel_id=1, source_target_pairs={{1,2},{2,1},{3,4},{4,3},{5,6},{6,5},{7,8},{8,7},{9,10},{10,9},{11,... | collective-permute-start | bytes 1179656 | tf_op jit(solution)/shard_map/ppermute | solution.py:316
  40.6 25.7 %copy-start.4 = (bf16[1,256,768]{2,1,0:T(8,128)(2,1)S(1)}, bf16[1,256,768]{2,1,0:T(8,128)(2,1)}, u32[]{:S(2)}) copy-start(bf16[1,256,768]{2,1,0:T(8,128)(2,1)} %param.9) | copy-start | bytes 1179652
  40.6 25.7 %copy-start.7 = (bf16[256,768]{1,0:T(8,128)(2,1)}, bf16[256,768]{1,0:T(8,128)(2,1)S(1)}, u32[]{:S(2)}) copy-start(bf16[256,768]{1,0:T(8,128)(2,1)S(1)} %collective-permute-done.1.outer.outer_h) | copy-start | bytes 1179652
  43.0 23.3 %collective-permute-start.2 = (bf16[768,768]{1,0:T(8,128)(2,1)}, bf16[768,768]{1,0:T(8,128)(2,1)S(1)}, u32[]{:S(2)}, u32[]{:S(2)}) collective-permute-start(bf16[768,768]{1,0:T(8,128)(2,1)} %pad_maximum_fusion), channel_id=1, source_target_pairs={{0,1},{1,0},{2,3},{3,2},{4,5},{5,4},{6,7},{7,6},{8,9},{9,8},{10,11... | collective-permute-start | bytes 3538952 | tf_op jit(solution)/shard_map/ppermute | solution.py:321
  46.3 18.5 %all-to-all-start.1 = ((f32[32,2,768]{2,1,0:T(2,128)}), f32[32,2,768]{2,1,0:T(2,128)S(1)}, u32[]{:S(2)}, u32[]{:S(2)}) async-start(f32[32,2,768]{2,1,0:T(2,128)} %merge.1), calls=%async_computation.1 | async-start | bytes 393216 | tf_op jit(solution)/shard_map/all_to_all | solution.py:285
  56.6 11.7 %copy-start.16 = (s32[2]{0:T(128)}, s32[2]{0:T(128)S(1)}, u32[]{:S(2)}) copy-start(s32[2]{0:T(128)S(1)} %pad_add_fusion.place) | copy-start | bytes 28
  65.7 0.6 copy-start.13
  66.3 2.0 %copy-start.8 = (bf16[768,768]{1,0:T(8,128)(2,1)}, bf16[768,768]{1,0:T(8,128)(2,1)S(1)}, u32[]{:S(2)}) copy-start(bf16[768,768]{1,0:T(8,128)(2,1)S(1)} %collective-permute-done.2.mate.mate_h) | copy-start | bytes 3538948
  68.3 1.2 copy-start.6
  69.5 26.2 %all-to-all-start.2 = ((bf16[8,48,2304]{2,1,0:T(8,128)(2,1)}), bf16[8,48,2304]{2,1,0:T(8,128)(2,1)S(1)}, u32[]{:S(2)}, u32[]{:S(2)}) async-start(bf16[8,48,2304]{2,1,0:T(8,128)(2,1)} %bitcast.23), calls=%async_computation.2 | async-start | bytes 3538944 | tf_op jit(solution)/shard_map/all_to_all | solution.py:285
  73.6 5.8 %collective-permute-start.3 = (bf16[8,3,48,768]{3,2,1,0:T(8,128)(2,1)}, bf16[8,3,48,768]{3,2,1,0:T(8,128)(2,1)S(1)}, u32[]{:S(2)}, u32[]{:S(2)}) collective-permute-start(bf16[8,3,48,768]{3,2,1,0:T(8,128)(2,1)} %bitcast.24), channel_id=1, source_target_pairs={{0,1},{1,0},{2,3},{3,2},{4,5},{5,4},{6,7},{7,6},{8,9},{9,8},{10,11... | collective-permute-start | bytes 5308424 | tf_op jit(solution)/shard_map/ppermute | solution.py:333
  79.4 1.2 copy-start.18
  87.6 16.4 %copy-start.2 = (bf16[1,256,768]{2,1,0:T(8,128)(2,1)S(1)}, bf16[1,256,768]{2,1,0:T(8,128)(2,1)}, u32[]{:S(2)}) copy-start(bf16[1,256,768]{2,1,0:T(8,128)(2,1)} %param.5) | copy-start | bytes 1179652
  87.6 36.7 %copy-start.9 = (bf16[768,768]{1,0:T(8,128)(2,1)S(1)}, bf16[768,768]{1,0:T(8,128)(2,1)}, u32[]{:S(2)}) copy-start(bf16[768,768]{1,0:T(8,128)(2,1)} %copy-done.8) | copy-start | bytes 3538948
  87.6 36.7 %copy-start.14 = (f32[4,768]{1,0:T(4,128)S(1)}, f32[4,768]{1,0:T(4,128)}, u32[]{:S(2)}) copy-start(f32[4,768]{1,0:T(4,128)} %copy-done.13) | copy-start | bytes 36868
  87.6 36.7 %copy-start.15 = (s32[1,768]{1,0:T(1,128)S(1)}, s32[1,768]{1,0:T(1,128)}, u32[]{:S(2)}) copy-start(s32[1,768]{1,0:T(1,128)} %fusion.channel) | copy-start | bytes 9220
  87.6 36.7 %copy-start.17 = (s32[2]{0:T(128)S(1)}, s32[2]{0:T(128)}, u32[]{:S(2)}) copy-start(s32[2]{0:T(128)} %copy-done.16) | copy-start | bytes 28
  96.0 0.7 copy-start.11
  96.7 12.6 %all-to-all-start.3 = ((bf16[4,256,128]{2,1,0:T(8,128)(2,1)}), bf16[4,256,128]{2,1,0:T(8,128)(2,1)S(1)}, u32[]{:S(2)}, u32[]{:S(2)}) async-start(bf16[4,256,128]{2,1,0:T(8,128)(2,1)} %copy-done.11), calls=%async_computation.3 | async-start | bytes 524288 | tf_op jit(solution)/shard_map/all_to_all | solution.py:285
  103.9 20.3 %collective-permute-start.4 = (bf16[256,768]{1,0:T(8,128)(2,1)S(1)}, bf16[256,768]{1,0:T(8,128)(2,1)S(1)}, u32[]{:S(2)}, u32[]{:S(2)}) collective-permute-start(bf16[256,768]{1,0:T(8,128)(2,1)S(1)} %bitcast.15), channel_id=1, source_target_pairs={{1,2},{2,1},{3,4},{4,3},{5,6},{6,5},{7,8},{8,7},{9,10},{10,9},{11,... | collective-permute-start | bytes 1179656 | tf_op jit(solution)/shard_map/ppermute | solution.py:350
  110.1 18.5 %all-to-all-start.4 = ((bf16[8,64,128]{2,1,0:T(8,128)(2,1)}), bf16[8,64,128]{2,1,0:T(8,128)(2,1)S(1)}, u32[]{:S(2)}, u32[]{:S(2)}) async-start(bf16[8,64,128]{2,1,0:T(8,128)(2,1)} %second.1), calls=%async_computation.4 | async-start | bytes 262144 | tf_op jit(solution)/shard_map/all_to_all | solution.py:285
  127.6 1.0 copy-start.10
  129.4 12.8 %all-to-all-start.5 = ((bf16[16,64,128]{2,1,0:T(8,128)(2,1)}), bf16[16,64,128]{2,1,0:T(8,128)(2,1)S(1)}, u32[]{:S(2)}, u32[]{:S(2)}) async-start(bf16[16,64,128]{2,1,0:T(8,128)(2,1)} %third.1), calls=%async_computation.5 | async-start | bytes 524288 | tf_op jit(solution)/shard_map/all_to_all | solution.py:285
  133.8 8.3 %copy-start.3 = (bf16[1,256,768]{2,1,0:T(8,128)(2,1)S(1)}, bf16[1,256,768]{2,1,0:T(8,128)(2,1)}, u32[]{:S(2)}) copy-start(bf16[1,256,768]{2,1,0:T(8,128)(2,1)} %param.5) | copy-start | bytes 1179652
  133.8 8.3 %copy-start.5 = (bf16[1,256,768]{2,1,0:T(8,128)(2,1)S(1)}, bf16[1,256,768]{2,1,0:T(8,128)(2,1)}, u32[]{:S(2)}) copy-start(bf16[1,256,768]{2,1,0:T(8,128)(2,1)} %param.9) | copy-start | bytes 1179652
  133.8 8.3 %copy-start.12 = (f32[256,768]{1,0:T(8,128)S(1)}, f32[256,768]{1,0:T(8,128)}, u32[]{:S(2)}) copy-start(f32[256,768]{1,0:T(8,128)} %get-tuple-element.44.pre_h) | copy-start | bytes 2359300
Sparse Core Ops, SparseCore 0:
  19.0 48.4 all-gather.2
